TPU v7x, 128 devices: a whole 4x4x4 slice. The times are simulated.
128 devices in a mesh: dp: 8 (over y, core), tensor: 16 (over x, z).
Axes of the slice: x: 4, y: 4, z: 4, core: 2. Of those that a mesh axis runs over, the one named last changes fastest.
Arguments:
- gradients: bfloat16 [8, 3072, 12288], P('dp', None, 'tensor'), may hold values from -40 to 40
- errors: bfloat16 [8, 3072, 12288], P('dp', None, 'tensor'), may hold values from -2 to 2
- weight: bfloat16 [3072, 12288], P(None, 'tensor'), may hold values from -6 to 6
- start_q: float32 [12288, 64], P('tensor'), may hold values from -6 to 6
Outputs:
- new_errors: bfloat16 [8, 3072, 12288], P('dp', None, 'tensor')
- new_weight: bfloat16 [3072, 12288], P(None, 'tensor')
- right_factor: float32 [12288, 64], P('tensor')
All inputs are finite; a program needn't handle non-finite values.
Results may differ from a plain program's by a relative error of at most 0.001.
Values sent between devices are 32-bit elements; how exact they have to be, the bound alone decides.
No kernel may reach another device: no remote copies, remote signals or barrier semaphores. Data moves between devices by JAX's collectives and lax.ppermute only.
A program may use at most 128 MiB of HBM per device.

v0:
```python
import jax
import jax.numpy as jnp
from jax import lax
from jax.sharding import PartitionSpec as P

ITERS = 2


HIGH = lax.Precision.HIGHEST


def factor_solve(gram, rows):
    chol = jnp.linalg.cholesky(gram)
    return lax.linalg.triangular_solve(chol, rows, left_side=False, lower=True, transpose_a=True)


def left_basis(merged, right_factor, replicas):
    term = jnp.dot(merged, right_factor, precision=HIGH, preferred_element_type=jnp.float32)
    left = lax.psum(term, ("dp", "tensor")) / replicas
    gram = jnp.dot(left.T, left, precision=HIGH, preferred_element_type=jnp.float32)
    return factor_solve(gram, left)


def shards(gradients, errors, weight, start_q):
    merged = gradients[0].astype(jnp.float32) + errors[0].astype(jnp.float32)
    replicas = lax.axis_size("dp")
    right_factor = start_q
    basis = None
    for step in range(ITERS):
        basis = left_basis(merged, right_factor, replicas)
        local_right = lax.dot_general(
            merged,
            basis,
            (((0,), (0,)), ((), ())),
            precision=HIGH,
            preferred_element_type=jnp.float32,
        )
        right_factor = lax.psum(local_right, "dp") / replicas
    approx = jnp.dot(basis, right_factor.T, precision=HIGH, preferred_element_type=jnp.float32)
    new_errors = (merged - approx).astype(jnp.bfloat16)[None]
    new_weight = (weight.astype(jnp.float32) - 0.5 * approx).astype(jnp.bfloat16)
    return (new_errors, new_weight, right_factor)


def solution(mesh):
    return jax.shard_map(
        shards,
        mesh=mesh,
        in_specs=(
            P("dp", None, "tensor"),
            P("dp", None, "tensor"),
            P(None, "tensor"),
            P("tensor", None),
        ),
        out_specs=(P("dp", None, "tensor"), P(None, "tensor"), P("tensor", None)),
        check_vma=False,
    )
```

profile of v0, /device:TPU:1, one launch (start us, length us, event | category | flops | bytes accessed | tf_op | source)
XLA Modules:
  0.0 521.3 jit_solution(1548747981070651228)
XLA Ops:
  7.2 0.0 copy-start
  7.2 0.0 all-reduce.5.cloned.1.call-start
  7.2 0.9 copy-done
  8.1 14.7 %fusion.6 = f32[3072,64]{0,1:T(8,128)} fusion(f32[768,64]{0,1:T(8,128)S(1)} %copy-done, bf16[1,3072,768]{2,1,0:T(8,128)(2,1)} %param.8, bf16[1,3072,768]{2,1,0:T(8,128)(2,1)} %param.7), kind=kOutput, calls=%fused_computation.7 | convolution fusion | flops 1819017216 | bytes 10420224 | tf_op jit(solution)/shard_map/dot_general | solution.py:18
  22.8 0.0 all-reduce.5.cloned.1.call-update
  22.8 0.2 all-reduce.7.cloned.1.call-start
  23.0 149.5 %all-reduce.5.cloned.1.call-done = f32[3072,64]{0,1:T(8,128)} async-done(((f32[3072,64]{0,1:T(8,128)}), f32[3072,64]{0,1:T(8,128)}) %all-reduce.5.cloned.1.call-update) | async-done | bytes 786448 | tf_op jit(solution)/shard_map/psum | solution.py:19
  172.5 2.2 fusion.14
  174.7 0.1 copy.7
  174.8 5.8 %cholesky.44 = f32[64,64]{1,0:T(8,128)S(1)} custom-call(f32[64,64]{1,0:T(8,128)S(1)} %fusion.27), custom_call_target="Cholesky" | custom-call | tf_op jit(solution)/shard_map/jit(cholesky)/cholesky | solution.py:13
  180.7 0.6 compare_reduce_fusion.1
  181.3 0.7 fusion.22
  182.0 4.9 custom-call.6
  186.9 2.0 convolution_bitcast_fusion.1
  188.9 10.1 %fusion.4 = f32[768,64]{0,1:T(8,128)} fusion(f32[3072,64]{0,1:T(8,128)S(1)} %convolution_bitcast_fusion.1, bf16[1,3072,768]{2,1,0:T(8,128)(2,1)} %param.8, bf16[1,3072,768]{2,1,0:T(8,128)(2,1)} %param.7), kind=kOutput, calls=%fused_computation.5 | convolution fusion | flops 1819017216 | bytes 10420224 | tf_op jit(solution)/shard_map/dot_general | solution.py:31
  199.0 0.0 all-reduce.7.cloned.1.call-update
  199.0 0.3 all-reduce.9.cloned.1.call-start
  199.2 55.7 %all-reduce.7.cloned.1.call-done = f32[768,64]{0,1:T(8,128)} async-done(((f32[768,64]{0,1:T(8,128)}), f32[768,64]{0,1:T(8,128)}) %all-reduce.7.cloned.1.call-update) | async-done | bytes 196624 | tf_op jit(solution)/shard_map/psum | solution.py:38
  255.0 14.7 %fusion.2 = f32[3072,64]{0,1:T(8,128)} fusion(bf16[1,3072,768]{2,1,0:T(8,128)(2,1)} %param.8, bf16[1,3072,768]{2,1,0:T(8,128)(2,1)} %param.7, f32[768,64]{0,1:T(8,128)} %all-reduce.7.cloned.1.call-done), kind=kOutput, calls=%fused_computation.3 | convolution fusion | flops 1819066368 | bytes 10420224 | tf_op jit(solution)/shard_map/dot_general | solution.py:18
  269.6 0.0 all-reduce.9.cloned.1.call-update
  269.7 0.3 all-reduce.11.cloned.1.call-start
  270.0 147.3 %all-reduce.9.cloned.1.call-done = f32[3072,64]{0,1:T(8,128)} async-done(((f32[3072,64]{0,1:T(8,128)}), f32[3072,64]{0,1:T(8,128)}) %all-reduce.9.cloned.1.call-update) | async-done | bytes 786448 | tf_op jit(solution)/shard_map/psum | solution.py:19
  417.3 2.2 fusion.11
  419.5 0.1 copy.8
  419.6 5.8 %cholesky.55 = f32[64,64]{1,0:T(8,128)S(1)} custom-call(f32[64,64]{1,0:T(8,128)S(1)} %fusion.25), custom_call_target="Cholesky" | custom-call | tf_op jit(solution)/shard_map/jit(cholesky)/cholesky | solution.py:13
  425.5 0.6 compare_reduce_fusion
  426.1 0.7 fusion.23
  426.8 4.9 custom-call.7
  431.7 2.0 convolution_bitcast_fusion
  433.7 10.0 %fusion = f32[768,64]{0,1:T(8,128)} fusion(f32[3072,64]{0,1:T(8,128)S(1)} %convolution_bitcast_fusion, bf16[1,3072,768]{2,1,0:T(8,128)(2,1)} %param.8, bf16[1,3072,768]{2,1,0:T(8,128)(2,1)} %param.7), kind=kOutput, calls=%fused_computation.1 | convolution fusion | flops 1819017216 | bytes 10420224 | tf_op jit(solution)/shard_map/dot_general | solution.py:31
  443.7 0.0 all-reduce.11.cloned.1.call-update
  443.7 56.0 %all-reduce.11.cloned.1.call-done = f32[768,64]{0,1:T(8,128)} async-done(((f32[768,64]{0,1:T(8,128)}), f32[768,64]{0,1:T(8,128)}) %all-reduce.11.cloned.1.call-update) | async-done | bytes 196624 | tf_op jit(solution)/shard_map/psum | solution.py:38
  499.7 0.9 broadcast_multiply_fusion
  500.6 0.0 copy-start.1
  500.7 14.1 %subtract_convert_fusion = (bf16[3072,768]{1,0:T(8,128)(2,1)}, bf16[1,3072,768]{2,1,0:T(8,128)(2,1)}) fusion(bf16[3072,768]{1,0:T(8,128)(2,1)} %param.9, bf16[1,3072,768]{2,1,0:T(8,128)(2,1)} %param.8, bf16[1,3072,768]{2,1,0:T(8,128)(2,1)} %param.7, f32[3072,64]{0,1:T(8,128)S(1)} %convolution_bitcast_fusion, f32[768,64]{0,1:T(8,128)S(1)} %broadcast_multiply_fusion), kind=kOutput, calls=%fused_computation.10 | convolution fusion | flops 1833172992 | bytes 24576000 | tf_op jit(solution)/shard_map/dot_general | solution.py:39
  514.8 0.0 copy-done.1
  (4 shorter events, 0.1 us)
Async XLA Ops:
  7.2 0.9 copy-start
  7.2 165.4 %all-reduce.5.cloned.1.call-start = ((), (), s32[]{:S(2)}) async-start(), calls=%async_computation | async-start | bytes 1572864 | tf_op jit(solution)/shard_map/psum | solution.py:19
  22.8 232.2 %all-reduce.7.cloned.1.call-start = ((), (), s32[]{:S(2)}) async-start(), calls=%async_computation.1 | async-start | bytes 393216 | tf_op jit(solution)/shard_map/psum | solution.py:38
  199.0 218.3 %all-reduce.9.cloned.1.call-start = ((), (), s32[]{:S(2)}) async-start(), calls=%async_computation.2 | async-start | bytes 1572864 | tf_op jit(solution)/shard_map/psum | solution.py:19
  269.7 230.0 %all-reduce.11.cloned.1.call-start = ((), (), s32[]{:S(2)}) async-start(), calls=%async_computation.3 | async-start | bytes 393216 | tf_op jit(solution)/shard_map/psum | solution.py:38
  500.6 14.2 %copy-start.1 = (f32[768,64]{0,1:T(8,128)}, f32[768,64]{0,1:T(8,128)S(1)}, u32[]{:S(2)}) copy-start(f32[768,64]{0,1:T(8,128)S(1)} %broadcast_multiply_fusion) | copy-start | bytes 589828
Sparse Core Ops, SparseCore 0:
  22.9 149.5 all-reduce.4
  199.1 55.8 all-reduce.6
  269.8 147.4 all-reduce.8
  443.8 55.8 all-reduce.10
where the time goes:
time: 523 us; the launch traced here: 521 us
  waiting for transfers between devices  409 us (78%)
  matrix products  71.9 us (14%)
  other arithmetic  25.1 us (5%)
  between operations  13.9 us (3%)
    psum x2, waiting for transfers between devices, left_basis(): left = lax.psum(term, ('dp', 'tensor')) / replicas  297 us
    psum x2, waiting for transfers between devices, shards(): right_factor = lax.psum(local_right, 'dp') / replicas  112 us
    dot_general x2, matrix products, left_basis(): jnp.dot(merged, right_factor, precision=HIGH, preferred_element_type=jnp....  29.3 us
    dot_general x2, matrix products, shards(): lax.dot_general(merged, basis, (((0,), (0,)), ((), ())), precision=HIGH,...  20.1 us
    dot_general x1, matrix products, shards(): jnp.dot(basis, right_factor.T, precision=HIGH, preferred_element_type=jnp...  14.1 us
    another operation x6, other arithmetic, factor_solve(): chol = jnp.linalg.cholesky(gram)  13 us
    another operation x4, other arithmetic, factor_solve(): lax.linalg.triangular_solve(chol, rows, left_side=False, lower=True, tran...  11.1 us
  transfers between devices with their start and end apart: 4, of which 4 were waited for; matrix products, arithmetic and copies ran while one was open for 0% of the time, Pallas kernels for 0%

commit v1 on v0

v1 whole, which is shorter than its diff:
```python
import functools

import jax
import jax.numpy as jnp
from jax import lax
from jax.experimental import pallas as pl
from jax.experimental.pallas import tpu as pltpu
from jax.sharding import Mesh, PartitionSpec as P

F32, BF16 = jnp.float32, jnp.bfloat16
HIGH = lax.Precision.HIGHEST
RANK, HALF = 64, 32
ROWS, COLS = 3072, 768
BLOCK = 768
BLOCKS = ROWS // BLOCK
CHIPS = 64
REPLICAS = 8
CHIP_AXES = ("y", "x", "z")
LIMIT = 40 * 2**20


def split(x, parts):
    terms = []
    for _ in range(parts):
        term = x.astype(BF16)
        terms.append(term)
        x = x - term.astype(F32)
    return terms


def fold(x):
    return x[:RANK] + (x[RANK : 2 * RANK] + x[2 * RANK :])


def ordered(core, mine, other):
    first = core == 0
    return jnp.concatenate([jnp.where(first, mine, other), jnp.where(first, other, mine)], axis=0)


def parted(core, x):
    first = core == 0
    top, bottom = x[:HALF], x[HALF:]
    return jnp.where(first, top, bottom), jnp.where(first, bottom, top)


def left_kernel(first, core, *refs):
    if first:
        q, g, e, mine, other, stack = refs
    else:
        z_mine, z_other, inverse, g, e, mine, other, stack = refs

    @pl.when(pl.program_id(0) == 0)
    def _():
        if first:
            right = q[...].T
        else:
            z = ordered(core[0], z_mine[...], z_other[...])
            right = jnp.dot(inverse[...], z, precision=HIGH, preferred_element_type=F32) * (1.0 / REPLICAS)
        stack[...] = jnp.concatenate(split(right, 3), axis=0)

    across = (((1,), (1,)), ((), ()))
    p = lax.dot_general(stack[...], g[...], across, preferred_element_type=F32)
    p = p + lax.dot_general(stack[...], e[...], across, preferred_element_type=F32)
    mine[0], other[0] = parted(core[0], fold(p))


def right_kernel(core, l_mine, l_other, g, e, z_mine, z_other, gram, total, products):
    step = pl.program_id(0)

    @pl.when(step == 0)
    def _():
        total[...] = jnp.zeros_like(total)
        products[...] = jnp.zeros_like(products)

    left = ordered(core[0], l_mine[0], l_other[0])
    stack = jnp.concatenate(split(left, 3), axis=0)
    z = jnp.dot(stack, g[...], preferred_element_type=F32)
    total[...] += fold(z + jnp.dot(stack, e[...], preferred_element_type=F32))
    products[...] += lax.dot_general(stack, stack, (((1,), (1,)), ((), ())), preferred_element_type=F32)

    @pl.when(step == BLOCKS - 1)
    def _():
        z_mine[...], z_other[...] = parted(core[0], total[...])
        rows = fold(products[...])
        gram[...] = rows[:, :RANK] + (rows[:, RANK : 2 * RANK] + rows[:, 2 * RANK :])


def factor_kernel(gram, inverse):
    rows = lax.broadcasted_iota(jnp.int32, (RANK, RANK), 0)
    cols = lax.broadcasted_iota(jnp.int32, (RANK, RANK), 1)
    work = jnp.concatenate([gram[...], (rows == cols).astype(F32)], axis=1)
    for k in range(RANK):
        scale = lax.rsqrt(work[k : k + 1, k : k + 1])
        row = work[k : k + 1, :] * scale
        inverse[k : k + 1, :] = row[:, RANK:]
        start = (k + 1) // 8 * 8
        if start >= RANK:
            break
        column = work[start:, k : k + 1] * scale
        below = lax.broadcasted_iota(jnp.int32, (RANK - start, 1), 0) + start > k
        rest = work[start:] - jnp.where(below, column, 0.0) * row
        work = jnp.concatenate([work[:start], rest], axis=0) if start else rest


def renew_kernel(core, z_mine, z_other, inverse, l_mine, l_other, g, e, w, new_e, new_w, right_out, stack):
    @pl.when(pl.program_id(0) == 0)
    def _():
        z = ordered(core[0], z_mine[...], z_other[...])
        right = jnp.dot(inverse[...], z, precision=HIGH, preferred_element_type=F32) * (1.0 / REPLICAS)
        right_out[...] = right.T
        mixed = lax.dot_general(
            inverse[...], right, (((0,), (0,)), ((), ())), precision=HIGH, preferred_element_type=F32
        )
        high, low = split(mixed, 2)
        stack[...] = jnp.concatenate([high, low, high], axis=0)

    left = ordered(core[0], l_mine[0], l_other[0])
    high, low = split(left, 2)
    factors = jnp.concatenate([high, high, low], axis=0)
    approx = lax.dot_general(factors, stack[...], (((0,), (0,)), ((), ())), preferred_element_type=F32)
    merged = g[...].astype(F32) + e[...].astype(F32)
    new_e[...] = (merged - approx).astype(BF16)
    new_w[...] = (w[...].astype(F32) - 0.5 * approx).astype(BF16)


def spec(shape, index):
    return pl.BlockSpec(shape, index)


def whole(shape):
    return pl.BlockSpec(shape, lambda i: (0,) * len(shape))


SCALAR = pl.BlockSpec(memory_space=pltpu.SMEM)
TILE = spec((BLOCK, COLS), lambda i: (i, 0))
PIECE = spec((1, HALF, BLOCK), lambda i: (i, 0, 0))
PIECES = jax.ShapeDtypeStruct((BLOCKS, HALF, BLOCK), F32)
ZHALF = jax.ShapeDtypeStruct((HALF, COLS), F32)


def cost(products, nbytes):
    return pl.CostEstimate(flops=2 * ROWS * COLS * RANK * products, bytes_accessed=nbytes, transcendentals=0)


def params():
    return pltpu.CompilerParams(vmem_limit_bytes=LIMIT, dimension_semantics=("arbitrary",))


def left_pass(core, right, g, e):
    first = len(right) == 1
    if first:
        specs = [whole((COLS, RANK))]
    else:
        specs = [whole((HALF, COLS)), whole((HALF, COLS)), whole((RANK, RANK))]
    return pl.pallas_call(
        functools.partial(left_kernel, first),
        grid=(BLOCKS,),
        in_specs=[SCALAR, *specs, TILE, TILE],
        out_specs=[PIECE, PIECE],
        out_shape=[PIECES, PIECES],
        scratch_shapes=[pltpu.VMEM((3 * RANK, COLS), BF16)],
        compiler_params=params(),
        cost_estimate=cost(6, 4 * ROWS * COLS),
        name="left_pass",
    )(core, *right, g, e)


def right_pass(core, l_mine, l_other, g, e):
    return pl.pallas_call(
        right_kernel,
        grid=(BLOCKS,),
        in_specs=[SCALAR, PIECE, PIECE, TILE, TILE],
        out_specs=[whole((HALF, COLS)), whole((HALF, COLS)), whole((RANK, RANK))],
        out_shape=[ZHALF, ZHALF, jax.ShapeDtypeStruct((RANK, RANK), F32)],
        scratch_shapes=[pltpu.VMEM((RANK, COLS), F32), pltpu.VMEM((3 * RANK, 3 * RANK), F32)],
        compiler_params=params(),
        cost_estimate=cost(6, 4 * ROWS * COLS),
        name="right_pass",
    )(core, l_mine, l_other, g, e)


def factor(gram):
    return pl.pallas_call(
        factor_kernel,
        out_shape=jax.ShapeDtypeStruct((RANK, RANK), F32),
        cost_estimate=pl.CostEstimate(flops=2 * RANK**3, bytes_accessed=8 * RANK**2, transcendentals=RANK),
        name="factor",
    )(gram)


def renew(core, z_mine, z_other, inverse, l_mine, l_other, g, e, w):
    array = jax.ShapeDtypeStruct((ROWS, COLS), BF16)
    return pl.pallas_call(
        renew_kernel,
        grid=(BLOCKS,),
        in_specs=[SCALAR, whole((HALF, COLS)), whole((HALF, COLS)), whole((RANK, RANK)), PIECE, PIECE, TILE, TILE, TILE],
        out_specs=[TILE, TILE, whole((COLS, RANK))],
        out_shape=[array, array, jax.ShapeDtypeStruct((COLS, RANK), F32)],
        scratch_shapes=[pltpu.VMEM((3 * RANK, COLS), BF16)],
        compiler_params=params(),
        cost_estimate=cost(3, 10 * ROWS * COLS),
        name="renew",
    )(core, z_mine, z_other, inverse, l_mine, l_other, g, e, w)


def swap(x):
    return lax.ppermute(x, "core", [(0, 1), (1, 0)])


def along_y(x, shift):
    return lax.ppermute(x, "y", [(i, (i + shift) % 4) for i in range(4)])


def sum_left(mine, other):
    term = (mine + swap(other)).reshape(CHIPS, 2, BLOCK)
    term = lax.all_to_all(term, CHIP_AXES, 0, 0, tiled=True)
    term = jnp.sum(term, axis=0, keepdims=True) * (1.0 / REPLICAS)
    term = jnp.broadcast_to(term, (CHIPS, 2, BLOCK))
    term = lax.all_to_all(term, CHIP_AXES, 0, 0, tiled=True)
    term = term.reshape(BLOCKS, HALF, BLOCK)
    return term, swap(term)


def sum_right(mine, other):
    half = mine + swap(other)
    parts = [along_y(half, shift) for shift in (1, 3, 2)]
    half = half + parts[0] + parts[1] + parts[2]
    return half, swap(half)


def shards(gradients, errors, weight, start_q):
    g, e = gradients[0], errors[0]
    core = lax.axis_index("core").astype(jnp.int32).reshape(1)
    left = sum_left(*left_pass(core, (start_q,), g, e))
    z_mine, z_other, gram = right_pass(core, *left, g, e)
    right = (*sum_right(z_mine, z_other), factor(gram))
    left = sum_left(*left_pass(core, right, g, e))
    z_mine, z_other, gram = right_pass(core, *left, g, e)
    right = (*sum_right(z_mine, z_other), factor(gram))
    new_e, new_w, right_factor = renew(core, *right, *left, g, e, weight)
    return new_e[None], new_w, right_factor


def solution(mesh):
    chips = Mesh(mesh.devices.reshape(4, 2, 4, 4), ("y", "core", "x", "z"))
    dp, tensor = ("y", "core"), ("x", "z")
    return jax.shard_map(
        shards,
        mesh=chips,
        in_specs=(P(dp, None, tensor), P(dp, None, tensor), P(None, tensor), P(tensor, None)),
        out_specs=(P(dp, None, tensor), P(None, tensor), P(tensor, None)),
        check_vma=False,
    )
```

time: 523 us -> 168 us (0.32)
  waiting for transfers between devices: 409 us -> 17.7 us
  matrix products: 71.9 us -> 0 us
  blocking collectives: 0 us -> 66.5 us
  Pallas kernels: 0 us -> 36.1 us
  local copies, waits for them, and re-layouts: 1.03 us -> 28 us
  other arithmetic: 25.1 us -> 0.48 us
  starting transfers between devices: 0.83 us -> 17.6 us
  between operations: 13.9 us -> 0.78 us
    psum x4 -> x0, waiting for transfers between devices: 409 us -> none  [the longest x2 297 us: left_basis(): left = lax.psum(term, ('dp', 'tensor')) / replicas]
    dot_general x7 -> x0, matrix products: 67.9 us -> none  [the longest x2 29.3 us: left_basis(): jnp.dot(merged, right_factor, precision=HIGH, preferred_element_type=jnp....]
    all_to_all x0 -> x4, blocking collectives: none -> 66.5 us  [sum_left(): term = lax.all_to_all(term, CHIP_AXES, 0, 0, tiled=True)]
    pallas_call x0 -> x7, Pallas kernels: none -> 36.1 us  [the longest x2 13.6 us: factor(): pl.pallas_call(factor_kernel, out_shape=jax.ShapeDtypeStruct((RANK, RANK)...]
    unnamed x4 -> x30, local copies, waits for them, and re-layouts: 0.89 us -> 26.8 us
    another operation x10 -> x0, other arithmetic: 24.1 us -> none  [the longest x6 13 us: factor_solve(): chol = jnp.linalg.cholesky(gram)]
    ppermute x0 -> x14, waiting for transfers between devices: none -> 17.7 us  [the longest x6 10 us: along_y(): return lax.ppermute(x, 'y', [(i, (i + shift) % 4) for i in range(4)])]
    ppermute x0 -> x14, starting transfers between devices: none -> 17.6 us  [the longest x8 12.6 us: swap(): return lax.ppermute(x, 'core', [(0, 1), (1, 0)])]
  transfers between devices with their start and end apart: 4 -> 14, of which waited for: 4 -> 12; matrix products, arithmetic and copies ran while one was open for 0% -> 0% of each run, Pallas kernels for 0% -> 8%
where the time goes in v1:
time: 168 us; the launch traced here: 167 us
  blocking collectives  66.5 us (40%)
  Pallas kernels  36.1 us (21%)
  local copies, waits for them, and re-layouts  28 us (17%)
  waiting for transfers between devices  17.7 us (11%)
  starting transfers between devices  17.6 us (10%)
    all_to_all x4, blocking collectives, sum_left(): term = lax.all_to_all(term, CHIP_AXES, 0, 0, tiled=True)  66.5 us
    unnamed x30, local copies, waits for them, and re-layouts  26.8 us
    pallas_call x2, Pallas kernels, factor(): pl.pallas_call(factor_kernel, out_shape=jax.ShapeDtypeStruct((RANK, RANK)...  13.6 us
    ppermute x8, starting transfers between devices, swap(): return lax.ppermute(x, 'core', [(0, 1), (1, 0)])  12.6 us
    ppermute x6, waiting for transfers between devices, along_y(): return lax.ppermute(x, 'y', [(i, (i + shift) % 4) for i in range(4)])  10 us
    pallas_call x1, Pallas kernels, renew(): pl.pallas_call(renew_kernel, grid=(BLOCKS,), in_specs=[SCALAR, whole((HAL...  8.32 us
    pallas_call x2, Pallas kernels, left_pass(): pl.pallas_call(functools.partial(left_kernel, first), grid=(BLOCKS,), in_...  7.9 us
    ppermute x8, waiting for transfers between devices, swap(): return lax.ppermute(x, 'core', [(0, 1), (1, 0)])  7.65 us
  transfers between devices with their start and end apart: 14, of which 12 were waited for; matrix products, arithmetic and copies ran while one was open for 0% of the time, Pallas kernels for 8%

profile of v1, /device:TPU:1, one launch (start us, length us, event | category | flops | bytes accessed | tf_op | source)
XLA Modules:
  0.0 167.1 jit_solution(2325350832150568015)
XLA Ops:
  0.6 1.1 copy.7.refs_0_
  1.7 2.3 %copy-done = bf16[1,3072,768]{2,1,0:T(8,128)(2,1)S(1)} copy-done((bf16[1,3072,768]{2,1,0:T(8,128)(2,1)S(1)}, bf16[1,3072,768]{2,1,0:T(8,128)(2,1)}, u32[]{:S(2)}) %copy-start) | copy-done | bytes 4718616
  4.1 2.3 %copy-done.5 = bf16[1,3072,768]{2,1,0:T(8,128)(2,1)S(1)} copy-done((bf16[1,3072,768]{2,1,0:T(8,128)(2,1)S(1)}, bf16[1,3072,768]{2,1,0:T(8,128)(2,1)}, u32[]{:S(2)}) %copy-start.5) | copy-done | bytes 4718616
  6.4 3.9 %left_pass.2 = (f32[4,32,768]{2,1,0:T(8,128)S(1)}, f32[4,32,768]{2,1,0:T(8,128)S(1)}) custom-call(s32[1]{0:T(128)} %bitcast.core, f32[768,64]{1,0:T(8,128)S(1)} %copy.7.refs_0_, bf16[3072,768]{1,0:T(8,128)(2,1)S(1)} %bitcast.4, bf16[3072,768]{1,0:T(8,128)(2,1)S(1)} %bitcast.9), custom_call_target="tpu_custom_call" | custom-call | flops 1811939328 | bytes 9437184 | tf_op jit(solution)/shard_map/left_pass/pallas_call | solution.py:155
  10.3 1.5 collective-permute-start
  11.8 1.3 collective-permute-done
  13.4 22.0 %all_to_all.20 = f32[64,2,768]{2,1,0:T(2,128)S(1)} all-to-all(f32[64,2,768]{2,1,0:T(2,128)S(1)} %reshape.30), channel_id=1, replica_groups=mesh['y'=4,'core'=2,'x'=4,'z'=4] {'y','x','z'}, dimensions={0} | all-to-all | bytes 786432 | tf_op jit(solution)/shard_map/all_to_all | solution.py:216
  35.6 14.6 %all_to_all.21 = f32[64,2,768]{2,1,0:T(2,128)S(1)} all-to-all(f32[64,2,768]{2,1,0:T(2,128)S(1)} %broadcast_in_dim.6), channel_id=1, replica_groups=mesh['y'=4,'core'=2,'x'=4,'z'=4] {'y','x','z'}, dimensions={0} | all-to-all | bytes 786432 | tf_op jit(solution)/shard_map/all_to_all | solution.py:219
  50.2 0.3 reshape.31.l_mine
  50.5 3.3 %collective-permute-start.1 = (f32[4,32,768]{2,1,0:T(8,128)S(1)}, f32[4,32,768]{2,1,0:T(8,128)S(1)}, u32[]{:S(2)}, u32[]{:S(2)}) collective-permute-start(f32[4,32,768]{2,1,0:T(8,128)S(1)} %reshape.31.l_mine), channel_id=1, source_target_pairs={{0,16},{16,0},{1,17},{17,1},{2,18},{18,2},{3,19},{19,3},{4,20},{20... | collective-permute-start | bytes 1179656 | tf_op jit(solution)/shard_map/ppermute | solution.py:207
  53.8 1.3 collective-permute-done.1.l_other
  55.2 2.3 %copy-done.1 = bf16[1,3072,768]{2,1,0:T(8,128)(2,1)S(1)} copy-done((bf16[1,3072,768]{2,1,0:T(8,128)(2,1)S(1)}, bf16[1,3072,768]{2,1,0:T(8,128)(2,1)}, u32[]{:S(2)}) %copy-start.1) | copy-done | bytes 4718616
  57.5 2.3 %copy-done.6 = bf16[1,3072,768]{2,1,0:T(8,128)(2,1)S(1)} copy-done((bf16[1,3072,768]{2,1,0:T(8,128)(2,1)S(1)}, bf16[1,3072,768]{2,1,0:T(8,128)(2,1)}, u32[]{:S(2)}) %copy-start.6) | copy-done | bytes 4718616
  59.8 3.1 %right_pass.2 = (f32[32,768]{1,0:T(8,128)S(1)}, f32[32,768]{1,0:T(8,128)S(1)}, f32[64,64]{1,0:T(8,128)S(1)}) custom-call(s32[1]{0:T(128)} %bitcast.core, f32[4,32,768]{2,1,0:T(8,128)S(1)} %reshape.31.l_mine, f32[4,32,768]{2,1,0:T(8,128)S(1)} %collective-permute-done.1.l_other, bf16[3072,768]{1,0:T(8,128)(2,1)S(1)} %bitcast.5, bf16[3072,768]{1,0:T(8,128)(2,1)S(1)} %bitcast.10), custom_call_target="tpu_custom_call" | custom-call | flops 1811939328 | bytes 9437184 | tf_op jit(solution)/shard_map/right_pass/pallas_call | solution.py:169
  63.0 0.4 collective-permute-start.2
  63.4 0.9 collective-permute-done.2
  64.4 0.4 collective-permute-start.5
  64.8 2.0 %collective-permute-start.4 = (f32[32,768]{1,0:T(8,128)S(1)}, f32[32,768]{1,0:T(8,128)S(1)}, u32[]{:S(2)}, u32[]{:S(2)}) collective-permute-start(f32[32,768]{1,0:T(8,128)S(1)} %add.31), channel_id=1, source_target_pairs={{0,96},{32,0},{64,32},{96,64},{1,97},{33,1},{65,33},{97,65},{2,98}... | collective-permute-start | bytes 294920 | tf_op jit(solution)/shard_map/ppermute | solution.py:211
  66.8 3.1 %collective-permute-done.5 = f32[32,768]{1,0:T(8,128)S(1)} collective-permute-done((f32[32,768]{1,0:T(8,128)S(1)}, f32[32,768]{1,0:T(8,128)S(1)}, u32[]{:S(2)}, u32[]{:S(2)}) %collective-permute-start.5) | collective-permute-done | bytes 98336 | tf_op jit(solution)/shard_map/ppermute | solution.py:211
  70.2 1.7 collective-permute-done.3
  71.9 1.8 %collective-permute-start.6 = (f32[32,768]{1,0:T(8,128)S(1)}, f32[32,768]{1,0:T(8,128)S(1)}, u32[]{:S(2)}, u32[]{:S(2)}) collective-permute-start(f32[32,768]{1,0:T(8,128)S(1)} %add_add_fusion.1.refs_0_), channel_id=1, source_target_pairs={{0,16},{16,0},{1,17},{17,1},{2,18},{18,2},{3,19},{19,3},{4,20},{20... | collective-permute-start | bytes 294920 | tf_op jit(solution)/shard_map/ppermute | solution.py:207
  73.7 6.8 %factor.2.refs_2_ = f32[64,64]{1,0:T(8,128)} custom-call(f32[64,64]{1,0:T(8,128)} %copy-done.12), custom_call_target="tpu_custom_call" | custom-call | flops 524288 | bytes 32768 | tf_op jit(solution)/shard_map/factor/pallas_call | solution.py:183
  80.5 2.3 %copy-done.2 = bf16[1,3072,768]{2,1,0:T(8,128)(2,1)S(1)} copy-done((bf16[1,3072,768]{2,1,0:T(8,128)(2,1)S(1)}, bf16[1,3072,768]{2,1,0:T(8,128)(2,1)}, u32[]{:S(2)}) %copy-start.2) | copy-done | bytes 4718616
  82.9 2.3 %copy-done.7 = bf16[1,3072,768]{2,1,0:T(8,128)(2,1)S(1)} copy-done((bf16[1,3072,768]{2,1,0:T(8,128)(2,1)S(1)}, bf16[1,3072,768]{2,1,0:T(8,128)(2,1)}, u32[]{:S(2)}) %copy-start.7) | copy-done | bytes 4718616
  85.2 0.8 copy-done.11
  86.0 4.0 %left_pass.3 = (f32[4,32,768]{2,1,0:T(8,128)S(1)}, f32[4,32,768]{2,1,0:T(8,128)S(1)}) custom-call(s32[1]{0:T(128)} %bitcast.core, f32[32,768]{1,0:T(8,128)S(1)} %add_add_fusion.1.refs_0_, f32[32,768]{1,0:T(8,128)S(1)} %collective-permute-done.6.refs_1_, f32[64,64]{1,0:T(8,128)S(1)} %copy-done.11, bf16[3072,768]{1,0:T(8,128)(2,1)S(1)} %bitcast.6, ...), custom_call_target="tpu_custom_call" | custom-call | flops 1811939328 | bytes 9437184 | tf_op jit(solution)/shard_map/left_pass/pallas_call | solution.py:155
  90.1 1.7 %collective-permute-done.7 = f32[4,32,768]{2,1,0:T(8,128)S(1)} collective-permute-done((f32[4,32,768]{2,1,0:T(8,128)S(1)}, f32[4,32,768]{2,1,0:T(8,128)S(1)}, u32[]{:S(2)}, u32[]{:S(2)}) %collective-permute-start.7) | collective-permute-done | bytes 393248 | tf_op jit(solution)/shard_map/ppermute | solution.py:207
  92.1 15.3 %all_to_all.22 = f32[64,2,768]{2,1,0:T(2,128)S(1)} all-to-all(f32[64,2,768]{2,1,0:T(2,128)S(1)} %reshape.32), channel_id=1, replica_groups=mesh['y'=4,'core'=2,'x'=4,'z'=4] {'y','x','z'}, dimensions={0} | all-to-all | bytes 786432 | tf_op jit(solution)/shard_map/all_to_all | solution.py:216
  107.6 14.7 %all_to_all.23 = f32[64,2,768]{2,1,0:T(2,128)S(1)} all-to-all(f32[64,2,768]{2,1,0:T(2,128)S(1)} %broadcast_in_dim.7), channel_id=1, replica_groups=mesh['y'=4,'core'=2,'x'=4,'z'=4] {'y','x','z'}, dimensions={0} | all-to-all | bytes 786432 | tf_op jit(solution)/shard_map/all_to_all | solution.py:219
  122.3 0.3 reshape.33.l_mine
  122.6 3.2 %collective-permute-start.8 = (f32[4,32,768]{2,1,0:T(8,128)S(1)}, f32[4,32,768]{2,1,0:T(8,128)S(1)}, u32[]{:S(2)}, u32[]{:S(2)}) collective-permute-start(f32[4,32,768]{2,1,0:T(8,128)S(1)} %reshape.33.l_mine), channel_id=1, source_target_pairs={{0,16},{16,0},{1,17},{17,1},{2,18},{18,2},{3,19},{19,3},{4,20},{20... | collective-permute-start | bytes 1179656 | tf_op jit(solution)/shard_map/ppermute | solution.py:207
  125.7 1.3 collective-permute-done.8.l_other
  127.1 2.3 %copy-done.3 = bf16[1,3072,768]{2,1,0:T(8,128)(2,1)S(1)} copy-done((bf16[1,3072,768]{2,1,0:T(8,128)(2,1)S(1)}, bf16[1,3072,768]{2,1,0:T(8,128)(2,1)}, u32[]{:S(2)}) %copy-start.3) | copy-done | bytes 4718616
  129.4 2.3 %copy-done.8 = bf16[1,3072,768]{2,1,0:T(8,128)(2,1)S(1)} copy-done((bf16[1,3072,768]{2,1,0:T(8,128)(2,1)S(1)}, bf16[1,3072,768]{2,1,0:T(8,128)(2,1)}, u32[]{:S(2)}) %copy-start.8) | copy-done | bytes 4718616
  131.8 3.1 %right_pass.3 = (f32[32,768]{1,0:T(8,128)S(1)}, f32[32,768]{1,0:T(8,128)S(1)}, f32[64,64]{1,0:T(8,128)S(1)}) custom-call(s32[1]{0:T(128)} %bitcast.core, f32[4,32,768]{2,1,0:T(8,128)S(1)} %reshape.33.l_mine, f32[4,32,768]{2,1,0:T(8,128)S(1)} %collective-permute-done.8.l_other, bf16[3072,768]{1,0:T(8,128)(2,1)S(1)} %bitcast.7, bf16[3072,768]{1,0:T(8,128)(2,1)S(1)} %bitcast.12), custom_call_target="tpu_custom_call" | custom-call | flops 1811939328 | bytes 9437184 | tf_op jit(solution)/shard_map/right_pass/pallas_call | solution.py:169
  134.9 0.4 collective-permute-start.9
  135.3 0.9 collective-permute-done.9
  136.3 0.4 collective-permute-start.12
  136.7 2.1 %collective-permute-start.11 = (f32[32,768]{1,0:T(8,128)S(1)}, f32[32,768]{1,0:T(8,128)S(1)}, u32[]{:S(2)}, u32[]{:S(2)}) collective-permute-start(f32[32,768]{1,0:T(8,128)S(1)} %add.36), channel_id=1, source_target_pairs={{0,96},{32,0},{64,32},{96,64},{1,97},{33,1},{65,33},{97,65},{2,98}... | collective-permute-start | bytes 294920 | tf_op jit(solution)/shard_map/ppermute | solution.py:211
  138.8 3.1 %collective-permute-done.12 = f32[32,768]{1,0:T(8,128)S(1)} collective-permute-done((f32[32,768]{1,0:T(8,128)S(1)}, f32[32,768]{1,0:T(8,128)S(1)}, u32[]{:S(2)}, u32[]{:S(2)}) %collective-permute-start.12) | collective-permute-done | bytes 98336 | tf_op jit(solution)/shard_map/ppermute | solution.py:211
  142.2 1.7 collective-permute-done.10
  143.8 1.8 %collective-permute-start.13 = (f32[32,768]{1,0:T(8,128)S(1)}, f32[32,768]{1,0:T(8,128)S(1)}, u32[]{:S(2)}, u32[]{:S(2)}) collective-permute-start(f32[32,768]{1,0:T(8,128)S(1)} %add_add_fusion.z_mine), channel_id=1, source_target_pairs={{0,16},{16,0},{1,17},{17,1},{2,18},{18,2},{3,19},{19,3},{4,20},{20... | collective-permute-start | bytes 294920 | tf_op jit(solution)/shard_map/ppermute | solution.py:207
  145.7 6.8 %factor.3.inverse = f32[64,64]{1,0:T(8,128)} custom-call(f32[64,64]{1,0:T(8,128)} %copy-done.13), custom_call_target="tpu_custom_call" | custom-call | flops 524288 | bytes 32768 | tf_op jit(solution)/shard_map/factor/pallas_call | solution.py:183
  152.5 2.3 %copy-done.4 = bf16[1,3072,768]{2,1,0:T(8,128)(2,1)S(1)} copy-done((bf16[1,3072,768]{2,1,0:T(8,128)(2,1)S(1)}, bf16[1,3072,768]{2,1,0:T(8,128)(2,1)}, u32[]{:S(2)}) %copy-start.4) | copy-done | bytes 4718616
  154.8 2.3 %copy-done.9 = bf16[1,3072,768]{2,1,0:T(8,128)(2,1)S(1)} copy-done((bf16[1,3072,768]{2,1,0:T(8,128)(2,1)S(1)}, bf16[1,3072,768]{2,1,0:T(8,128)(2,1)}, u32[]{:S(2)}) %copy-start.9) | copy-done | bytes 4718616
  157.2 0.8 copy-done.10
  157.9 8.3 %renew.1 = (bf16[3072,768]{1,0:T(8,128)(2,1)}, bf16[3072,768]{1,0:T(8,128)(2,1)}, f32[768,64]{1,0:T(8,128)S(1)}) custom-call(s32[1]{0:T(128)} %bitcast.core, f32[32,768]{1,0:T(8,128)S(1)} %add_add_fusion.z_mine, f32[32,768]{1,0:T(8,128)S(1)} %collective-permute-done.13.z_other, f32[64,64]{1,0:T(8,128)S(1)} %copy-done.10, f32[4,32,768]{2,1,0:T(8,128)S(1)} %reshape.33.l_mine, ...), custom_call_target="tpu_custom_call" | custom-call | flops 905969664 | bytes 23592960 | tf_op jit(solution)/shard_map/renew/pallas_call | solution.py:193
  166.2 0.8 copy.8
  (37 shorter events, 1.8 us)
Async XLA Ops:
  1.7 2.3 %copy-start = (bf16[1,3072,768]{2,1,0:T(8,128)(2,1)S(1)}, bf16[1,3072,768]{2,1,0:T(8,128)(2,1)}, u32[]{:S(2)}) copy-start(bf16[1,3072,768]{2,1,0:T(8,128)(2,1)} %param.4) | copy-start | bytes 14155780
  4.1 2.3 %copy-start.5 = (bf16[1,3072,768]{2,1,0:T(8,128)(2,1)S(1)}, bf16[1,3072,768]{2,1,0:T(8,128)(2,1)}, u32[]{:S(2)}) copy-start(bf16[1,3072,768]{2,1,0:T(8,128)(2,1)} %param.5) | copy-start | bytes 14155780
  10.3 2.9 %collective-permute-start = (f32[4,32,768]{2,1,0:T(8,128)S(1)}, f32[4,32,768]{2,1,0:T(8,128)S(1)}, u32[]{:S(2)}, u32[]{:S(2)}) collective-permute-start(f32[4,32,768]{2,1,0:T(8,128)S(1)} %get-tuple-element.17), channel_id=1, source_target_pairs={{0,16},{16,0},{1,17},{17,1},{2,18},{18,2},{3,19},{19,3},{4,20},{20... | collective-permute-start | bytes 1179656 | tf_op jit(solution)/shard_map/ppermute | solution.py:207
  50.5 4.6 %collective-permute-start.1 = (f32[4,32,768]{2,1,0:T(8,128)S(1)}, f32[4,32,768]{2,1,0:T(8,128)S(1)}, u32[]{:S(2)}, u32[]{:S(2)}) collective-permute-start(f32[4,32,768]{2,1,0:T(8,128)S(1)} %reshape.31.l_mine), channel_id=1, source_target_pairs={{0,16},{16,0},{1,17},{17,1},{2,18},{18,2},{3,19},{19,3},{4,20},{20... | collective-permute-start | bytes 1179656 | tf_op jit(solution)/shard_map/ppermute | solution.py:207
  55.2 2.3 %copy-start.1 = (bf16[1,3072,768]{2,1,0:T(8,128)(2,1)S(1)}, bf16[1,3072,768]{2,1,0:T(8,128)(2,1)}, u32[]{:S(2)}) copy-start(bf16[1,3072,768]{2,1,0:T(8,128)(2,1)} %param.4) | copy-start | bytes 14155780
  57.5 2.3 %copy-start.6 = (bf16[1,3072,768]{2,1,0:T(8,128)(2,1)S(1)}, bf16[1,3072,768]{2,1,0:T(8,128)(2,1)}, u32[]{:S(2)}) copy-start(bf16[1,3072,768]{2,1,0:T(8,128)(2,1)} %param.5) | copy-start | bytes 14155780
  62.9 8.9 %copy-start.12 = (f32[64,64]{1,0:T(8,128)}, f32[64,64]{1,0:T(8,128)S(1)}, u32[]{:S(2)}) copy-start(f32[64,64]{1,0:T(8,128)S(1)} %get-tuple-element.20.gram) | copy-start | bytes 49156
  63.0 1.4 collective-permute-start.2
  64.4 5.6 %collective-permute-start.5 = (f32[32,768]{1,0:T(8,128)S(1)}, f32[32,768]{1,0:T(8,128)S(1)}, u32[]{:S(2)}, u32[]{:S(2)}) collective-permute-start(f32[32,768]{1,0:T(8,128)S(1)} %add.31), channel_id=1, source_target_pairs={{0,64},{32,96},{64,0},{96,32},{1,65},{33,97},{65,1},{97,33},{2,66}... | collective-permute-start | bytes 294920 | tf_op jit(solution)/shard_map/ppermute | solution.py:211
  64.8 5.4 %collective-permute-start.4 = (f32[32,768]{1,0:T(8,128)S(1)}, f32[32,768]{1,0:T(8,128)S(1)}, u32[]{:S(2)}, u32[]{:S(2)}) collective-permute-start(f32[32,768]{1,0:T(8,128)S(1)} %add.31), channel_id=1, source_target_pairs={{0,96},{32,0},{64,32},{96,64},{1,97},{33,1},{65,33},{97,65},{2,98}... | collective-permute-start | bytes 294920 | tf_op jit(solution)/shard_map/ppermute | solution.py:211
  66.8 5.0 %collective-permute-start.3 = (f32[32,768]{1,0:T(8,128)S(1)}, f32[32,768]{1,0:T(8,128)S(1)}, u32[]{:S(2)}, u32[]{:S(2)}) collective-permute-start(f32[32,768]{1,0:T(8,128)S(1)} %add.31), channel_id=1, source_target_pairs={{0,32},{32,64},{64,96},{96,0},{1,33},{33,65},{65,97},{97,1},{2,34}... | collective-permute-start | bytes 294920 | tf_op jit(solution)/shard_map/ppermute | solution.py:211
  71.9 8.6 %collective-permute-start.6 = (f32[32,768]{1,0:T(8,128)S(1)}, f32[32,768]{1,0:T(8,128)S(1)}, u32[]{:S(2)}, u32[]{:S(2)}) collective-permute-start(f32[32,768]{1,0:T(8,128)S(1)} %add_add_fusion.1.refs_0_), channel_id=1, source_target_pairs={{0,16},{16,0},{1,17},{17,1},{2,18},{18,2},{3,19},{19,3},{4,20},{20... | collective-permute-start | bytes 294920 | tf_op jit(solution)/shard_map/ppermute | solution.py:207
  80.5 2.3 %copy-start.2 = (bf16[1,3072,768]{2,1,0:T(8,128)(2,1)S(1)}, bf16[1,3072,768]{2,1,0:T(8,128)(2,1)}, u32[]{:S(2)}) copy-start(bf16[1,3072,768]{2,1,0:T(8,128)(2,1)} %param.4) | copy-start | bytes 14155780
  82.9 2.3 %copy-start.7 = (bf16[1,3072,768]{2,1,0:T(8,128)(2,1)S(1)}, bf16[1,3072,768]{2,1,0:T(8,128)(2,1)}, u32[]{:S(2)}) copy-start(bf16[1,3072,768]{2,1,0:T(8,128)(2,1)} %param.5) | copy-start | bytes 14155780
  85.2 0.8 copy-start.11
  90.0 1.8 %collective-permute-start.7 = (f32[4,32,768]{2,1,0:T(8,128)S(1)}, f32[4,32,768]{2,1,0:T(8,128)S(1)}, u32[]{:S(2)}, u32[]{:S(2)}) collective-permute-start(f32[4,32,768]{2,1,0:T(8,128)S(1)} %get-tuple-element.22), channel_id=1, source_target_pairs={{0,16},{16,0},{1,17},{17,1},{2,18},{18,2},{3,19},{19,3},{4,20},{20... | collective-permute-start | bytes 1179656 | tf_op jit(solution)/shard_map/ppermute | solution.py:207
  122.6 4.5 %collective-permute-start.8 = (f32[4,32,768]{2,1,0:T(8,128)S(1)}, f32[4,32,768]{2,1,0:T(8,128)S(1)}, u32[]{:S(2)}, u32[]{:S(2)}) collective-permute-start(f32[4,32,768]{2,1,0:T(8,128)S(1)} %reshape.33.l_mine), channel_id=1, source_target_pairs={{0,16},{16,0},{1,17},{17,1},{2,18},{18,2},{3,19},{19,3},{4,20},{20... | collective-permute-start | bytes 1179656 | tf_op jit(solution)/shard_map/ppermute | solution.py:207
  127.1 2.3 %copy-start.3 = (bf16[1,3072,768]{2,1,0:T(8,128)(2,1)S(1)}, bf16[1,3072,768]{2,1,0:T(8,128)(2,1)}, u32[]{:S(2)}) copy-start(bf16[1,3072,768]{2,1,0:T(8,128)(2,1)} %param.4) | copy-start | bytes 14155780
  129.4 2.3 %copy-start.8 = (bf16[1,3072,768]{2,1,0:T(8,128)(2,1)S(1)}, bf16[1,3072,768]{2,1,0:T(8,128)(2,1)}, u32[]{:S(2)}) copy-start(bf16[1,3072,768]{2,1,0:T(8,128)(2,1)} %param.5) | copy-start | bytes 14155780
  134.9 8.9 %copy-start.13 = (f32[64,64]{1,0:T(8,128)}, f32[64,64]{1,0:T(8,128)S(1)}, u32[]{:S(2)}) copy-start(f32[64,64]{1,0:T(8,128)S(1)} %get-tuple-element.25.gram) | copy-start | bytes 49156
  134.9 1.4 collective-permute-start.9
  136.3 5.6 %collective-permute-start.12 = (f32[32,768]{1,0:T(8,128)S(1)}, f32[32,768]{1,0:T(8,128)S(1)}, u32[]{:S(2)}, u32[]{:S(2)}) collective-permute-start(f32[32,768]{1,0:T(8,128)S(1)} %add.36), channel_id=1, source_target_pairs={{0,64},{32,96},{64,0},{96,32},{1,65},{33,97},{65,1},{97,33},{2,66}... | collective-permute-start | bytes 294920 | tf_op jit(solution)/shard_map/ppermute | solution.py:211
  136.7 5.4 %collective-permute-start.11 = (f32[32,768]{1,0:T(8,128)S(1)}, f32[32,768]{1,0:T(8,128)S(1)}, u32[]{:S(2)}, u32[]{:S(2)}) collective-permute-start(f32[32,768]{1,0:T(8,128)S(1)} %add.36), channel_id=1, source_target_pairs={{0,96},{32,0},{64,32},{96,64},{1,97},{33,1},{65,33},{97,65},{2,98}... | collective-permute-start | bytes 294920 | tf_op jit(solution)/shard_map/ppermute | solution.py:211
  138.8 5.0 %collective-permute-start.10 = (f32[32,768]{1,0:T(8,128)S(1)}, f32[32,768]{1,0:T(8,128)S(1)}, u32[]{:S(2)}, u32[]{:S(2)}) collective-permute-start(f32[32,768]{1,0:T(8,128)S(1)} %add.36), channel_id=1, source_target_pairs={{0,32},{32,64},{64,96},{96,0},{1,33},{33,65},{65,97},{97,1},{2,34}... | collective-permute-start | bytes 294920 | tf_op jit(solution)/shard_map/ppermute | solution.py:211
  143.8 8.6 %collective-permute-start.13 = (f32[32,768]{1,0:T(8,128)S(1)}, f32[32,768]{1,0:T(8,128)S(1)}, u32[]{:S(2)}, u32[]{:S(2)}) collective-permute-start(f32[32,768]{1,0:T(8,128)S(1)} %add_add_fusion.z_mine), channel_id=1, source_target_pairs={{0,16},{16,0},{1,17},{17,1},{2,18},{18,2},{3,19},{19,3},{4,20},{20... | collective-permute-start | bytes 294920 | tf_op jit(solution)/shard_map/ppermute | solution.py:207
  152.5 2.3 %copy-start.4 = (bf16[1,3072,768]{2,1,0:T(8,128)(2,1)S(1)}, bf16[1,3072,768]{2,1,0:T(8,128)(2,1)}, u32[]{:S(2)}) copy-start(bf16[1,3072,768]{2,1,0:T(8,128)(2,1)} %param.4) | copy-start | bytes 14155780
  154.8 2.3 %copy-start.9 = (bf16[1,3072,768]{2,1,0:T(8,128)(2,1)S(1)}, bf16[1,3072,768]{2,1,0:T(8,128)(2,1)}, u32[]{:S(2)}) copy-start(bf16[1,3072,768]{2,1,0:T(8,128)(2,1)} %param.5) | copy-start | bytes 14155780
  157.2 0.8 copy-start.10

commit v2 on v1

v2 whole, which is shorter than its diff:
```python
import jax
import jax.numpy as jnp
from jax import lax
from jax.experimental import pallas as pl
from jax.experimental.pallas import tpu as pltpu
from jax.sharding import Mesh, PartitionSpec as P

F32, BF16 = jnp.float32, jnp.bfloat16
HIGH = lax.Precision.HIGHEST
RANK, HALF = 64, 32
ROWS, COLS = 3072, 768
BLOCK = 768
BLOCKS = ROWS // BLOCK
WIDE = 256
SLAB = 384
SLABS = ROWS // SLAB
CHIPS = 64
TILES = HALF * ROWS // 512
REPLICAS = 8
CHIP_AXES = ("y", "x", "z")
LIMIT, SMALL = 32 * 2**20, 8 * 2**20


def split(x, parts):
    terms = []
    for _ in range(parts):
        term = x.astype(BF16)
        terms.append(term)
        x = x - term.astype(F32)
    return terms


def fold(x):
    return x[:RANK] + (x[RANK : 2 * RANK] + x[2 * RANK :])


def ordered(core, mine, other):
    first = core == 0
    return jnp.concatenate([jnp.where(first, mine, other), jnp.where(first, other, mine)], axis=0)


def parted(core, x):
    first = core == 0
    top, bottom = x[:HALF], x[HALF:]
    return jnp.where(first, top, bottom), jnp.where(first, bottom, top)


def put(pieces, block, x):
    for lane in range(BLOCK // 128):
        for group in range(HALF // 4):
            tile = (block * (BLOCK // 128) + lane) * (HALF // 4) + group
            pieces[tile] = x[4 * group : 4 * group + 4, 128 * lane : 128 * lane + 128]


def take(pieces, block):
    columns = []
    for lane in range(BLOCK // 128):
        start = (block * (BLOCK // 128) + lane) * (HALF // 4)
        columns.append(jnp.concatenate([pieces[start + group] for group in range(HALF // 4)], axis=0))
    return jnp.concatenate(columns, axis=1)


def put_both(core, mine, other, block, x):
    for pieces, half in zip((mine, other), parted(core, x)):
        put(pieces, block, half)


def mean_kernel(terms, out):
    share = terms[...].reshape(CHIPS, TILES // CHIPS, 4, 128)
    total = jnp.sum(share, axis=0) * (1.0 / REPLICAS)
    out[...] = jnp.broadcast_to(total[None], share.shape).reshape(out.shape)


def stacked(x):
    return jnp.concatenate(split(x, 3), axis=0)


def times_rows(stack, g, e, block):
    rows = pl.ds(block * BLOCK, BLOCK)
    across = (((1,), (1,)), ((), ()))
    p = lax.dot_general(stack[...], g[rows, :], across, preferred_element_type=F32)
    return fold(p + lax.dot_general(stack[...], e[rows, :], across, preferred_element_type=F32))


def first_left_kernel(core, q, g_far, e_far, mine, other, g, e, stack, g_sem, e_sem):
    copies = []
    for block in range(BLOCKS):
        rows = pl.ds(block * BLOCK, BLOCK)
        pair = (
            pltpu.make_async_copy(g_far.at[rows, :], g.at[rows, :], g_sem.at[block]),
            pltpu.make_async_copy(e_far.at[rows, :], e.at[rows, :], e_sem.at[block]),
        )
        for copy in pair:
            copy.start()
        copies.append(pair)
    stack[...] = stacked(q[...])
    for block, pair in enumerate(copies):
        for copy in pair:
            copy.wait()
        put_both(core[0], mine, other, block, times_rows(stack, g, e, block))


def left_kernel(core, z_mine, z_other, inverse, g, e, mine, other, stack):
    z = ordered(core[0], z_mine[...], z_other[...])
    right = jnp.dot(inverse[...], z, precision=HIGH, preferred_element_type=F32) * (1.0 / REPLICAS)
    stack[...] = stacked(right)
    for block in range(BLOCKS):
        put_both(core[0], mine, other, block, times_rows(stack, g, e, block))


def right_kernel(core, l_mine, l_other, g, e, z_mine, z_other, gram, stack):
    for block in range(BLOCKS):
        left = ordered(core[0], take(l_mine, block), take(l_other, block))
        stack[:, pl.ds(block * BLOCK, BLOCK)] = stacked(left)
    for part in range(COLS // WIDE):
        cols = pl.ds(part * WIDE, WIDE)
        z = jnp.dot(stack[...], g[:, cols], preferred_element_type=F32)
        z = fold(z + jnp.dot(stack[...], e[:, cols], preferred_element_type=F32))
        z_mine[:, cols], z_other[:, cols] = parted(core[0], z)
    products = lax.dot_general(stack[...], stack[...], (((1,), (1,)), ((), ())), preferred_element_type=F32)
    rows = fold(products)
    gram[...] = rows[:, :RANK] + (rows[:, RANK : 2 * RANK] + rows[:, 2 * RANK :])


def factor_kernel(gram, inverse):
    rows = lax.broadcasted_iota(jnp.int32, (RANK, RANK), 0)
    cols = lax.broadcasted_iota(jnp.int32, (RANK, RANK), 1)
    work = jnp.concatenate([gram[...], (rows == cols).astype(F32)], axis=1)
    for start in range(0, RANK, 8):
        column = [jnp.broadcast_to(work[:, start + j : start + j + 1], work.shape) for j in range(8)]
        row = [work[j : j + 1, :] for j in range(8)]
        for j in range(8):
            pivot = column[j][j : j + 1, :]
            inverse[start + j : start + j + 1, :] = (row[j] * lax.rsqrt(pivot))[:, RANK:]
            scaled = row[j] / pivot
            for i in range(j + 1, 8):
                factor = column[i][j : j + 1, :] / pivot
                row[i] = row[i] - column[i][j : j + 1, :] * scaled
                column[i] = column[i] - column[j] * factor
            if start + 8 < RANK:
                work = work - column[j] * scaled
        work = work[8:]


def renew_kernel(
    core, z_mine, z_other, inverse, l_mine, l_other, g, e, w_far, new_e, new_w, right_out, stack, e_near, w_near, in_sem, e_sem, w_sem
):
    def rows(step):
        return pl.ds(step * SLAB, SLAB)

    loads = []
    for step in range(SLABS):
        loads.append(pltpu.make_async_copy(w_far.at[rows(step), :], w_near.at[rows(step), :], in_sem.at[step]))
        loads[-1].start()
    z = ordered(core[0], z_mine[...], z_other[...])
    right = jnp.dot(inverse[...], z, precision=HIGH, preferred_element_type=F32) * (1.0 / REPLICAS)
    right_out[...] = right
    mixed = lax.dot_general(inverse[...], right, (((0,), (0,)), ((), ())), precision=HIGH, preferred_element_type=F32)
    high, low = split(mixed, 2)
    stack[...] = jnp.concatenate([high, low, high], axis=0)
    stores = []
    for step in range(SLABS):
        block, within = divmod(step * SLAB, BLOCK)
        if within == 0:
            whole = ordered(core[0], take(l_mine, block), take(l_other, block))
        left = whole[:, within : within + SLAB]
        high, low = split(left, 2)
        factors = jnp.concatenate([high, high, low], axis=0)
        approx = lax.dot_general(factors, stack[...], (((0,), (0,)), ((), ())), preferred_element_type=F32)
        merged = g[rows(step), :].astype(F32) + e[rows(step), :].astype(F32)
        e_near[rows(step), :] = (merged - approx).astype(BF16)
        stores.append(pltpu.make_async_copy(e_near.at[rows(step), :], new_e.at[rows(step), :], e_sem.at[step]))
        stores[-1].start()
        loads[step].wait()
        w_near[rows(step), :] = (w_near[rows(step), :].astype(F32) - 0.5 * approx).astype(BF16)
        stores.append(pltpu.make_async_copy(w_near.at[rows(step), :], new_w.at[rows(step), :], w_sem.at[step]))
        stores[-1].start()
    for store in stores:
        store.wait()


SCALAR = pl.BlockSpec(memory_space=pltpu.SMEM)
NEAR = pl.BlockSpec(memory_space=pltpu.VMEM)
FAR = pl.BlockSpec(memory_space=pltpu.HBM)
PIECES = jax.ShapeDtypeStruct((TILES, 4, 128), F32)
ZHALF = jax.ShapeDtypeStruct((HALF, COLS), F32)
SQUARE = jax.ShapeDtypeStruct((RANK, RANK), F32)
STACK = pltpu.VMEM((3 * RANK, COLS), BF16)


def cost(products, nbytes):
    return pl.CostEstimate(flops=2 * ROWS * COLS * RANK * products, bytes_accessed=nbytes, transcendentals=0)


def params(limit):
    return pltpu.CompilerParams(vmem_limit_bytes=limit)


def near(*arrays):
    return [pltpu.with_memory_space_constraint(x, pltpu.VMEM) for x in arrays]


def far(*arrays):
    return [pltpu.with_memory_space_constraint(x, pltpu.HBM) for x in arrays]


def first_left_pass(core, q, g, e):
    return pl.pallas_call(
        first_left_kernel,
        in_specs=[SCALAR, NEAR, FAR, FAR],
        out_specs=[NEAR] * 4,
        out_shape=[PIECES, PIECES, pltpu.VMEM((ROWS, COLS), BF16), pltpu.VMEM((ROWS, COLS), BF16)],
        scratch_shapes=[STACK, pltpu.SemaphoreType.DMA((BLOCKS,)), pltpu.SemaphoreType.DMA((BLOCKS,))],
        compiler_params=params(LIMIT),
        cost_estimate=cost(6, 4 * ROWS * COLS),
        name="first_left_pass",
    )(core, q, *far(g, e))


def left_pass(core, z_mine, z_other, inverse, g, e):
    return pl.pallas_call(
        left_kernel,
        in_specs=[SCALAR] + [NEAR] * 5,
        out_specs=[NEAR] * 2,
        out_shape=[PIECES, PIECES],
        scratch_shapes=[STACK],
        compiler_params=params(LIMIT),
        cost_estimate=cost(6, 4 * ROWS * COLS),
        name="left_pass",
    )(core, z_mine, z_other, inverse, *near(g, e))


def right_pass(core, l_mine, l_other, g, e):
    return pl.pallas_call(
        right_kernel,
        in_specs=[SCALAR] + [NEAR] * 4,
        out_specs=[NEAR] * 3,
        out_shape=[ZHALF, ZHALF, SQUARE],
        scratch_shapes=[pltpu.VMEM((3 * RANK, ROWS), BF16)],
        compiler_params=params(LIMIT),
        cost_estimate=cost(6, 4 * ROWS * COLS),
        name="right_pass",
    )(core, l_mine, l_other, *near(g, e))


def factor(gram):
    return pl.pallas_call(
        factor_kernel,
        out_shape=SQUARE,
        compiler_params=params(SMALL),
        cost_estimate=pl.CostEstimate(flops=4 * 10**9, bytes_accessed=8 * RANK**2, transcendentals=RANK),
        name="factor",
    )(gram)


def renew(core, z_mine, z_other, inverse, l_mine, l_other, g, e, w):
    array = jax.ShapeDtypeStruct((ROWS, COLS), BF16)
    return pl.pallas_call(
        renew_kernel,
        in_specs=[SCALAR] + [NEAR] * 7 + [FAR],
        out_specs=[FAR, FAR, NEAR],
        out_shape=[array, array, jax.ShapeDtypeStruct((RANK, COLS), F32)],
        scratch_shapes=[
            STACK,
            pltpu.VMEM((ROWS, COLS), BF16),
            pltpu.VMEM((ROWS, COLS), BF16),
            *[pltpu.SemaphoreType.DMA((SLABS,)) for _ in range(3)],
        ],
        compiler_params=params(LIMIT),
        cost_estimate=cost(3, 10 * ROWS * COLS),
        name="renew",
    )(core, z_mine, z_other, inverse, l_mine, l_other, *near(g, e), *far(w))


def swap(x):
    return lax.ppermute(x, "core", [(0, 1), (1, 0)])


def along_y(x, shift):
    return lax.ppermute(x, "y", [(i, (i + shift) % 4) for i in range(4)])


def mean(terms):
    return pl.pallas_call(
        mean_kernel,
        out_shape=PIECES,
        compiler_params=params(SMALL),
        cost_estimate=pl.CostEstimate(flops=HALF * ROWS, bytes_accessed=8 * HALF * ROWS, transcendentals=0),
        name="mean",
    )(terms)


def exchange(x):
    x = x.reshape(CHIPS, TILES // CHIPS, 4, 128)
    return lax.all_to_all(x, CHIP_AXES, 0, 0, tiled=True).reshape(TILES, 4, 128)


def sum_left(mine, other):
    term = exchange(mean(exchange(mine + swap(other))))
    return term, swap(term)


def sum_right(mine, other):
    half = mine + swap(other)
    parts = [along_y(half, shift) for shift in (1, 3, 2)]
    half = half + parts[0] + parts[1] + parts[2]
    return half, swap(half)


def shards(gradients, errors, weight, start_q):
    g, e = gradients[0], errors[0]
    core = lax.axis_index("core").astype(jnp.int32).reshape(1)
    mine, other, g, e = first_left_pass(core, start_q.T, g, e)
    left = sum_left(mine, other)
    z_mine, z_other, gram = right_pass(core, *left, g, e)
    right = (*sum_right(z_mine, z_other), factor(gram))
    left = sum_left(*left_pass(core, *right, g, e))
    z_mine, z_other, gram = right_pass(core, *left, g, e)
    right = (*sum_right(z_mine, z_other), factor(gram))
    new_e, new_w, right_factor = renew(core, *right, *left, g, e, weight)
    return new_e[None], new_w, right_factor.T


def solution(mesh):
    chips = Mesh(mesh.devices.reshape(4, 2, 4, 4), ("y", "core", "x", "z"))
    dp, tensor = ("y", "core"), ("x", "z")
    return jax.shard_map(
        shards,
        mesh=chips,
        in_specs=(P(dp, None, tensor), P(dp, None, tensor), P(None, tensor), P(tensor, None)),
        out_specs=(P(dp, None, tensor), P(None, tensor), P(tensor, None)),
        check_vma=False,
    )
```

time: 168 us -> 129 us (0.77)
  local copies, waits for them, and re-layouts: 28 us -> 0.92 us
  Pallas kernels: 36.1 us -> 25.3 us
    unnamed x30 -> x2, local copies, waits for them, and re-layouts: 26.8 us -> 0.92 us
    pallas_call x7 -> x9, Pallas kernels: 36.1 us -> 25.3 us  [the longest x1 7.35 us: renew(): pl.pallas_call(renew_kernel, in_specs=[SCALAR] + [NEAR] * 7 + [FAR], out_...]
  transfers between devices with their start and end apart: 14 -> 14, of which waited for: 12 -> 12; matrix products, arithmetic and copies ran while one was open for 0% -> 0% of each run, Pallas kernels for 8% -> 3%
where the time goes in v2:
time: 129 us
  blocking collectives  66.7 us (52%)
  Pallas kernels  25.3 us (20%)
  waiting for transfers between devices  17.7 us (14%)
  starting transfers between devices  17.2 us (13%)
    all_to_all x4, blocking collectives, exchange(): return lax.all_to_all(x, CHIP_AXES, 0, 0, tiled=True).reshape(TILES, 4, 128)  66.7 us
    ppermute x8, starting transfers between devices, swap(): return lax.ppermute(x, 'core', [(0, 1), (1, 0)])  12.2 us
    ppermute x6, waiting for transfers between devices, along_y(): return lax.ppermute(x, 'y', [(i, (i + shift) % 4) for i in range(4)])  10 us
    ppermute x8, waiting for transfers between devices, swap(): return lax.ppermute(x, 'core', [(0, 1), (1, 0)])  7.65 us
    pallas_call x1, Pallas kernels, renew(): pl.pallas_call(renew_kernel, in_specs=[SCALAR] + [NEAR] * 7 + [FAR], out_...  7.35 us
    pallas_call x1, Pallas kernels, first_left_pass(): pl.pallas_call(first_left_kernel, in_specs=[SCALAR, NEAR, FAR, FAR], out_...  6.02 us
    ppermute x6, starting transfers between devices, along_y(): return lax.ppermute(x, 'y', [(i, (i + shift) % 4) for i in range(4)])  4.98 us
    pallas_call x2, Pallas kernels, right_pass(): pl.pallas_call(right_kernel, in_specs=[SCALAR] + [NEAR] * 4, out_specs=[N...  4.93 us
  transfers between devices with their start and end apart: 14, of which 12 were waited for; matrix products, arithmetic and copies ran while one was open for 0% of the time, Pallas kernels for 3%

profile of v2, /device:TPU:1, one launch (start us, length us, event | category | flops | bytes accessed | tf_op | source)
XLA Modules:
  0.0 128.9 jit_solution(14390763430132282120)
XLA Ops:
  0.6 0.0 copy-start
  0.6 0.9 copy-done
  1.6 6.0 %first_left_pass.1 = (f32[192,4,128]{2,1,0:T(4,128)S(1)}, f32[192,4,128]{2,1,0:T(4,128)S(1)}, bf16[3072,768]{1,0:T(8,128)(2,1)S(1)}, bf16[3072,768]{1,0:T(8,128)(2,1)S(1)}) custom-call(s32[1]{0:T(128)} %bitcast.core, f32[64,768]{1,0:T(8,128)S(1)} %bitcast.23, bf16[3072,768]{1,0:T(8,128)(2,1)} %bitcast.24, bf16[3072,768]{1,0:T(8,128)(2,1)} %bitcast.25), custom_call_target="tpu_custom_call" | custom-call | flops 1811939328 | bytes 9437184 | tf_op jit(solution)/shard_map/first_left_pass/pallas_call | solution.py:208
  7.6 1.5 %collective-permute-start = (f32[192,4,128]{2,1,0:T(4,128)S(1)}, f32[192,4,128]{2,1,0:T(4,128)S(1)}, u32[]{:S(2)}, u32[]{:S(2)}) collective-permute-start(f32[192,4,128]{2,1,0:T(4,128)S(1)} %get-tuple-element.19), channel_id=1, source_target_pairs={{0,16},{16,0},{1,17},{17,1},{2,18},{18,2},{3,19},{19,3},{4,20},{20... | collective-permute-start | bytes 1179656 | tf_op jit(solution)/shard_map/ppermute | solution.py:276
  9.1 1.3 %collective-permute-done = f32[192,4,128]{2,1,0:T(4,128)S(1)} collective-permute-done((f32[192,4,128]{2,1,0:T(4,128)S(1)}, f32[192,4,128]{2,1,0:T(4,128)S(1)}, u32[]{:S(2)}, u32[]{:S(2)}) %collective-permute-start) | collective-permute-done | bytes 393248 | tf_op jit(solution)/shard_map/ppermute | solution.py:276
  10.4 0.1 add.30
  10.5 22.0 %all_to_all.20 = f32[64,3,4,128]{3,2,1,0:T(4,128)S(1)} all-to-all(f32[64,3,4,128]{3,2,1,0:T(4,128)S(1)} %bitcast.26), channel_id=1, replica_groups=mesh['y'=4,'core'=2,'x'=4,'z'=4] {'y','x','z'}, dimensions={0} | all-to-all | bytes 786432 | tf_op jit(solution)/shard_map/all_to_all | solution.py:295
  32.5 0.1 mean.2
  32.6 14.6 %all_to_all.21 = f32[64,3,4,128]{3,2,1,0:T(4,128)S(1)} all-to-all(f32[64,3,4,128]{3,2,1,0:T(4,128)S(1)} %bitcast.20), channel_id=1, replica_groups=mesh['y'=4,'core'=2,'x'=4,'z'=4] {'y','x','z'}, dimensions={0} | all-to-all | bytes 786432 | tf_op jit(solution)/shard_map/all_to_all | solution.py:295
  47.2 3.2 %collective-permute-start.1 = (f32[192,4,128]{2,1,0:T(4,128)S(1)}, f32[192,4,128]{2,1,0:T(4,128)S(1)}, u32[]{:S(2)}, u32[]{:S(2)}) collective-permute-start(f32[192,4,128]{2,1,0:T(4,128)S(1)} %bitcast.17), channel_id=1, source_target_pairs={{0,16},{16,0},{1,17},{17,1},{2,18},{18,2},{3,19},{19,3},{4,20},{20... | collective-permute-start | bytes 1179656 | tf_op jit(solution)/shard_map/ppermute | solution.py:276
  50.4 1.3 %collective-permute-done.1.l_other = f32[192,4,128]{2,1,0:T(4,128)S(1)} collective-permute-done((f32[192,4,128]{2,1,0:T(4,128)S(1)}, f32[192,4,128]{2,1,0:T(4,128)S(1)}, u32[]{:S(2)}, u32[]{:S(2)}) %collective-permute-start.1) | collective-permute-done | bytes 393248 | tf_op jit(solution)/shard_map/ppermute | solution.py:276
  51.8 2.5 %right_pass.2 = (f32[32,768]{1,0:T(8,128)S(1)}, f32[32,768]{1,0:T(8,128)S(1)}, f32[64,64]{1,0:T(8,128)S(1)}) custom-call(s32[1]{0:T(128)} %bitcast.core, f32[192,4,128]{2,1,0:T(4,128)S(1)} %bitcast.18, f32[192,4,128]{2,1,0:T(4,128)S(1)} %collective-permute-done.1.l_other, bf16[3072,768]{1,0:T(8,128)(2,1)S(1)} %get-tuple-element.20.g, ...), custom_call_target="tpu_custom_call" | custom-call | flops 1811939328 | bytes 9437184 | tf_op jit(solution)/shard_map/right_pass/pallas_call | solution.py:234
  54.3 0.5 collective-permute-start.2
  54.7 0.9 collective-permute-done.2
  55.7 0.4 collective-permute-start.5
  56.1 2.0 %collective-permute-start.4 = (f32[32,768]{1,0:T(8,128)S(1)}, f32[32,768]{1,0:T(8,128)S(1)}, u32[]{:S(2)}, u32[]{:S(2)}) collective-permute-start(f32[32,768]{1,0:T(8,128)S(1)} %add.31), channel_id=1, source_target_pairs={{0,96},{32,0},{64,32},{96,64},{1,97},{33,1},{65,33},{97,65},{2,98}... | collective-permute-start | bytes 294920 | tf_op jit(solution)/shard_map/ppermute | solution.py:280
  58.1 0.0 collective-permute-start.3
  58.1 3.1 %collective-permute-done.5 = f32[32,768]{1,0:T(8,128)S(1)} collective-permute-done((f32[32,768]{1,0:T(8,128)S(1)}, f32[32,768]{1,0:T(8,128)S(1)}, u32[]{:S(2)}, u32[]{:S(2)}) %collective-permute-start.5) | collective-permute-done | bytes 98336 | tf_op jit(solution)/shard_map/ppermute | solution.py:280
  61.3 0.2 collective-permute-done.4
  61.5 1.7 %collective-permute-done.3 = f32[32,768]{1,0:T(8,128)S(1)} collective-permute-done((f32[32,768]{1,0:T(8,128)S(1)}, f32[32,768]{1,0:T(8,128)S(1)}, u32[]{:S(2)}, u32[]{:S(2)}) %collective-permute-start.3) | collective-permute-done | bytes 98336 | tf_op jit(solution)/shard_map/ppermute | solution.py:280
  63.2 1.8 %collective-permute-start.6 = (f32[32,768]{1,0:T(8,128)S(1)}, f32[32,768]{1,0:T(8,128)S(1)}, u32[]{:S(2)}, u32[]{:S(2)}) collective-permute-start(f32[32,768]{1,0:T(8,128)S(1)} %add_add_fusion.1.z_mine), channel_id=1, source_target_pairs={{0,16},{16,0},{1,17},{17,1},{2,18},{18,2},{3,19},{19,3},{4,20},{20... | collective-permute-start | bytes 294920 | tf_op jit(solution)/shard_map/ppermute | solution.py:276
  65.0 1.6 %factor.2.inverse = f32[64,64]{1,0:T(8,128)S(1)} custom-call(f32[64,64]{1,0:T(8,128)S(1)} %get-tuple-element.24.gram), custom_call_target="tpu_custom_call" | custom-call | flops 4000000000 | bytes 32768 | tf_op jit(solution)/shard_map/factor/pallas_call | solution.py:247
  66.7 0.0 collective-permute-done.6.z_other
  66.7 3.4 %left_pass.1 = (f32[192,4,128]{2,1,0:T(4,128)S(1)}, f32[192,4,128]{2,1,0:T(4,128)S(1)}) custom-call(s32[1]{0:T(128)} %bitcast.core, f32[32,768]{1,0:T(8,128)S(1)} %add_add_fusion.1.z_mine, f32[32,768]{1,0:T(8,128)S(1)} %collective-permute-done.6.z_other, f32[64,64]{1,0:T(8,128)S(1)} %factor.2.inverse, bf16[3072,768]{1,0:T(8,128)(2,1)S(1)} %get-tuple-element.20.g, ...), custom_call_target="tpu_custom_call" | custom-call | flops 1811939328 | bytes 9437184 | tf_op jit(solution)/shard_map/left_pass/pallas_call | solution.py:221
  70.1 0.1 collective-permute-start.7
  70.2 1.7 %collective-permute-done.7 = f32[192,4,128]{2,1,0:T(4,128)S(1)} collective-permute-done((f32[192,4,128]{2,1,0:T(4,128)S(1)}, f32[192,4,128]{2,1,0:T(4,128)S(1)}, u32[]{:S(2)}, u32[]{:S(2)}) %collective-permute-start.7) | collective-permute-done | bytes 393248 | tf_op jit(solution)/shard_map/ppermute | solution.py:276
  71.9 0.1 add.35
  72.0 15.4 %all_to_all.22 = f32[64,3,4,128]{3,2,1,0:T(4,128)S(1)} all-to-all(f32[64,3,4,128]{3,2,1,0:T(4,128)S(1)} %bitcast.27), channel_id=1, replica_groups=mesh['y'=4,'core'=2,'x'=4,'z'=4] {'y','x','z'}, dimensions={0} | all-to-all | bytes 786432 | tf_op jit(solution)/shard_map/all_to_all | solution.py:295
  87.4 0.1 mean.3
  87.5 14.7 %all_to_all.23 = f32[64,3,4,128]{3,2,1,0:T(4,128)S(1)} all-to-all(f32[64,3,4,128]{3,2,1,0:T(4,128)S(1)} %bitcast.22), channel_id=1, replica_groups=mesh['y'=4,'core'=2,'x'=4,'z'=4] {'y','x','z'}, dimensions={0} | all-to-all | bytes 786432 | tf_op jit(solution)/shard_map/all_to_all | solution.py:295
  102.2 2.9 %collective-permute-start.8 = (f32[192,4,128]{2,1,0:T(4,128)S(1)}, f32[192,4,128]{2,1,0:T(4,128)S(1)}, u32[]{:S(2)}, u32[]{:S(2)}) collective-permute-start(f32[192,4,128]{2,1,0:T(4,128)S(1)} %bitcast.14), channel_id=1, source_target_pairs={{0,16},{16,0},{1,17},{17,1},{2,18},{18,2},{3,19},{19,3},{4,20},{20... | collective-permute-start | bytes 1179656 | tf_op jit(solution)/shard_map/ppermute | solution.py:276
  105.1 1.3 %collective-permute-done.8.l_other = f32[192,4,128]{2,1,0:T(4,128)S(1)} collective-permute-done((f32[192,4,128]{2,1,0:T(4,128)S(1)}, f32[192,4,128]{2,1,0:T(4,128)S(1)}, u32[]{:S(2)}, u32[]{:S(2)}) %collective-permute-start.8) | collective-permute-done | bytes 393248 | tf_op jit(solution)/shard_map/ppermute | solution.py:276
  106.5 2.5 %right_pass.3 = (f32[32,768]{1,0:T(8,128)S(1)}, f32[32,768]{1,0:T(8,128)S(1)}, f32[64,64]{1,0:T(8,128)S(1)}) custom-call(s32[1]{0:T(128)} %bitcast.core, f32[192,4,128]{2,1,0:T(4,128)S(1)} %bitcast.15, f32[192,4,128]{2,1,0:T(4,128)S(1)} %collective-permute-done.8.l_other, bf16[3072,768]{1,0:T(8,128)(2,1)S(1)} %get-tuple-element.20.g, ...), custom_call_target="tpu_custom_call" | custom-call | flops 1811939328 | bytes 9437184 | tf_op jit(solution)/shard_map/right_pass/pallas_call | solution.py:234
  108.9 0.5 collective-permute-start.9
  109.4 0.9 collective-permute-done.9
  110.4 0.4 collective-permute-start.12
  110.8 2.1 %collective-permute-start.11 = (f32[32,768]{1,0:T(8,128)S(1)}, f32[32,768]{1,0:T(8,128)S(1)}, u32[]{:S(2)}, u32[]{:S(2)}) collective-permute-start(f32[32,768]{1,0:T(8,128)S(1)} %add.36), channel_id=1, source_target_pairs={{0,96},{32,0},{64,32},{96,64},{1,97},{33,1},{65,33},{97,65},{2,98}... | collective-permute-start | bytes 294920 | tf_op jit(solution)/shard_map/ppermute | solution.py:280
  112.9 0.0 collective-permute-start.10
  112.9 3.1 %collective-permute-done.12 = f32[32,768]{1,0:T(8,128)S(1)} collective-permute-done((f32[32,768]{1,0:T(8,128)S(1)}, f32[32,768]{1,0:T(8,128)S(1)}, u32[]{:S(2)}, u32[]{:S(2)}) %collective-permute-start.12) | collective-permute-done | bytes 98336 | tf_op jit(solution)/shard_map/ppermute | solution.py:280
  116.0 0.3 collective-permute-done.11
  116.2 1.7 %collective-permute-done.10 = f32[32,768]{1,0:T(8,128)S(1)} collective-permute-done((f32[32,768]{1,0:T(8,128)S(1)}, f32[32,768]{1,0:T(8,128)S(1)}, u32[]{:S(2)}, u32[]{:S(2)}) %collective-permute-start.10) | collective-permute-done | bytes 98336 | tf_op jit(solution)/shard_map/ppermute | solution.py:280
  117.9 1.8 %collective-permute-start.13 = (f32[32,768]{1,0:T(8,128)S(1)}, f32[32,768]{1,0:T(8,128)S(1)}, u32[]{:S(2)}, u32[]{:S(2)}) collective-permute-start(f32[32,768]{1,0:T(8,128)S(1)} %add_add_fusion.z_mine), channel_id=1, source_target_pairs={{0,16},{16,0},{1,17},{17,1},{2,18},{18,2},{3,19},{19,3},{4,20},{20... | collective-permute-start | bytes 294920 | tf_op jit(solution)/shard_map/ppermute | solution.py:276
  119.7 1.6 %factor.3.inverse = f32[64,64]{1,0:T(8,128)S(1)} custom-call(f32[64,64]{1,0:T(8,128)S(1)} %get-tuple-element.29.gram), custom_call_target="tpu_custom_call" | custom-call | flops 4000000000 | bytes 32768 | tf_op jit(solution)/shard_map/factor/pallas_call | solution.py:247
  121.4 0.0 collective-permute-done.13.z_other
  121.4 7.4 %renew.1 = (bf16[3072,768]{1,0:T(8,128)(2,1)}, bf16[3072,768]{1,0:T(8,128)(2,1)}, f32[64,768]{1,0:T(8,128)}) custom-call(s32[1]{0:T(128)} %bitcast.core, f32[32,768]{1,0:T(8,128)S(1)} %add_add_fusion.z_mine, f32[32,768]{1,0:T(8,128)S(1)} %collective-permute-done.13.z_other, f32[64,64]{1,0:T(8,128)S(1)} %factor.3.inverse, f32[192,4,128]{2,1,0:T(4,128)S(1)} %bitcast.16, ...), custom_call_target="tpu_custom_call" | custom-call | flops 905969664 | bytes 23592960 | tf_op jit(solution)/shard_map/renew/pallas_call | solution.py:258
  (4 shorter events, 0.1 us)
Async XLA Ops:
  0.6 0.9 copy-start
  7.6 2.8 %collective-permute-start = (f32[192,4,128]{2,1,0:T(4,128)S(1)}, f32[192,4,128]{2,1,0:T(4,128)S(1)}, u32[]{:S(2)}, u32[]{:S(2)}) collective-permute-start(f32[192,4,128]{2,1,0:T(4,128)S(1)} %get-tuple-element.19), channel_id=1, source_target_pairs={{0,16},{16,0},{1,17},{17,1},{2,18},{18,2},{3,19},{19,3},{4,20},{20... | collective-permute-start | bytes 1179656 | tf_op jit(solution)/shard_map/ppermute | solution.py:276
  47.2 4.6 %collective-permute-start.1 = (f32[192,4,128]{2,1,0:T(4,128)S(1)}, f32[192,4,128]{2,1,0:T(4,128)S(1)}, u32[]{:S(2)}, u32[]{:S(2)}) collective-permute-start(f32[192,4,128]{2,1,0:T(4,128)S(1)} %bitcast.17), channel_id=1, source_target_pairs={{0,16},{16,0},{1,17},{17,1},{2,18},{18,2},{3,19},{19,3},{4,20},{20... | collective-permute-start | bytes 1179656 | tf_op jit(solution)/shard_map/ppermute | solution.py:276
  54.3 1.4 %collective-permute-start.2 = (f32[32,768]{1,0:T(8,128)S(1)}, f32[32,768]{1,0:T(8,128)S(1)}, u32[]{:S(2)}, u32[]{:S(2)}) collective-permute-start(f32[32,768]{1,0:T(8,128)S(1)} %get-tuple-element.23), channel_id=1, source_target_pairs={{0,16},{16,0},{1,17},{17,1},{2,18},{18,2},{3,19},{19,3},{4,20},{20... | collective-permute-start | bytes 294920 | tf_op jit(solution)/shard_map/ppermute | solution.py:276
  55.7 5.6 %collective-permute-start.5 = (f32[32,768]{1,0:T(8,128)S(1)}, f32[32,768]{1,0:T(8,128)S(1)}, u32[]{:S(2)}, u32[]{:S(2)}) collective-permute-start(f32[32,768]{1,0:T(8,128)S(1)} %add.31), channel_id=1, source_target_pairs={{0,64},{32,96},{64,0},{96,32},{1,65},{33,97},{65,1},{97,33},{2,66}... | collective-permute-start | bytes 294920 | tf_op jit(solution)/shard_map/ppermute | solution.py:280
  56.1 5.4 %collective-permute-start.4 = (f32[32,768]{1,0:T(8,128)S(1)}, f32[32,768]{1,0:T(8,128)S(1)}, u32[]{:S(2)}, u32[]{:S(2)}) collective-permute-start(f32[32,768]{1,0:T(8,128)S(1)} %add.31), channel_id=1, source_target_pairs={{0,96},{32,0},{64,32},{96,64},{1,97},{33,1},{65,33},{97,65},{2,98}... | collective-permute-start | bytes 294920 | tf_op jit(solution)/shard_map/ppermute | solution.py:280
  58.1 5.0 %collective-permute-start.3 = (f32[32,768]{1,0:T(8,128)S(1)}, f32[32,768]{1,0:T(8,128)S(1)}, u32[]{:S(2)}, u32[]{:S(2)}) collective-permute-start(f32[32,768]{1,0:T(8,128)S(1)} %add.31), channel_id=1, source_target_pairs={{0,32},{32,64},{64,96},{96,0},{1,33},{33,65},{65,97},{97,1},{2,34}... | collective-permute-start | bytes 294920 | tf_op jit(solution)/shard_map/ppermute | solution.py:280
  63.2 3.5 %collective-permute-start.6 = (f32[32,768]{1,0:T(8,128)S(1)}, f32[32,768]{1,0:T(8,128)S(1)}, u32[]{:S(2)}, u32[]{:S(2)}) collective-permute-start(f32[32,768]{1,0:T(8,128)S(1)} %add_add_fusion.1.z_mine), channel_id=1, source_target_pairs={{0,16},{16,0},{1,17},{17,1},{2,18},{18,2},{3,19},{19,3},{4,20},{20... | collective-permute-start | bytes 294920 | tf_op jit(solution)/shard_map/ppermute | solution.py:276
  70.1 1.8 %collective-permute-start.7 = (f32[192,4,128]{2,1,0:T(4,128)S(1)}, f32[192,4,128]{2,1,0:T(4,128)S(1)}, u32[]{:S(2)}, u32[]{:S(2)}) collective-permute-start(f32[192,4,128]{2,1,0:T(4,128)S(1)} %get-tuple-element.26), channel_id=1, source_target_pairs={{0,16},{16,0},{1,17},{17,1},{2,18},{18,2},{3,19},{19,3},{4,20},{20... | collective-permute-start | bytes 1179656 | tf_op jit(solution)/shard_map/ppermute | solution.py:276
  102.2 4.2 %collective-permute-start.8 = (f32[192,4,128]{2,1,0:T(4,128)S(1)}, f32[192,4,128]{2,1,0:T(4,128)S(1)}, u32[]{:S(2)}, u32[]{:S(2)}) collective-permute-start(f32[192,4,128]{2,1,0:T(4,128)S(1)} %bitcast.14), channel_id=1, source_target_pairs={{0,16},{16,0},{1,17},{17,1},{2,18},{18,2},{3,19},{19,3},{4,20},{20... | collective-permute-start | bytes 1179656 | tf_op jit(solution)/shard_map/ppermute | solution.py:276
  108.9 1.4 %collective-permute-start.9 = (f32[32,768]{1,0:T(8,128)S(1)}, f32[32,768]{1,0:T(8,128)S(1)}, u32[]{:S(2)}, u32[]{:S(2)}) collective-permute-start(f32[32,768]{1,0:T(8,128)S(1)} %get-tuple-element.28), channel_id=1, source_target_pairs={{0,16},{16,0},{1,17},{17,1},{2,18},{18,2},{3,19},{19,3},{4,20},{20... | collective-permute-start | bytes 294920 | tf_op jit(solution)/shard_map/ppermute | solution.py:276
  110.4 5.6 %collective-permute-start.12 = (f32[32,768]{1,0:T(8,128)S(1)}, f32[32,768]{1,0:T(8,128)S(1)}, u32[]{:S(2)}, u32[]{:S(2)}) collective-permute-start(f32[32,768]{1,0:T(8,128)S(1)} %add.36), channel_id=1, source_target_pairs={{0,64},{32,96},{64,0},{96,32},{1,65},{33,97},{65,1},{97,33},{2,66}... | collective-permute-start | bytes 294920 | tf_op jit(solution)/shard_map/ppermute | solution.py:280
  110.8 5.4 %collective-permute-start.11 = (f32[32,768]{1,0:T(8,128)S(1)}, f32[32,768]{1,0:T(8,128)S(1)}, u32[]{:S(2)}, u32[]{:S(2)}) collective-permute-start(f32[32,768]{1,0:T(8,128)S(1)} %add.36), channel_id=1, source_target_pairs={{0,96},{32,0},{64,32},{96,64},{1,97},{33,1},{65,33},{97,65},{2,98}... | collective-permute-start | bytes 294920 | tf_op jit(solution)/shard_map/ppermute | solution.py:280
  112.9 5.0 %collective-permute-start.10 = (f32[32,768]{1,0:T(8,128)S(1)}, f32[32,768]{1,0:T(8,128)S(1)}, u32[]{:S(2)}, u32[]{:S(2)}) collective-permute-start(f32[32,768]{1,0:T(8,128)S(1)} %add.36), channel_id=1, source_target_pairs={{0,32},{32,64},{64,96},{96,0},{1,33},{33,65},{65,97},{97,1},{2,34}... | collective-permute-start | bytes 294920 | tf_op jit(solution)/shard_map/ppermute | solution.py:280
  117.9 3.5 %collective-permute-start.13 = (f32[32,768]{1,0:T(8,128)S(1)}, f32[32,768]{1,0:T(8,128)S(1)}, u32[]{:S(2)}, u32[]{:S(2)}) collective-permute-start(f32[32,768]{1,0:T(8,128)S(1)} %add_add_fusion.z_mine), channel_id=1, source_target_pairs={{0,16},{16,0},{1,17},{17,1},{2,18},{18,2},{3,19},{19,3},{4,20},{20... | collective-permute-start | bytes 294920 | tf_op jit(solution)/shard_map/ppermute | solution.py:276

commit v3 on v2

--- a/solution.py
+++ b/solution.py
@@ -9,11 +9,9 @@
 HIGH = lax.Precision.HIGHEST
 RANK, HALF = 64, 32
 ROWS, COLS = 3072, 768
-BLOCK = 768
-BLOCKS = ROWS // BLOCK
 WIDE = 256
-SLAB = 384
-SLABS = ROWS // SLAB
+EVEN = (1024,) * 3
+LAST = (256,) * 12
 CHIPS = 64
 TILES = HALF * ROWS // 512
 REPLICAS = 8
@@ -45,24 +43,33 @@
     return jnp.where(first, top, bottom), jnp.where(first, bottom, top)
 
 
-def put(pieces, block, x):
-    for lane in range(BLOCK // 128):
+def put(pieces, start, x):
+    for lane in range(x.shape[1] // 128):
         for group in range(HALF // 4):
-            tile = (block * (BLOCK // 128) + lane) * (HALF // 4) + group
+            tile = (start // 128 + lane) * (HALF // 4) + group
             pieces[tile] = x[4 * group : 4 * group + 4, 128 * lane : 128 * lane + 128]
 
 
-def take(pieces, block):
+def take(pieces, start, size):
     columns = []
-    for lane in range(BLOCK // 128):
-        start = (block * (BLOCK // 128) + lane) * (HALF // 4)
-        columns.append(jnp.concatenate([pieces[start + group] for group in range(HALF // 4)], axis=0))
+    for lane in range(start // 128, (start + size) // 128):
+        tiles = [pieces[lane * (HALF // 4) + group] for group in range(HALF // 4)]
+        columns.append(jnp.concatenate(tiles, axis=0))
     return jnp.concatenate(columns, axis=1)
 
 
-def put_both(core, mine, other, block, x):
+def put_both(core, mine, other, start, x):
     for pieces, half in zip((mine, other), parted(core, x)):
-        put(pieces, block, half)
+        put(pieces, start, half)
+
+
+def take_both(core, mine, other, start, size):
+    return ordered(core, take(mine, start, size), take(other, start, size))
+
+
+def ranges(sizes):
+    starts = [sum(sizes[:i]) for i in range(len(sizes))]
+    return list(zip(starts, sizes))
 
 
 def mean_kernel(terms, out):
@@ -75,43 +82,50 @@
     return jnp.concatenate(split(x, 3), axis=0)
 
 
-def times_rows(stack, g, e, block):
-    rows = pl.ds(block * BLOCK, BLOCK)
+def times_rows(stack, g, e, start, size):
+    rows = pl.ds(start, size)
     across = (((1,), (1,)), ((), ()))
     p = lax.dot_general(stack[...], g[rows, :], across, preferred_element_type=F32)
     return fold(p + lax.dot_general(stack[...], e[rows, :], across, preferred_element_type=F32))
 
 
-def first_left_kernel(core, q, g_far, e_far, mine, other, g, e, stack, g_sem, e_sem):
+def first_left_kernel(core, q_far, g_far, e_far, mine, other, g, e, stack, q, q_sem, g_sem, e_sem):
+    q_copy = pltpu.make_async_copy(q_far, q, q_sem)
+    q_copy.start()
+    pieces = ranges(EVEN)
     copies = []
-    for block in range(BLOCKS):
-        rows = pl.ds(block * BLOCK, BLOCK)
-        pair = (
-            pltpu.make_async_copy(g_far.at[rows, :], g.at[rows, :], g_sem.at[block]),
-            pltpu.make_async_copy(e_far.at[rows, :], e.at[rows, :], e_sem.at[block]),
+    for i, (start, size) in enumerate(pieces):
+        rows = pl.ds(start, size)
+        copies.append(
+            (
+                pltpu.make_async_copy(g_far.at[rows, :], g.at[rows, :], g_sem.at[i]),
+                pltpu.make_async_copy(e_far.at[rows, :], e.at[rows, :], e_sem.at[i]),
+            )
         )
+    for pair in copies[:2]:
         for copy in pair:
             copy.start()
-        copies.append(pair)
+    q_copy.wait()
     stack[...] = stacked(q[...])
-    for block, pair in enumerate(copies):
-        for copy in pair:
+    for i, (start, size) in enumerate(pieces):
+        for copy in copies[i]:
             copy.wait()
-        put_both(core[0], mine, other, block, times_rows(stack, g, e, block))
+        for copy in copies[i + 2] if i + 2 < len(copies) else ():
+            copy.start()
+        put_both(core[0], mine, other, start, times_rows(stack, g, e, start, size))
 
 
 def left_kernel(core, z_mine, z_other, inverse, g, e, mine, other, stack):
     z = ordered(core[0], z_mine[...], z_other[...])
     right = jnp.dot(inverse[...], z, precision=HIGH, preferred_element_type=F32) * (1.0 / REPLICAS)
     stack[...] = stacked(right)
-    for block in range(BLOCKS):
-        put_both(core[0], mine, other, block, times_rows(stack, g, e, block))
+    for start, size in ranges(EVEN):
+        put_both(core[0], mine, other, start, times_rows(stack, g, e, start, size))
 
 
 def right_kernel(core, l_mine, l_other, g, e, z_mine, z_other, gram, stack):
-    for block in range(BLOCKS):
-        left = ordered(core[0], take(l_mine, block), take(l_other, block))
-        stack[:, pl.ds(block * BLOCK, BLOCK)] = stacked(left)
+    for start, size in ranges(EVEN):
+        stack[:, pl.ds(start, size)] = stacked(take_both(core[0], l_mine, l_other, start, size))
     for part in range(COLS // WIDE):
         cols = pl.ds(part * WIDE, WIDE)
         z = jnp.dot(stack[...], g[:, cols], preferred_element_type=F32)
@@ -142,38 +156,32 @@
         work = work[8:]
 
 
-def renew_kernel(
-    core, z_mine, z_other, inverse, l_mine, l_other, g, e, w_far, new_e, new_w, right_out, stack, e_near, w_near, in_sem, e_sem, w_sem
-):
-    def rows(step):
-        return pl.ds(step * SLAB, SLAB)
-
-    loads = []
-    for step in range(SLABS):
-        loads.append(pltpu.make_async_copy(w_far.at[rows(step), :], w_near.at[rows(step), :], in_sem.at[step]))
-        loads[-1].start()
+def ready_kernel(core, l_mine, l_other, w_far, factors, w, w_sem):
+    load = pltpu.make_async_copy(w_far, w, w_sem)
+    load.start()
+    for start, size in ranges(EVEN):
+        high, low = split(take_both(core[0], l_mine, l_other, start, size), 2)
+        factors[pl.ds(start, size), :] = jnp.concatenate([high, high, low], axis=0).T
+    load.wait()
+
+
+def renew_kernel(core, z_mine, z_other, inverse, factors, g, e, w, new_e, new_w, right_out, e_near, w_near, e_sem, w_sem):
     z = ordered(core[0], z_mine[...], z_other[...])
     right = jnp.dot(inverse[...], z, precision=HIGH, preferred_element_type=F32) * (1.0 / REPLICAS)
     right_out[...] = right
     mixed = lax.dot_general(inverse[...], right, (((0,), (0,)), ((), ())), precision=HIGH, preferred_element_type=F32)
     high, low = split(mixed, 2)
-    stack[...] = jnp.concatenate([high, low, high], axis=0)
+    stack = jnp.concatenate([high, low, high], axis=0)
     stores = []
-    for step in range(SLABS):
-        block, within = divmod(step * SLAB, BLOCK)
-        if within == 0:
-            whole = ordered(core[0], take(l_mine, block), take(l_other, block))
-        left = whole[:, within : within + SLAB]
-        high, low = split(left, 2)
-        factors = jnp.concatenate([high, high, low], axis=0)
-        approx = lax.dot_general(factors, stack[...], (((0,), (0,)), ((), ())), preferred_element_type=F32)
-        merged = g[rows(step), :].astype(F32) + e[rows(step), :].astype(F32)
-        e_near[rows(step), :] = (merged - approx).astype(BF16)
-        stores.append(pltpu.make_async_copy(e_near.at[rows(step), :], new_e.at[rows(step), :], e_sem.at[step]))
+    for i, (start, size) in enumerate(ranges(LAST)):
+        rows = pl.ds(start, size)
+        approx = jnp.dot(factors[rows, :], stack, preferred_element_type=F32)
+        merged = g[rows, :].astype(F32) + e[rows, :].astype(F32)
+        e_near[rows, :] = (merged - approx).astype(BF16)
+        stores.append(pltpu.make_async_copy(e_near.at[rows, :], new_e.at[rows, :], e_sem.at[i]))
         stores[-1].start()
-        loads[step].wait()
-        w_near[rows(step), :] = (w_near[rows(step), :].astype(F32) - 0.5 * approx).astype(BF16)
-        stores.append(pltpu.make_async_copy(w_near.at[rows(step), :], new_w.at[rows(step), :], w_sem.at[step]))
+        w_near[rows, :] = (w[rows, :].astype(F32) - 0.5 * approx).astype(BF16)
+        stores.append(pltpu.make_async_copy(w_near.at[rows, :], new_w.at[rows, :], w_sem.at[i]))
         stores[-1].start()
     for store in stores:
         store.wait()
@@ -184,6 +192,7 @@
 FAR = pl.BlockSpec(memory_space=pltpu.HBM)
 PIECES = jax.ShapeDtypeStruct((TILES, 4, 128), F32)
 ZHALF = jax.ShapeDtypeStruct((HALF, COLS), F32)
+NEAR_ARRAY = pltpu.VMEM((ROWS, COLS), BF16)
 SQUARE = jax.ShapeDtypeStruct((RANK, RANK), F32)
 STACK = pltpu.VMEM((3 * RANK, COLS), BF16)
 
@@ -204,17 +213,27 @@
     return [pltpu.with_memory_space_constraint(x, pltpu.HBM) for x in arrays]
 
 
+def semaphores(count):
+    return pltpu.SemaphoreType.DMA((count,))
+
+
 def first_left_pass(core, q, g, e):
     return pl.pallas_call(
         first_left_kernel,
-        in_specs=[SCALAR, NEAR, FAR, FAR],
+        in_specs=[SCALAR, FAR, FAR, FAR],
         out_specs=[NEAR] * 4,
-        out_shape=[PIECES, PIECES, pltpu.VMEM((ROWS, COLS), BF16), pltpu.VMEM((ROWS, COLS), BF16)],
-        scratch_shapes=[STACK, pltpu.SemaphoreType.DMA((BLOCKS,)), pltpu.SemaphoreType.DMA((BLOCKS,))],
+        out_shape=[PIECES, PIECES, NEAR_ARRAY, NEAR_ARRAY],
+        scratch_shapes=[
+            STACK,
+            pltpu.VMEM((RANK, COLS), F32),
+            pltpu.SemaphoreType.DMA,
+            semaphores(len(EVEN)),
+            semaphores(len(EVEN)),
+        ],
         compiler_params=params(LIMIT),
         cost_estimate=cost(6, 4 * ROWS * COLS),
         name="first_left_pass",
-    )(core, q, *far(g, e))
+    )(core, *far(q, g, e))
 
 
 def left_pass(core, z_mine, z_other, inverse, g, e):
@@ -253,23 +272,36 @@
     )(gram)
 
 
-def renew(core, z_mine, z_other, inverse, l_mine, l_other, g, e, w):
+def ready(core, l_mine, l_other, w):
+    return pl.pallas_call(
+        ready_kernel,
+        in_specs=[SCALAR, NEAR, NEAR, FAR],
+        out_specs=[NEAR] * 2,
+        out_shape=[pltpu.VMEM((ROWS, 3 * RANK), BF16), NEAR_ARRAY],
+        scratch_shapes=[pltpu.SemaphoreType.DMA],
+        compiler_params=params(SMALL),
+        cost_estimate=cost(1, 4 * ROWS * COLS),
+        name="ready",
+    )(core, l_mine, l_other, *far(w))
+
+
+def renew(core, z_mine, z_other, inverse, factors, g, e, w):
     array = jax.ShapeDtypeStruct((ROWS, COLS), BF16)
     return pl.pallas_call(
         renew_kernel,
-        in_specs=[SCALAR] + [NEAR] * 7 + [FAR],
+        in_specs=[SCALAR] + [NEAR] * 7,
         out_specs=[FAR, FAR, NEAR],
         out_shape=[array, array, jax.ShapeDtypeStruct((RANK, COLS), F32)],
         scratch_shapes=[
-            STACK,
             pltpu.VMEM((ROWS, COLS), BF16),
             pltpu.VMEM((ROWS, COLS), BF16),
-            *[pltpu.SemaphoreType.DMA((SLABS,)) for _ in range(3)],
+            semaphores(len(LAST)),
+            semaphores(len(LAST)),
         ],
         compiler_params=params(LIMIT),
         cost_estimate=cost(3, 10 * ROWS * COLS),
         name="renew",
-    )(core, z_mine, z_other, inverse, l_mine, l_other, *near(g, e), *far(w))
+    )(core, z_mine, z_other, inverse, *near(factors, g, e, w))
 
 
 def swap(x):
@@ -300,24 +332,30 @@
     return term, swap(term)
 
 
-def sum_right(mine, other):
+def sum_right(mine, other, beside=None):
     half = mine + swap(other)
+    if beside is not None:
+        step, args = beside
+        half, args = lax.optimization_barrier((half, args))
+        done = step(*args)
     parts = [along_y(half, shift) for shift in (1, 3, 2)]
+    if beside is not None:
+        parts, done = lax.optimization_barrier((parts, done))
     half = half + parts[0] + parts[1] + parts[2]
-    return half, swap(half)
+    both = (half, swap(half))
+    return both if beside is None else (both, done)
 
 
 def shards(gradients, errors, weight, start_q):
-    g, e = gradients[0], errors[0]
     core = lax.axis_index("core").astype(jnp.int32).reshape(1)
-    mine, other, g, e = first_left_pass(core, start_q.T, g, e)
+    mine, other, g, e = first_left_pass(core, start_q.T, gradients[0], errors[0])
     left = sum_left(mine, other)
     z_mine, z_other, gram = right_pass(core, *left, g, e)
-    right = (*sum_right(z_mine, z_other), factor(gram))
-    left = sum_left(*left_pass(core, *right, g, e))
+    right = sum_right(z_mine, z_other)
+    left = sum_left(*left_pass(core, *right, factor(gram), g, e))
     z_mine, z_other, gram = right_pass(core, *left, g, e)
-    right = (*sum_right(z_mine, z_other), factor(gram))
-    new_e, new_w, right_factor = renew(core, *right, *left, g, e, weight)
+    right, (factors, w) = sum_right(z_mine, z_other, (ready, (core, *left, weight)))
+    new_e, new_w, right_factor = renew(core, *right, factor(gram), factors, g, e, w)
     return new_e[None], new_w, right_factor.T
 
 

time: 129 us -> 125 us (0.969)
  waiting for transfers between devices: 17.7 us -> 15.3 us
    ppermute x6, waiting for transfers between devices: 10 us -> 7.65 us  [along_y(): return lax.ppermute(x, 'y', [(i, (i + shift) % 4) for i in range(4)])]
    pallas_call x2 -> x3, Pallas kernels: 13.4 us -> 13.2 us  [the longest x1 5.48 us: first_left_pass(): pl.pallas_call(first_left_kernel, in_specs=[SCALAR, FAR, FAR, FAR], out_s...]
  transfers between devices with their start and end apart: 14 -> 14, of which waited for: 12 -> 12; matrix products, arithmetic and copies ran while one was open for 0% -> 0% of each run, Pallas kernels for 3% -> 5%
where the time goes in v3:
time: 125 us
  blocking collectives  66.5 us (53%)
  Pallas kernels  24.7 us (20%)
  starting transfers between devices  17.2 us (14%)
  waiting for transfers between devices  15.3 us (12%)
    all_to_all x4, blocking collectives, exchange(): return lax.all_to_all(x, CHIP_AXES, 0, 0, tiled=True).reshape(TILES, 4, 128)  66.5 us
    ppermute x8, starting transfers between devices, swap(): return lax.ppermute(x, 'core', [(0, 1), (1, 0)])  12.3 us
    ppermute x6, waiting for transfers between devices, along_y(): return lax.ppermute(x, 'y', [(i, (i + shift) % 4) for i in range(4)])  7.65 us
    ppermute x8, waiting for transfers between devices, swap(): return lax.ppermute(x, 'core', [(0, 1), (1, 0)])  7.65 us
    pallas_call x1, Pallas kernels, first_left_pass(): pl.pallas_call(first_left_kernel, in_specs=[SCALAR, FAR, FAR, FAR], out_s...  5.48 us
    pallas_call x1, Pallas kernels, renew(): pl.pallas_call(renew_kernel, in_specs=[SCALAR] + [NEAR] * 7, out_specs=[F...  5.39 us
    ppermute x6, starting transfers between devices, along_y(): return lax.ppermute(x, 'y', [(i, (i + shift) % 4) for i in range(4)])  4.98 us
    pallas_call x2, Pallas kernels, right_pass(): pl.pallas_call(right_kernel, in_specs=[SCALAR] + [NEAR] * 4, out_specs=[N...  4.93 us
  transfers between devices with their start and end apart: 14, of which 12 were waited for; matrix products, arithmetic and copies ran while one was open for 0% of the time, Pallas kernels for 5%

profile of v3, /device:TPU:1, one launch (start us, length us, event | category | flops | bytes accessed | tf_op | source)
XLA Modules:
  0.0 124.8 jit_solution(5766100235169429174)
XLA Ops:
  0.6 5.5 %first_left_pass.1 = (f32[192,4,128]{2,1,0:T(4,128)S(1)}, f32[192,4,128]{2,1,0:T(4,128)S(1)}, bf16[3072,768]{1,0:T(8,128)(2,1)S(1)}, bf16[3072,768]{1,0:T(8,128)(2,1)S(1)}) custom-call(s32[1]{0:T(128)} %bitcast.core, f32[64,768]{1,0:T(8,128)} %bitcast.27, bf16[3072,768]{1,0:T(8,128)(2,1)} %bitcast.23, bf16[3072,768]{1,0:T(8,128)(2,1)} %bitcast.24), custom_call_target="tpu_custom_call" | custom-call | flops 1811939328 | bytes 9437184 | tf_op jit(solution)/shard_map/first_left_pass/pallas_call | solution.py:221
  6.1 1.5 %collective-permute-start = (f32[192,4,128]{2,1,0:T(4,128)S(1)}, f32[192,4,128]{2,1,0:T(4,128)S(1)}, u32[]{:S(2)}, u32[]{:S(2)}) collective-permute-start(f32[192,4,128]{2,1,0:T(4,128)S(1)} %get-tuple-element.31), channel_id=1, source_target_pairs={{0,16},{16,0},{1,17},{17,1},{2,18},{18,2},{3,19},{19,3},{4,20},{20... | collective-permute-start | bytes 1179656 | tf_op jit(solution)/shard_map/ppermute | solution.py:308
  7.6 1.3 %collective-permute-done = f32[192,4,128]{2,1,0:T(4,128)S(1)} collective-permute-done((f32[192,4,128]{2,1,0:T(4,128)S(1)}, f32[192,4,128]{2,1,0:T(4,128)S(1)}, u32[]{:S(2)}, u32[]{:S(2)}) %collective-permute-start) | collective-permute-done | bytes 393248 | tf_op jit(solution)/shard_map/ppermute | solution.py:308
  9.0 0.1 add.30
  9.1 22.0 %all_to_all.20 = f32[64,3,4,128]{3,2,1,0:T(4,128)S(1)} all-to-all(f32[64,3,4,128]{3,2,1,0:T(4,128)S(1)} %bitcast.25), channel_id=1, replica_groups=mesh['y'=4,'core'=2,'x'=4,'z'=4] {'y','x','z'}, dimensions={0} | all-to-all | bytes 786432 | tf_op jit(solution)/shard_map/all_to_all | solution.py:327
  31.0 0.1 mean.2
  31.2 14.6 %all_to_all.21 = f32[64,3,4,128]{3,2,1,0:T(4,128)S(1)} all-to-all(f32[64,3,4,128]{3,2,1,0:T(4,128)S(1)} %bitcast.20), channel_id=1, replica_groups=mesh['y'=4,'core'=2,'x'=4,'z'=4] {'y','x','z'}, dimensions={0} | all-to-all | bytes 786432 | tf_op jit(solution)/shard_map/all_to_all | solution.py:327
  45.8 3.2 %collective-permute-start.1 = (f32[192,4,128]{2,1,0:T(4,128)S(1)}, f32[192,4,128]{2,1,0:T(4,128)S(1)}, u32[]{:S(2)}, u32[]{:S(2)}) collective-permute-start(f32[192,4,128]{2,1,0:T(4,128)S(1)} %bitcast.17), channel_id=1, source_target_pairs={{0,16},{16,0},{1,17},{17,1},{2,18},{18,2},{3,19},{19,3},{4,20},{20... | collective-permute-start | bytes 1179656 | tf_op jit(solution)/shard_map/ppermute | solution.py:308
  49.0 1.3 %collective-permute-done.1.l_other = f32[192,4,128]{2,1,0:T(4,128)S(1)} collective-permute-done((f32[192,4,128]{2,1,0:T(4,128)S(1)}, f32[192,4,128]{2,1,0:T(4,128)S(1)}, u32[]{:S(2)}, u32[]{:S(2)}) %collective-permute-start.1) | collective-permute-done | bytes 393248 | tf_op jit(solution)/shard_map/ppermute | solution.py:308
  50.3 2.5 %right_pass.2 = (f32[32,768]{1,0:T(8,128)S(1)}, f32[32,768]{1,0:T(8,128)S(1)}, f32[64,64]{1,0:T(8,128)S(1)}) custom-call(s32[1]{0:T(128)} %bitcast.core, f32[192,4,128]{2,1,0:T(4,128)S(1)} %bitcast.18, f32[192,4,128]{2,1,0:T(4,128)S(1)} %collective-permute-done.1.l_other, bf16[3072,768]{1,0:T(8,128)(2,1)S(1)} %get-tuple-element.32.g, ...), custom_call_target="tpu_custom_call" | custom-call | flops 1811939328 | bytes 9437184 | tf_op jit(solution)/shard_map/right_pass/pallas_call | solution.py:253
  52.8 0.5 collective-permute-start.2
  53.3 0.9 collective-permute-done.2
  54.2 0.4 collective-permute-start.5
  54.7 2.0 %collective-permute-start.4 = (f32[32,768]{1,0:T(8,128)S(1)}, f32[32,768]{1,0:T(8,128)S(1)}, u32[]{:S(2)}, u32[]{:S(2)}) collective-permute-start(f32[32,768]{1,0:T(8,128)S(1)} %add.31), channel_id=1, source_target_pairs={{0,96},{32,0},{64,32},{96,64},{1,97},{33,1},{65,33},{97,65},{2,98}... | collective-permute-start | bytes 294920 | tf_op jit(solution)/shard_map/ppermute | solution.py:312
  56.7 0.0 collective-permute-start.3
  56.7 3.1 %collective-permute-done.5 = f32[32,768]{1,0:T(8,128)S(1)} collective-permute-done((f32[32,768]{1,0:T(8,128)S(1)}, f32[32,768]{1,0:T(8,128)S(1)}, u32[]{:S(2)}, u32[]{:S(2)}) %collective-permute-start.5) | collective-permute-done | bytes 98336 | tf_op jit(solution)/shard_map/ppermute | solution.py:312
  59.8 0.2 collective-permute-done.4
  60.0 1.7 %collective-permute-done.3 = f32[32,768]{1,0:T(8,128)S(1)} collective-permute-done((f32[32,768]{1,0:T(8,128)S(1)}, f32[32,768]{1,0:T(8,128)S(1)}, u32[]{:S(2)}, u32[]{:S(2)}) %collective-permute-start.3) | collective-permute-done | bytes 98336 | tf_op jit(solution)/shard_map/ppermute | solution.py:312
  61.7 1.8 %collective-permute-start.6 = (f32[32,768]{1,0:T(8,128)S(1)}, f32[32,768]{1,0:T(8,128)S(1)}, u32[]{:S(2)}, u32[]{:S(2)}) collective-permute-start(f32[32,768]{1,0:T(8,128)S(1)} %add_add_fusion.1.z_mine), channel_id=1, source_target_pairs={{0,16},{16,0},{1,17},{17,1},{2,18},{18,2},{3,19},{19,3},{4,20},{20... | collective-permute-start | bytes 294920 | tf_op jit(solution)/shard_map/ppermute | solution.py:308
  63.6 1.6 %factor.2.inverse = f32[64,64]{1,0:T(8,128)S(1)} custom-call(f32[64,64]{1,0:T(8,128)S(1)} %get-tuple-element.36.gram), custom_call_target="tpu_custom_call" | custom-call | flops 4000000000 | bytes 32768 | tf_op jit(solution)/shard_map/factor/pallas_call | solution.py:266
  65.2 0.0 collective-permute-done.6.z_other
  65.2 3.0 %left_pass.1 = (f32[192,4,128]{2,1,0:T(4,128)S(1)}, f32[192,4,128]{2,1,0:T(4,128)S(1)}) custom-call(s32[1]{0:T(128)} %bitcast.core, f32[32,768]{1,0:T(8,128)S(1)} %add_add_fusion.1.z_mine, f32[32,768]{1,0:T(8,128)S(1)} %collective-permute-done.6.z_other, f32[64,64]{1,0:T(8,128)S(1)} %factor.2.inverse, bf16[3072,768]{1,0:T(8,128)(2,1)S(1)} %get-tuple-element.32.g, ...), custom_call_target="tpu_custom_call" | custom-call | flops 1811939328 | bytes 9437184 | tf_op jit(solution)/shard_map/left_pass/pallas_call | solution.py:240
  68.2 0.1 collective-permute-start.7
  68.3 1.7 %collective-permute-done.7 = f32[192,4,128]{2,1,0:T(4,128)S(1)} collective-permute-done((f32[192,4,128]{2,1,0:T(4,128)S(1)}, f32[192,4,128]{2,1,0:T(4,128)S(1)}, u32[]{:S(2)}, u32[]{:S(2)}) %collective-permute-start.7) | collective-permute-done | bytes 393248 | tf_op jit(solution)/shard_map/ppermute | solution.py:308
  70.0 0.1 add.35
  70.1 15.3 %all_to_all.22 = f32[64,3,4,128]{3,2,1,0:T(4,128)S(1)} all-to-all(f32[64,3,4,128]{3,2,1,0:T(4,128)S(1)} %bitcast.26), channel_id=1, replica_groups=mesh['y'=4,'core'=2,'x'=4,'z'=4] {'y','x','z'}, dimensions={0} | all-to-all | bytes 786432 | tf_op jit(solution)/shard_map/all_to_all | solution.py:327
  85.3 0.1 mean.3
  85.5 14.7 %all_to_all.23 = f32[64,3,4,128]{3,2,1,0:T(4,128)S(1)} all-to-all(f32[64,3,4,128]{3,2,1,0:T(4,128)S(1)} %bitcast.22), channel_id=1, replica_groups=mesh['y'=4,'core'=2,'x'=4,'z'=4] {'y','x','z'}, dimensions={0} | all-to-all | bytes 786432 | tf_op jit(solution)/shard_map/all_to_all | solution.py:327
  100.1 2.9 %collective-permute-start.8 = (f32[192,4,128]{2,1,0:T(4,128)S(1)}, f32[192,4,128]{2,1,0:T(4,128)S(1)}, u32[]{:S(2)}, u32[]{:S(2)}) collective-permute-start(f32[192,4,128]{2,1,0:T(4,128)S(1)} %bitcast.14), channel_id=1, source_target_pairs={{0,16},{16,0},{1,17},{17,1},{2,18},{18,2},{3,19},{19,3},{4,20},{20... | collective-permute-start | bytes 1179656 | tf_op jit(solution)/shard_map/ppermute | solution.py:308
  103.0 1.3 %collective-permute-done.8.l_other = f32[192,4,128]{2,1,0:T(4,128)S(1)} collective-permute-done((f32[192,4,128]{2,1,0:T(4,128)S(1)}, f32[192,4,128]{2,1,0:T(4,128)S(1)}, u32[]{:S(2)}, u32[]{:S(2)}) %collective-permute-start.8) | collective-permute-done | bytes 393248 | tf_op jit(solution)/shard_map/ppermute | solution.py:308
  104.4 2.5 %right_pass.3 = (f32[32,768]{1,0:T(8,128)S(1)}, f32[32,768]{1,0:T(8,128)S(1)}, f32[64,64]{1,0:T(8,128)S(1)}) custom-call(s32[1]{0:T(128)} %bitcast.core, f32[192,4,128]{2,1,0:T(4,128)S(1)} %bitcast.15, f32[192,4,128]{2,1,0:T(4,128)S(1)} %collective-permute-done.8.l_other, bf16[3072,768]{1,0:T(8,128)(2,1)S(1)} %get-tuple-element.32.g, ...), custom_call_target="tpu_custom_call" | custom-call | flops 1811939328 | bytes 9437184 | tf_op jit(solution)/shard_map/right_pass/pallas_call | solution.py:253
  106.9 0.5 collective-permute-start.9
  107.3 0.9 collective-permute-done.9
  108.3 0.4 collective-permute-start.12
  108.7 2.1 %collective-permute-start.11 = (f32[32,768]{1,0:T(8,128)S(1)}, f32[32,768]{1,0:T(8,128)S(1)}, u32[]{:S(2)}, u32[]{:S(2)}) collective-permute-start(f32[32,768]{1,0:T(8,128)S(1)} %add.36), channel_id=1, source_target_pairs={{0,96},{32,0},{64,32},{96,64},{1,97},{33,1},{65,33},{97,65},{2,98}... | collective-permute-start | bytes 294920 | tf_op jit(solution)/shard_map/ppermute | solution.py:312
  110.8 0.0 collective-permute-start.10
  110.8 2.4 %ready.1 = (bf16[3072,192]{1,0:T(8,128)(2,1)S(1)}, bf16[3072,768]{1,0:T(8,128)(2,1)S(1)}) custom-call(s32[1]{0:T(128)} %bitcast.core, f32[192,4,128]{2,1,0:T(4,128)S(1)} %bitcast.16, f32[192,4,128]{2,1,0:T(4,128)S(1)} %collective-permute-done.8.l_other, bf16[3072,768]{1,0:T(8,128)(2,1)} %w_far), custom_call_target="tpu_custom_call" | custom-call | flops 301989888 | bytes 9437184 | tf_op jit(solution)/shard_map/ready/pallas_call | solution.py:276
  113.2 0.7 collective-permute-done.12
  113.9 0.3 collective-permute-done.11
  114.2 1.7 %collective-permute-done.10 = f32[32,768]{1,0:T(8,128)S(1)} collective-permute-done((f32[32,768]{1,0:T(8,128)S(1)}, f32[32,768]{1,0:T(8,128)S(1)}, u32[]{:S(2)}, u32[]{:S(2)}) %collective-permute-start.10) | collective-permute-done | bytes 98336 | tf_op jit(solution)/shard_map/ppermute | solution.py:312
  115.8 1.8 %collective-permute-start.13 = (f32[32,768]{1,0:T(8,128)S(1)}, f32[32,768]{1,0:T(8,128)S(1)}, u32[]{:S(2)}, u32[]{:S(2)}) collective-permute-start(f32[32,768]{1,0:T(8,128)S(1)} %add_add_fusion.z_mine), channel_id=1, source_target_pairs={{0,16},{16,0},{1,17},{17,1},{2,18},{18,2},{3,19},{19,3},{4,20},{20... | collective-permute-start | bytes 294920 | tf_op jit(solution)/shard_map/ppermute | solution.py:308
  117.7 1.6 %factor.3.inverse = f32[64,64]{1,0:T(8,128)S(1)} custom-call(f32[64,64]{1,0:T(8,128)S(1)} %get-tuple-element.51.gram), custom_call_target="tpu_custom_call" | custom-call | flops 4000000000 | bytes 32768 | tf_op jit(solution)/shard_map/factor/pallas_call | solution.py:266
  119.3 0.0 collective-permute-done.13.z_other
  119.3 5.4 %renew.1 = (bf16[3072,768]{1,0:T(8,128)(2,1)}, bf16[3072,768]{1,0:T(8,128)(2,1)}, f32[64,768]{1,0:T(8,128)}) custom-call(s32[1]{0:T(128)} %bitcast.core, f32[32,768]{1,0:T(8,128)S(1)} %add_add_fusion.z_mine, f32[32,768]{1,0:T(8,128)S(1)} %collective-permute-done.13.z_other, f32[64,64]{1,0:T(8,128)S(1)} %factor.3.inverse, ...), custom_call_target="tpu_custom_call" | custom-call | flops 905969664 | bytes 23592960 | tf_op jit(solution)/shard_map/renew/pallas_call | solution.py:290
  (4 shorter events, 0.1 us)
Async XLA Ops:
  6.1 2.8 %collective-permute-start = (f32[192,4,128]{2,1,0:T(4,128)S(1)}, f32[192,4,128]{2,1,0:T(4,128)S(1)}, u32[]{:S(2)}, u32[]{:S(2)}) collective-permute-start(f32[192,4,128]{2,1,0:T(4,128)S(1)} %get-tuple-element.31), channel_id=1, source_target_pairs={{0,16},{16,0},{1,17},{17,1},{2,18},{18,2},{3,19},{19,3},{4,20},{20... | collective-permute-start | bytes 1179656 | tf_op jit(solution)/shard_map/ppermute | solution.py:308
  45.8 4.6 %collective-permute-start.1 = (f32[192,4,128]{2,1,0:T(4,128)S(1)}, f32[192,4,128]{2,1,0:T(4,128)S(1)}, u32[]{:S(2)}, u32[]{:S(2)}) collective-permute-start(f32[192,4,128]{2,1,0:T(4,128)S(1)} %bitcast.17), channel_id=1, source_target_pairs={{0,16},{16,0},{1,17},{17,1},{2,18},{18,2},{3,19},{19,3},{4,20},{20... | collective-permute-start | bytes 1179656 | tf_op jit(solution)/shard_map/ppermute | solution.py:308
  52.8 1.4 %collective-permute-start.2 = (f32[32,768]{1,0:T(8,128)S(1)}, f32[32,768]{1,0:T(8,128)S(1)}, u32[]{:S(2)}, u32[]{:S(2)}) collective-permute-start(f32[32,768]{1,0:T(8,128)S(1)} %get-tuple-element.35), channel_id=1, source_target_pairs={{0,16},{16,0},{1,17},{17,1},{2,18},{18,2},{3,19},{19,3},{4,20},{20... | collective-permute-start | bytes 294920 | tf_op jit(solution)/shard_map/ppermute | solution.py:308
  54.2 5.6 %collective-permute-start.5 = (f32[32,768]{1,0:T(8,128)S(1)}, f32[32,768]{1,0:T(8,128)S(1)}, u32[]{:S(2)}, u32[]{:S(2)}) collective-permute-start(f32[32,768]{1,0:T(8,128)S(1)} %add.31), channel_id=1, source_target_pairs={{0,64},{32,96},{64,0},{96,32},{1,65},{33,97},{65,1},{97,33},{2,66}... | collective-permute-start | bytes 294920 | tf_op jit(solution)/shard_map/ppermute | solution.py:312
  54.7 5.4 %collective-permute-start.4 = (f32[32,768]{1,0:T(8,128)S(1)}, f32[32,768]{1,0:T(8,128)S(1)}, u32[]{:S(2)}, u32[]{:S(2)}) collective-permute-start(f32[32,768]{1,0:T(8,128)S(1)} %add.31), channel_id=1, source_target_pairs={{0,96},{32,0},{64,32},{96,64},{1,97},{33,1},{65,33},{97,65},{2,98}... | collective-permute-start | bytes 294920 | tf_op jit(solution)/shard_map/ppermute | solution.py:312
  56.7 5.0 %collective-permute-start.3 = (f32[32,768]{1,0:T(8,128)S(1)}, f32[32,768]{1,0:T(8,128)S(1)}, u32[]{:S(2)}, u32[]{:S(2)}) collective-permute-start(f32[32,768]{1,0:T(8,128)S(1)} %add.31), channel_id=1, source_target_pairs={{0,32},{32,64},{64,96},{96,0},{1,33},{33,65},{65,97},{97,1},{2,34}... | collective-permute-start | bytes 294920 | tf_op jit(solution)/shard_map/ppermute | solution.py:312
  61.7 3.5 %collective-permute-start.6 = (f32[32,768]{1,0:T(8,128)S(1)}, f32[32,768]{1,0:T(8,128)S(1)}, u32[]{:S(2)}, u32[]{:S(2)}) collective-permute-start(f32[32,768]{1,0:T(8,128)S(1)} %add_add_fusion.1.z_mine), channel_id=1, source_target_pairs={{0,16},{16,0},{1,17},{17,1},{2,18},{18,2},{3,19},{19,3},{4,20},{20... | collective-permute-start | bytes 294920 | tf_op jit(solution)/shard_map/ppermute | solution.py:308
  68.2 1.8 %collective-permute-start.7 = (f32[192,4,128]{2,1,0:T(4,128)S(1)}, f32[192,4,128]{2,1,0:T(4,128)S(1)}, u32[]{:S(2)}, u32[]{:S(2)}) collective-permute-start(f32[192,4,128]{2,1,0:T(4,128)S(1)} %get-tuple-element.38), channel_id=1, source_target_pairs={{0,16},{16,0},{1,17},{17,1},{2,18},{18,2},{3,19},{19,3},{4,20},{20... | collective-permute-start | bytes 1179656 | tf_op jit(solution)/shard_map/ppermute | solution.py:308
  100.1 4.2 %collective-permute-start.8 = (f32[192,4,128]{2,1,0:T(4,128)S(1)}, f32[192,4,128]{2,1,0:T(4,128)S(1)}, u32[]{:S(2)}, u32[]{:S(2)}) collective-permute-start(f32[192,4,128]{2,1,0:T(4,128)S(1)} %bitcast.14), channel_id=1, source_target_pairs={{0,16},{16,0},{1,17},{17,1},{2,18},{18,2},{3,19},{19,3},{4,20},{20... | collective-permute-start | bytes 1179656 | tf_op jit(solution)/shard_map/ppermute | solution.py:308
  106.9 1.4 %collective-permute-start.9 = (f32[32,768]{1,0:T(8,128)S(1)}, f32[32,768]{1,0:T(8,128)S(1)}, u32[]{:S(2)}, u32[]{:S(2)}) collective-permute-start(f32[32,768]{1,0:T(8,128)S(1)} %get-tuple-element.40), channel_id=1, source_target_pairs={{0,16},{16,0},{1,17},{17,1},{2,18},{18,2},{3,19},{19,3},{4,20},{20... | collective-permute-start | bytes 294920 | tf_op jit(solution)/shard_map/ppermute | solution.py:308
  108.3 5.6 %collective-permute-start.12 = (f32[32,768]{1,0:T(8,128)S(1)}, f32[32,768]{1,0:T(8,128)S(1)}, u32[]{:S(2)}, u32[]{:S(2)}) collective-permute-start(f32[32,768]{1,0:T(8,128)S(1)} %add.36), channel_id=1, source_target_pairs={{0,64},{32,96},{64,0},{96,32},{1,65},{33,97},{65,1},{97,33},{2,66}... | collective-permute-start | bytes 294920 | tf_op jit(solution)/shard_map/ppermute | solution.py:312
  108.7 5.4 %collective-permute-start.11 = (f32[32,768]{1,0:T(8,128)S(1)}, f32[32,768]{1,0:T(8,128)S(1)}, u32[]{:S(2)}, u32[]{:S(2)}) collective-permute-start(f32[32,768]{1,0:T(8,128)S(1)} %add.36), channel_id=1, source_target_pairs={{0,96},{32,0},{64,32},{96,64},{1,97},{33,1},{65,33},{97,65},{2,98}... | collective-permute-start | bytes 294920 | tf_op jit(solution)/shard_map/ppermute | solution.py:312
  110.8 5.0 %collective-permute-start.10 = (f32[32,768]{1,0:T(8,128)S(1)}, f32[32,768]{1,0:T(8,128)S(1)}, u32[]{:S(2)}, u32[]{:S(2)}) collective-permute-start(f32[32,768]{1,0:T(8,128)S(1)} %add.36), channel_id=1, source_target_pairs={{0,32},{32,64},{64,96},{96,0},{1,33},{33,65},{65,97},{97,1},{2,34}... | collective-permute-start | bytes 294920 | tf_op jit(solution)/shard_map/ppermute | solution.py:312
  115.8 3.5 %collective-permute-start.13 = (f32[32,768]{1,0:T(8,128)S(1)}, f32[32,768]{1,0:T(8,128)S(1)}, u32[]{:S(2)}, u32[]{:S(2)}) collective-permute-start(f32[32,768]{1,0:T(8,128)S(1)} %add_add_fusion.z_mine), channel_id=1, source_target_pairs={{0,16},{16,0},{1,17},{17,1},{2,18},{18,2},{3,19},{19,3},{4,20},{20... | collective-permute-start | bytes 294920 | tf_op jit(solution)/shard_map/ppermute | solution.py:308

commit v4 on v3

--- a/solution.py
+++ b/solution.py
@@ -10,13 +10,15 @@
 RANK, HALF = 64, 32
 ROWS, COLS = 3072, 768
 WIDE = 256
+OWN = ROWS // 2
 EVEN = (1024,) * 3
+PART = (768,) * 2
 LAST = (256,) * 12
 CHIPS = 64
 TILES = HALF * ROWS // 512
 REPLICAS = 8
 CHIP_AXES = ("y", "x", "z")
-LIMIT, SMALL = 32 * 2**20, 8 * 2**20
+LIMIT, SMALL = 16 * 2**20, 6 * 2**20
 
 
 def split(x, parts):
@@ -44,27 +46,35 @@
 
 
 def put(pieces, start, x):
+    groups = x.shape[0] // 4
     for lane in range(x.shape[1] // 128):
-        for group in range(HALF // 4):
-            tile = (start // 128 + lane) * (HALF // 4) + group
+        for group in range(groups):
+            tile = (start // 128 + lane) * groups + group
             pieces[tile] = x[4 * group : 4 * group + 4, 128 * lane : 128 * lane + 128]
 
 
 def take(pieces, start, size):
+    groups = RANK // 4
     columns = []
     for lane in range(start // 128, (start + size) // 128):
-        tiles = [pieces[lane * (HALF // 4) + group] for group in range(HALF // 4)]
+        tiles = [pieces[lane * groups + group] for group in range(groups)]
         columns.append(jnp.concatenate(tiles, axis=0))
     return jnp.concatenate(columns, axis=1)
 
 
-def put_both(core, mine, other, start, x):
-    for pieces, half in zip((mine, other), parted(core, x)):
-        put(pieces, start, half)
-
-
-def take_both(core, mine, other, start, size):
-    return ordered(core, take(mine, start, size), take(other, start, size))
+def put_rows(core, mine, other, start, x):
+    for half in range(2):
+        low, high = max(start, half * OWN), min(start + x.shape[1], (half + 1) * OWN)
+        if low < high:
+            own = x[:, low - start : high - start]
+
+            @pl.when(core == half)
+            def _():
+                put(mine, low - half * OWN, own)
+
+            @pl.when(core != half)
+            def _():
+                put(other, low - half * OWN, own)
 
 
 def ranges(sizes):
@@ -112,34 +122,52 @@
             copy.wait()
         for copy in copies[i + 2] if i + 2 < len(copies) else ():
             copy.start()
-        put_both(core[0], mine, other, start, times_rows(stack, g, e, start, size))
-
-
-def left_kernel(core, z_mine, z_other, inverse, g, e, mine, other, stack):
+        put_rows(core[0], mine, other, start, times_rows(stack, g, e, start, size))
+
+
+def right_stack(core, z_mine, z_other, inverse):
     z = ordered(core[0], z_mine[...], z_other[...])
-    right = jnp.dot(inverse[...], z, precision=HIGH, preferred_element_type=F32) * (1.0 / REPLICAS)
-    stack[...] = stacked(right)
-    for start, size in ranges(EVEN):
-        put_both(core[0], mine, other, start, times_rows(stack, g, e, start, size))
-
-
-def right_kernel(core, l_mine, l_other, g, e, z_mine, z_other, gram, stack):
-    for start, size in ranges(EVEN):
-        stack[:, pl.ds(start, size)] = stacked(take_both(core[0], l_mine, l_other, start, size))
+    return stacked(jnp.dot(inverse[...], z, precision=HIGH, preferred_element_type=F32) * (1.0 / REPLICAS))
+
+
+def give_kernel(core, g, e, send):
+    for start in range(0, OWN, 256):
+        rows = pl.ds(pl.multiple_of((1 - core[0]) * OWN + start, 256), 256)
+        send[pl.ds(start, 256), :] = g[rows, :].astype(F32) + e[rows, :].astype(F32)
+
+
+def merge_kernel(core, g, e, received, high, low):
+    for start in range(0, OWN, 256):
+        rows = pl.ds(pl.multiple_of(core[0] * OWN + start, 256), 256)
+        here = pl.ds(start, 256)
+        total = g[rows, :].astype(F32) + e[rows, :].astype(F32) + received[here, :]
+        high[here, :], low[here, :] = split(total, 2)
+
+
+def left_kernel(core, z_mine, z_other, inverse, high, low, term, stack):
+    stack[...] = right_stack(core, z_mine, z_other, inverse)
+    for start, size in ranges(PART):
+        put(term, start, times_rows(stack, high, low, start, size))
+
+
+def right_kernel(core, left, high, low, z_mine, z_other, gram, stack):
+    for start, size in ranges(PART):
+        stack[:, pl.ds(start, size)] = stacked(take(left, start, size))
     for part in range(COLS // WIDE):
         cols = pl.ds(part * WIDE, WIDE)
-        z = jnp.dot(stack[...], g[:, cols], preferred_element_type=F32)
-        z = fold(z + jnp.dot(stack[...], e[:, cols], preferred_element_type=F32))
+        z = jnp.dot(stack[...], high[:, cols], preferred_element_type=F32)
+        z = fold(z + jnp.dot(stack[...], low[:, cols], preferred_element_type=F32))
         z_mine[:, cols], z_other[:, cols] = parted(core[0], z)
     products = lax.dot_general(stack[...], stack[...], (((1,), (1,)), ((), ())), preferred_element_type=F32)
     rows = fold(products)
     gram[...] = rows[:, :RANK] + (rows[:, RANK : 2 * RANK] + rows[:, 2 * RANK :])
 
 
-def factor_kernel(gram, inverse):
+def factor_kernel(grams, inverse):
     rows = lax.broadcasted_iota(jnp.int32, (RANK, RANK), 0)
     cols = lax.broadcasted_iota(jnp.int32, (RANK, RANK), 1)
-    work = jnp.concatenate([gram[...], (rows == cols).astype(F32)], axis=1)
+    gram = sum(part[...] for part in grams)
+    work = jnp.concatenate([gram, (rows == cols).astype(F32)], axis=1)
     for start in range(0, RANK, 8):
         column = [jnp.broadcast_to(work[:, start + j : start + j + 1], work.shape) for j in range(8)]
         row = [work[j : j + 1, :] for j in range(8)]
@@ -159,9 +187,11 @@
 def ready_kernel(core, l_mine, l_other, w_far, factors, w, w_sem):
     load = pltpu.make_async_copy(w_far, w, w_sem)
     load.start()
-    for start, size in ranges(EVEN):
-        high, low = split(take_both(core[0], l_mine, l_other, start, size), 2)
-        factors[pl.ds(start, size), :] = jnp.concatenate([high, high, low], axis=0).T
+    for pieces, base in ((l_mine, core[0]), (l_other, 1 - core[0])):
+        for start, size in ranges(PART):
+            high, low = split(take(pieces, start, size), 2)
+            rows = pl.ds(pl.multiple_of(base * OWN + start, 256), size)
+            factors[rows, :] = jnp.concatenate([high, high, low], axis=0).T
     load.wait()
 
 
@@ -193,6 +223,7 @@
 PIECES = jax.ShapeDtypeStruct((TILES, 4, 128), F32)
 ZHALF = jax.ShapeDtypeStruct((HALF, COLS), F32)
 NEAR_ARRAY = pltpu.VMEM((ROWS, COLS), BF16)
+NEAR_HALF = pltpu.VMEM((OWN, COLS), BF16)
 SQUARE = jax.ShapeDtypeStruct((RANK, RANK), F32)
 STACK = pltpu.VMEM((3 * RANK, COLS), BF16)
 
@@ -236,40 +267,64 @@
     )(core, *far(q, g, e))
 
 
-def left_pass(core, z_mine, z_other, inverse, g, e):
+def give(core, g, e):
+    return pl.pallas_call(
+        give_kernel,
+        in_specs=[SCALAR] + [NEAR] * 2,
+        out_specs=NEAR,
+        out_shape=pltpu.VMEM((OWN, COLS), F32),
+        compiler_params=params(SMALL),
+        cost_estimate=pl.CostEstimate(flops=10**9, bytes_accessed=8 * OWN * COLS, transcendentals=0),
+        name="give",
+    )(core, *near(g, e))
+
+
+def merge(core, g, e, received):
+    return pl.pallas_call(
+        merge_kernel,
+        in_specs=[SCALAR] + [NEAR] * 3,
+        out_specs=[NEAR] * 2,
+        out_shape=[NEAR_HALF, NEAR_HALF],
+        compiler_params=params(SMALL),
+        cost_estimate=pl.CostEstimate(flops=10**9, bytes_accessed=8 * OWN * COLS, transcendentals=0),
+        name="merge",
+    )(core, *near(g, e, received))
+
+
+def left_pass(core, z_mine, z_other, inverse, high, low):
     return pl.pallas_call(
         left_kernel,
         in_specs=[SCALAR] + [NEAR] * 5,
-        out_specs=[NEAR] * 2,
-        out_shape=[PIECES, PIECES],
+        out_specs=NEAR,
+        out_shape=PIECES,
         scratch_shapes=[STACK],
-        compiler_params=params(LIMIT),
-        cost_estimate=cost(6, 4 * ROWS * COLS),
+        compiler_params=params(SMALL),
+        cost_estimate=cost(3, 2 * ROWS * COLS),
         name="left_pass",
-    )(core, z_mine, z_other, inverse, *near(g, e))
-
-
-def right_pass(core, l_mine, l_other, g, e):
+    )(core, z_mine, z_other, inverse, *near(high, low))
+
+
+def right_pass(core, left, high, low):
     return pl.pallas_call(
         right_kernel,
-        in_specs=[SCALAR] + [NEAR] * 4,
+        in_specs=[SCALAR] + [NEAR] * 3,
         out_specs=[NEAR] * 3,
         out_shape=[ZHALF, ZHALF, SQUARE],
-        scratch_shapes=[pltpu.VMEM((3 * RANK, ROWS), BF16)],
-        compiler_params=params(LIMIT),
-        cost_estimate=cost(6, 4 * ROWS * COLS),
+        scratch_shapes=[pltpu.VMEM((3 * RANK, OWN), BF16)],
+        compiler_params=params(SMALL),
+        cost_estimate=cost(3, 2 * ROWS * COLS),
         name="right_pass",
-    )(core, l_mine, l_other, *near(g, e))
-
-
-def factor(gram):
+    )(core, left, *near(high, low))
+
+
+def factor(*grams):
     return pl.pallas_call(
         factor_kernel,
         out_shape=SQUARE,
         compiler_params=params(SMALL),
         cost_estimate=pl.CostEstimate(flops=4 * 10**9, bytes_accessed=8 * RANK**2, transcendentals=RANK),
         name="factor",
-    )(gram)
+    )(grams)
 
 
 def ready(core, l_mine, l_other, w):
@@ -327,35 +382,31 @@
     return lax.all_to_all(x, CHIP_AXES, 0, 0, tiled=True).reshape(TILES, 4, 128)
 
 
-def sum_left(mine, other):
-    term = exchange(mean(exchange(mine + swap(other))))
-    return term, swap(term)
-
-
-def sum_right(mine, other, beside=None):
-    half = mine + swap(other)
-    if beside is not None:
-        step, args = beside
-        half, args = lax.optimization_barrier((half, args))
-        done = step(*args)
+def mean_left(term):
+    return exchange(mean(exchange(term)))
+
+
+def sum_right(mine, other, run=None):
+    half, given = lax.optimization_barrier((mine + swap(other), run[1] if run else ()))
     parts = [along_y(half, shift) for shift in (1, 3, 2)]
-    if beside is not None:
-        parts, done = lax.optimization_barrier((parts, done))
+    parts, done = lax.optimization_barrier((parts, run[0](*given) if run else ()))
     half = half + parts[0] + parts[1] + parts[2]
-    both = (half, swap(half))
-    return both if beside is None else (both, done)
+    return (half, swap(half)), done
 
 
 def shards(gradients, errors, weight, start_q):
     core = lax.axis_index("core").astype(jnp.int32).reshape(1)
     mine, other, g, e = first_left_pass(core, start_q.T, gradients[0], errors[0])
-    left = sum_left(mine, other)
-    z_mine, z_other, gram = right_pass(core, *left, g, e)
-    right = sum_right(z_mine, z_other)
-    left = sum_left(*left_pass(core, *right, factor(gram), g, e))
-    z_mine, z_other, gram = right_pass(core, *left, g, e)
-    right, (factors, w) = sum_right(z_mine, z_other, (ready, (core, *left, weight)))
-    new_e, new_w, right_factor = renew(core, *right, factor(gram), factors, g, e, w)
+    term, send = lax.optimization_barrier((mine + swap(other), give(core, g, e)))
+    left, received = lax.optimization_barrier((mean_left(term), swap(send)))
+    high, low = merge(core, g, e, received)
+    z_mine, z_other, gram = right_pass(core, left, high, low)
+    right, _ = sum_right(z_mine, z_other)
+    left = mean_left(left_pass(core, *right, factor(gram, swap(gram)), high, low))
+    left_other = swap(left)
+    z_mine, z_other, gram = right_pass(core, left, high, low)
+    right, (factors, w) = sum_right(z_mine, z_other, (ready, (core, left, left_other, weight)))
+    new_e, new_w, right_factor = renew(core, *right, factor(gram, swap(gram)), factors, g, e, w)
     return new_e[None], new_w, right_factor.T
 
 

time: 125 us -> 119 us (0.952)
  waiting for transfers between devices: 15.3 us -> 8.78 us
  Pallas kernels: 24.7 us -> 23.3 us
    ppermute x8 -> x9, waiting for transfers between devices: 7.65 us -> 3.14 us  [swap(): return lax.ppermute(x, 'core', [(0, 1), (1, 0)])]
    ppermute x6, waiting for transfers between devices: 7.65 us -> 5.65 us  [along_y(): return lax.ppermute(x, 'y', [(i, (i + shift) % 4) for i in range(4)])]
    pallas_call x3 -> x5, Pallas kernels: 7.89 us -> 6.28 us  [the longest x2 2.78 us: right_pass(): pl.pallas_call(right_kernel, in_specs=[SCALAR] + [NEAR] * 3, out_specs=[N...]
    ppermute x8 -> x9, starting transfers between devices: 12.3 us -> 13.1 us  [swap(): return lax.ppermute(x, 'core', [(0, 1), (1, 0)])]
  transfers between devices with their start and end apart: 14 -> 15, of which waited for: 12 -> 8; matrix products, arithmetic and copies ran while one was open for 0% -> 0% of each run, Pallas kernels for 5% -> 7%
where the time goes in v4:
time: 119 us; the launch traced here: 118 us
  blocking collectives  66.9 us (56%)
  Pallas kernels  23.3 us (20%)
  starting transfers between devices  18.4 us (15%)
  waiting for transfers between devices  8.78 us (7%)
    all_to_all x4, blocking collectives, exchange(): return lax.all_to_all(x, CHIP_AXES, 0, 0, tiled=True).reshape(TILES, 4, 128)  66.9 us
    ppermute x9, starting transfers between devices, swap(): return lax.ppermute(x, 'core', [(0, 1), (1, 0)])  13.1 us
    ppermute x6, waiting for transfers between devices, along_y(): return lax.ppermute(x, 'y', [(i, (i + shift) % 4) for i in range(4)])  5.65 us
    pallas_call x1, Pallas kernels, first_left_pass(): pl.pallas_call(first_left_kernel, in_specs=[SCALAR, FAR, FAR, FAR], out_s...  5.58 us
    pallas_call x1, Pallas kernels, renew(): pl.pallas_call(renew_kernel, in_specs=[SCALAR] + [NEAR] * 7, out_specs=[F...  5.39 us
    ppermute x6, starting transfers between devices, along_y(): return lax.ppermute(x, 'y', [(i, (i + shift) % 4) for i in range(4)])  5.29 us
    pallas_call x2, Pallas kernels, factor(): pl.pallas_call(factor_kernel, out_shape=SQUARE, compiler_params=params(SM...  3.29 us
    ppermute x9, waiting for transfers between devices, swap(): return lax.ppermute(x, 'core', [(0, 1), (1, 0)])  3.14 us
  transfers between devices with their start and end apart: 15, of which 8 were waited for; matrix products, arithmetic and copies ran while one was open for 0% of the time, Pallas kernels for 7%

profile of v4, /device:TPU:1, one launch (start us, length us, event | category | flops | bytes accessed | tf_op | source)
XLA Modules:
  0.0 118.5 jit_solution(4559655083117569341)
XLA Ops:
  0.6 5.6 %first_left_pass.1 = (f32[192,4,128]{2,1,0:T(4,128)S(1)}, f32[192,4,128]{2,1,0:T(4,128)S(1)}, bf16[3072,768]{1,0:T(8,128)(2,1)S(1)}, bf16[3072,768]{1,0:T(8,128)(2,1)S(1)}) custom-call(s32[1]{0:T(128)} %bitcast.core, f32[64,768]{1,0:T(8,128)} %bitcast.26, bf16[3072,768]{1,0:T(8,128)(2,1)} %bitcast.23, bf16[3072,768]{1,0:T(8,128)(2,1)} %bitcast.24), custom_call_target="tpu_custom_call" | custom-call | flops 1811939328 | bytes 9437184 | tf_op jit(solution)/shard_map/first_left_pass/pallas_call | solution.py:252
  6.2 1.5 %collective-permute-start = (f32[192,4,128]{2,1,0:T(4,128)S(1)}, f32[192,4,128]{2,1,0:T(4,128)S(1)}, u32[]{:S(2)}, u32[]{:S(2)}) collective-permute-start(f32[192,4,128]{2,1,0:T(4,128)S(1)} %get-tuple-element.38), channel_id=1, source_target_pairs={{0,16},{16,0},{1,17},{17,1},{2,18},{18,2},{3,19},{19,3},{4,20},{20... | collective-permute-start | bytes 1179656 | tf_op jit(solution)/shard_map/ppermute | solution.py:363
  7.7 0.5 give.1
  8.2 0.9 collective-permute-done
  9.1 0.1 add.27
  9.2 0.5 collective-permute-start.1
  9.6 22.2 %all_to_all.20 = f32[64,3,4,128]{3,2,1,0:T(4,128)S(1)} all-to-all(f32[64,3,4,128]{3,2,1,0:T(4,128)S(1)} %bitcast.25), channel_id=1, replica_groups=mesh['y'=4,'core'=2,'x'=4,'z'=4] {'y','x','z'}, dimensions={0} | all-to-all | bytes 786432 | tf_op jit(solution)/shard_map/all_to_all | solution.py:382
  31.8 0.1 mean.2
  31.9 14.7 %all_to_all.21 = f32[64,3,4,128]{3,2,1,0:T(4,128)S(1)} all-to-all(f32[64,3,4,128]{3,2,1,0:T(4,128)S(1)} %bitcast.18), channel_id=1, replica_groups=mesh['y'=4,'core'=2,'x'=4,'z'=4] {'y','x','z'}, dimensions={0} | all-to-all | bytes 786432 | tf_op jit(solution)/shard_map/all_to_all | solution.py:382
  46.6 0.0 collective-permute-done.1.received
  46.6 1.1 merge.1
  47.8 1.4 %right_pass.2 = (f32[32,768]{1,0:T(8,128)S(1)}, f32[32,768]{1,0:T(8,128)S(1)}, f32[64,64]{1,0:T(8,128)S(1)}) custom-call(s32[1]{0:T(128)} %bitcast.core, f32[192,4,128]{2,1,0:T(4,128)S(1)} %bitcast.21, bf16[1536,768]{1,0:T(8,128)(2,1)S(1)} %get-tuple-element.45.high, bf16[1536,768]{1,0:T(8,128)(2,1)S(1)} %get-tuple-element.46.low), custom_call_target="tpu_custom_call" | custom-call | flops 905969664 | bytes 4718592 | tf_op jit(solution)/shard_map/right_pass/pallas_call | solution.py:308
  49.1 3.0 %collective-permute-start.2 = (f32[32,768]{1,0:T(8,128)S(1)}, f32[32,768]{1,0:T(8,128)S(1)}, u32[]{:S(2)}, u32[]{:S(2)}) collective-permute-start(f32[32,768]{1,0:T(8,128)S(1)} %get-tuple-element.48), channel_id=1, source_target_pairs={{0,16},{16,0},{1,17},{17,1},{2,18},{18,2},{3,19},{19,3},{4,20},{20... | collective-permute-start | bytes 294920 | tf_op jit(solution)/shard_map/ppermute | solution.py:363
  52.1 0.9 collective-permute-done.2
  53.1 0.4 collective-permute-start.5
  53.5 2.1 %collective-permute-start.4 = (f32[32,768]{1,0:T(8,128)S(1)}, f32[32,768]{1,0:T(8,128)S(1)}, u32[]{:S(2)}, u32[]{:S(2)}) collective-permute-start(f32[32,768]{1,0:T(8,128)S(1)} %add.28), channel_id=1, source_target_pairs={{0,96},{32,0},{64,32},{96,64},{1,97},{33,1},{65,33},{97,65},{2,98}... | collective-permute-start | bytes 294920 | tf_op jit(solution)/shard_map/ppermute | solution.py:367
  55.6 0.0 collective-permute-start.3
  55.6 0.9 collective-permute-start.7
  56.5 2.2 %collective-permute-done.5 = f32[32,768]{1,0:T(8,128)S(1)} collective-permute-done((f32[32,768]{1,0:T(8,128)S(1)}, f32[32,768]{1,0:T(8,128)S(1)}, u32[]{:S(2)}, u32[]{:S(2)}) %collective-permute-start.5) | collective-permute-done | bytes 98336 | tf_op jit(solution)/shard_map/ppermute | solution.py:367
  58.7 0.3 collective-permute-done.4
  59.0 1.7 %collective-permute-done.3 = f32[32,768]{1,0:T(8,128)S(1)} collective-permute-done((f32[32,768]{1,0:T(8,128)S(1)}, f32[32,768]{1,0:T(8,128)S(1)}, u32[]{:S(2)}, u32[]{:S(2)}) %collective-permute-start.3) | collective-permute-done | bytes 98336 | tf_op jit(solution)/shard_map/ppermute | solution.py:367
  60.6 1.8 %collective-permute-start.6 = (f32[32,768]{1,0:T(8,128)S(1)}, f32[32,768]{1,0:T(8,128)S(1)}, u32[]{:S(2)}, u32[]{:S(2)}) collective-permute-start(f32[32,768]{1,0:T(8,128)S(1)} %add_add_fusion.1.z_mine), channel_id=1, source_target_pairs={{0,16},{16,0},{1,17},{17,1},{2,18},{18,2},{3,19},{19,3},{4,20},{20... | collective-permute-start | bytes 294920 | tf_op jit(solution)/shard_map/ppermute | solution.py:363
  62.5 0.0 collective-permute-done.7.grams_1_
  62.5 1.6 %factor.2.inverse = f32[64,64]{1,0:T(8,128)S(1)} custom-call(f32[64,64]{1,0:T(8,128)S(1)} %get-tuple-element.52.grams_0_, f32[64,64]{1,0:T(8,128)S(1)} %collective-permute-done.7.grams_1_), custom_call_target="tpu_custom_call" | custom-call | flops 4000000000 | bytes 32768 | tf_op jit(solution)/shard_map/factor/pallas_call | solution.py:321
  64.1 0.0 collective-permute-done.6.z_other
  64.1 1.9 %left_pass.1 = f32[192,4,128]{2,1,0:T(4,128)S(1)} custom-call(s32[1]{0:T(128)} %bitcast.core, f32[32,768]{1,0:T(8,128)S(1)} %add_add_fusion.1.z_mine, f32[32,768]{1,0:T(8,128)S(1)} %collective-permute-done.6.z_other, f32[64,64]{1,0:T(8,128)S(1)} %factor.2.inverse, bf16[1536,768]{1,0:T(8,128)(2,1)S(1)} %get-tuple-element.45.high, ...), custom_call_target="tpu_custom_call" | custom-call | flops 905969664 | bytes 4718592 | tf_op jit(solution)/shard_map/left_pass/pallas_call | solution.py:295
  66.0 15.4 %all_to_all.22 = f32[64,3,4,128]{3,2,1,0:T(4,128)S(1)} all-to-all(f32[64,3,4,128]{3,2,1,0:T(4,128)S(1)} %bitcast.22), channel_id=1, replica_groups=mesh['y'=4,'core'=2,'x'=4,'z'=4] {'y','x','z'}, dimensions={0} | all-to-all | bytes 786432 | tf_op jit(solution)/shard_map/all_to_all | solution.py:382
  81.4 0.1 mean.3
  81.5 14.7 %all_to_all.23 = f32[64,3,4,128]{3,2,1,0:T(4,128)S(1)} all-to-all(f32[64,3,4,128]{3,2,1,0:T(4,128)S(1)} %bitcast.20), channel_id=1, replica_groups=mesh['y'=4,'core'=2,'x'=4,'z'=4] {'y','x','z'}, dimensions={0} | all-to-all | bytes 786432 | tf_op jit(solution)/shard_map/all_to_all | solution.py:382
  96.2 2.8 %collective-permute-start.9 = (f32[192,4,128]{2,1,0:T(4,128)S(1)}, f32[192,4,128]{2,1,0:T(4,128)S(1)}, u32[]{:S(2)}, u32[]{:S(2)}) collective-permute-start(f32[192,4,128]{2,1,0:T(4,128)S(1)} %bitcast.14), channel_id=1, source_target_pairs={{0,16},{16,0},{1,17},{17,1},{2,18},{18,2},{3,19},{19,3},{4,20},{20... | collective-permute-start | bytes 1179656 | tf_op jit(solution)/shard_map/ppermute | solution.py:363
  99.0 1.4 %right_pass.3 = (f32[32,768]{1,0:T(8,128)S(1)}, f32[32,768]{1,0:T(8,128)S(1)}, f32[64,64]{1,0:T(8,128)S(1)}) custom-call(s32[1]{0:T(128)} %bitcast.core, f32[192,4,128]{2,1,0:T(4,128)S(1)} %bitcast.15, bf16[1536,768]{1,0:T(8,128)(2,1)S(1)} %get-tuple-element.45.high, bf16[1536,768]{1,0:T(8,128)(2,1)S(1)} %get-tuple-element.46.low), custom_call_target="tpu_custom_call" | custom-call | flops 905969664 | bytes 4718592 | tf_op jit(solution)/shard_map/right_pass/pallas_call | solution.py:308
  100.4 0.1 collective-permute-start.8
  100.5 1.3 %collective-permute-done.8 = f32[32,768]{1,0:T(8,128)S(1)} collective-permute-done((f32[32,768]{1,0:T(8,128)S(1)}, f32[32,768]{1,0:T(8,128)S(1)}, u32[]{:S(2)}, u32[]{:S(2)}) %collective-permute-start.8) | collective-permute-done | bytes 98336 | tf_op jit(solution)/shard_map/ppermute | solution.py:363
  101.8 0.0 collective-permute-done.9.l_other
  101.8 0.4 collective-permute-start.12
  102.2 2.4 %collective-permute-start.11 = (f32[32,768]{1,0:T(8,128)S(1)}, f32[32,768]{1,0:T(8,128)S(1)}, u32[]{:S(2)}, u32[]{:S(2)}) collective-permute-start(f32[32,768]{1,0:T(8,128)S(1)} %add.32), channel_id=1, source_target_pairs={{0,96},{32,0},{64,32},{96,64},{1,97},{33,1},{65,33},{97,65},{2,98}... | collective-permute-start | bytes 294920 | tf_op jit(solution)/shard_map/ppermute | solution.py:367
  104.6 0.0 collective-permute-start.10
  104.6 0.7 collective-permute-start.14
  105.3 2.5 %ready.1 = (bf16[3072,192]{1,0:T(8,128)(2,1)S(1)}, bf16[3072,768]{1,0:T(8,128)(2,1)S(1)}) custom-call(s32[1]{0:T(128)} %bitcast.core, f32[192,4,128]{2,1,0:T(4,128)S(1)} %bitcast.16, f32[192,4,128]{2,1,0:T(4,128)S(1)} %collective-permute-done.9.l_other, bf16[3072,768]{1,0:T(8,128)(2,1)} %w_far), custom_call_target="tpu_custom_call" | custom-call | flops 301989888 | bytes 9437184 | tf_op jit(solution)/shard_map/ready/pallas_call | solution.py:331
  107.8 0.0 collective-permute-done.12
  107.8 0.2 collective-permute-done.11
  108.0 1.4 %collective-permute-done.10 = f32[32,768]{1,0:T(8,128)S(1)} collective-permute-done((f32[32,768]{1,0:T(8,128)S(1)}, f32[32,768]{1,0:T(8,128)S(1)}, u32[]{:S(2)}, u32[]{:S(2)}) %collective-permute-start.10) | collective-permute-done | bytes 98336 | tf_op jit(solution)/shard_map/ppermute | solution.py:367
  109.4 1.8 %collective-permute-start.13 = (f32[32,768]{1,0:T(8,128)S(1)}, f32[32,768]{1,0:T(8,128)S(1)}, u32[]{:S(2)}, u32[]{:S(2)}) collective-permute-start(f32[32,768]{1,0:T(8,128)S(1)} %add_add_fusion.z_mine), channel_id=1, source_target_pairs={{0,16},{16,0},{1,17},{17,1},{2,18},{18,2},{3,19},{19,3},{4,20},{20... | collective-permute-start | bytes 294920 | tf_op jit(solution)/shard_map/ppermute | solution.py:363
  111.3 0.0 collective-permute-done.14.grams_1_
  111.3 1.6 %factor.3.inverse = f32[64,64]{1,0:T(8,128)S(1)} custom-call(f32[64,64]{1,0:T(8,128)S(1)} %get-tuple-element.65.grams_0_, f32[64,64]{1,0:T(8,128)S(1)} %collective-permute-done.14.grams_1_), custom_call_target="tpu_custom_call" | custom-call | flops 4000000000 | bytes 32768 | tf_op jit(solution)/shard_map/factor/pallas_call | solution.py:321
  112.9 0.0 collective-permute-done.13.z_other
  112.9 5.4 %renew.1 = (bf16[3072,768]{1,0:T(8,128)(2,1)}, bf16[3072,768]{1,0:T(8,128)(2,1)}, f32[64,768]{1,0:T(8,128)}) custom-call(s32[1]{0:T(128)} %bitcast.core, f32[32,768]{1,0:T(8,128)S(1)} %add_add_fusion.z_mine, f32[32,768]{1,0:T(8,128)S(1)} %collective-permute-done.13.z_other, f32[64,64]{1,0:T(8,128)S(1)} %factor.3.inverse, ...), custom_call_target="tpu_custom_call" | custom-call | flops 905969664 | bytes 23592960 | tf_op jit(solution)/shard_map/renew/pallas_call | solution.py:345
  (4 shorter events, 0.1 us)
Async XLA Ops:
  6.2 2.8 %collective-permute-start = (f32[192,4,128]{2,1,0:T(4,128)S(1)}, f32[192,4,128]{2,1,0:T(4,128)S(1)}, u32[]{:S(2)}, u32[]{:S(2)}) collective-permute-start(f32[192,4,128]{2,1,0:T(4,128)S(1)} %get-tuple-element.38), channel_id=1, source_target_pairs={{0,16},{16,0},{1,17},{17,1},{2,18},{18,2},{3,19},{19,3},{4,20},{20... | collective-permute-start | bytes 1179656 | tf_op jit(solution)/shard_map/ppermute | solution.py:363
  9.2 37.4 %collective-permute-start.1 = (f32[1536,768]{1,0:T(8,128)S(1)}, f32[1536,768]{1,0:T(8,128)S(1)}, u32[]{:S(2)}, u32[]{:S(2)}) collective-permute-start(f32[1536,768]{1,0:T(8,128)S(1)} %give.1), channel_id=1, source_target_pairs={{0,16},{16,0},{1,17},{17,1},{2,18},{18,2},{3,19},{19,3},{4,20},{20... | collective-permute-start | bytes 14155784 | tf_op jit(solution)/shard_map/ppermute | solution.py:363
  49.1 3.9 %collective-permute-start.2 = (f32[32,768]{1,0:T(8,128)S(1)}, f32[32,768]{1,0:T(8,128)S(1)}, u32[]{:S(2)}, u32[]{:S(2)}) collective-permute-start(f32[32,768]{1,0:T(8,128)S(1)} %get-tuple-element.48), channel_id=1, source_target_pairs={{0,16},{16,0},{1,17},{17,1},{2,18},{18,2},{3,19},{19,3},{4,20},{20... | collective-permute-start | bytes 294920 | tf_op jit(solution)/shard_map/ppermute | solution.py:363
  53.1 5.6 %collective-permute-start.5 = (f32[32,768]{1,0:T(8,128)S(1)}, f32[32,768]{1,0:T(8,128)S(1)}, u32[]{:S(2)}, u32[]{:S(2)}) collective-permute-start(f32[32,768]{1,0:T(8,128)S(1)} %add.28), channel_id=1, source_target_pairs={{0,64},{32,96},{64,0},{96,32},{1,65},{33,97},{65,1},{97,33},{2,66}... | collective-permute-start | bytes 294920 | tf_op jit(solution)/shard_map/ppermute | solution.py:367
  53.5 5.4 %collective-permute-start.4 = (f32[32,768]{1,0:T(8,128)S(1)}, f32[32,768]{1,0:T(8,128)S(1)}, u32[]{:S(2)}, u32[]{:S(2)}) collective-permute-start(f32[32,768]{1,0:T(8,128)S(1)} %add.28), channel_id=1, source_target_pairs={{0,96},{32,0},{64,32},{96,64},{1,97},{33,1},{65,33},{97,65},{2,98}... | collective-permute-start | bytes 294920 | tf_op jit(solution)/shard_map/ppermute | solution.py:367
  55.6 5.0 %collective-permute-start.3 = (f32[32,768]{1,0:T(8,128)S(1)}, f32[32,768]{1,0:T(8,128)S(1)}, u32[]{:S(2)}, u32[]{:S(2)}) collective-permute-start(f32[32,768]{1,0:T(8,128)S(1)} %add.28), channel_id=1, source_target_pairs={{0,32},{32,64},{64,96},{96,0},{1,33},{33,65},{65,97},{97,1},{2,34}... | collective-permute-start | bytes 294920 | tf_op jit(solution)/shard_map/ppermute | solution.py:367
  55.6 6.8 %collective-permute-start.7 = (f32[64,64]{1,0:T(8,128)S(1)}, f32[64,64]{1,0:T(8,128)S(1)}, u32[]{:S(2)}, u32[]{:S(2)}) collective-permute-start(f32[64,64]{1,0:T(8,128)S(1)} %get-tuple-element.52.grams_0_), channel_id=1, source_target_pairs={{0,16},{16,0},{1,17},{17,1},{2,18},{18,2},{3,19},{19,3},{4,20},{20... | collective-permute-start | bytes 49160 | tf_op jit(solution)/shard_map/ppermute | solution.py:363
  60.6 3.5 %collective-permute-start.6 = (f32[32,768]{1,0:T(8,128)S(1)}, f32[32,768]{1,0:T(8,128)S(1)}, u32[]{:S(2)}, u32[]{:S(2)}) collective-permute-start(f32[32,768]{1,0:T(8,128)S(1)} %add_add_fusion.1.z_mine), channel_id=1, source_target_pairs={{0,16},{16,0},{1,17},{17,1},{2,18},{18,2},{3,19},{19,3},{4,20},{20... | collective-permute-start | bytes 294920 | tf_op jit(solution)/shard_map/ppermute | solution.py:363
  96.2 5.6 %collective-permute-start.9 = (f32[192,4,128]{2,1,0:T(4,128)S(1)}, f32[192,4,128]{2,1,0:T(4,128)S(1)}, u32[]{:S(2)}, u32[]{:S(2)}) collective-permute-start(f32[192,4,128]{2,1,0:T(4,128)S(1)} %bitcast.14), channel_id=1, source_target_pairs={{0,16},{16,0},{1,17},{17,1},{2,18},{18,2},{3,19},{19,3},{4,20},{20... | collective-permute-start | bytes 1179656 | tf_op jit(solution)/shard_map/ppermute | solution.py:363
  100.4 1.4 %collective-permute-start.8 = (f32[32,768]{1,0:T(8,128)S(1)}, f32[32,768]{1,0:T(8,128)S(1)}, u32[]{:S(2)}, u32[]{:S(2)}) collective-permute-start(f32[32,768]{1,0:T(8,128)S(1)} %get-tuple-element.54), channel_id=1, source_target_pairs={{0,16},{16,0},{1,17},{17,1},{2,18},{18,2},{3,19},{19,3},{4,20},{20... | collective-permute-start | bytes 294920 | tf_op jit(solution)/shard_map/ppermute | solution.py:363
  101.8 6.0 %collective-permute-start.12 = (f32[32,768]{1,0:T(8,128)S(1)}, f32[32,768]{1,0:T(8,128)S(1)}, u32[]{:S(2)}, u32[]{:S(2)}) collective-permute-start(f32[32,768]{1,0:T(8,128)S(1)} %add.32), channel_id=1, source_target_pairs={{0,64},{32,96},{64,0},{96,32},{1,65},{33,97},{65,1},{97,33},{2,66}... | collective-permute-start | bytes 294920 | tf_op jit(solution)/shard_map/ppermute | solution.py:367
  102.2 5.8 %collective-permute-start.11 = (f32[32,768]{1,0:T(8,128)S(1)}, f32[32,768]{1,0:T(8,128)S(1)}, u32[]{:S(2)}, u32[]{:S(2)}) collective-permute-start(f32[32,768]{1,0:T(8,128)S(1)} %add.32), channel_id=1, source_target_pairs={{0,96},{32,0},{64,32},{96,64},{1,97},{33,1},{65,33},{97,65},{2,98}... | collective-permute-start | bytes 294920 | tf_op jit(solution)/shard_map/ppermute | solution.py:367
  104.6 4.8 %collective-permute-start.10 = (f32[32,768]{1,0:T(8,128)S(1)}, f32[32,768]{1,0:T(8,128)S(1)}, u32[]{:S(2)}, u32[]{:S(2)}) collective-permute-start(f32[32,768]{1,0:T(8,128)S(1)} %add.32), channel_id=1, source_target_pairs={{0,32},{32,64},{64,96},{96,0},{1,33},{33,65},{65,97},{97,1},{2,34}... | collective-permute-start | bytes 294920 | tf_op jit(solution)/shard_map/ppermute | solution.py:367
  104.6 6.7 %collective-permute-start.14 = (f32[64,64]{1,0:T(8,128)S(1)}, f32[64,64]{1,0:T(8,128)S(1)}, u32[]{:S(2)}, u32[]{:S(2)}) collective-permute-start(f32[64,64]{1,0:T(8,128)S(1)} %get-tuple-element.65.grams_0_), channel_id=1, source_target_pairs={{0,16},{16,0},{1,17},{17,1},{2,18},{18,2},{3,19},{19,3},{4,20},{20... | collective-permute-start | bytes 49160 | tf_op jit(solution)/shard_map/ppermute | solution.py:363
  109.4 3.5 %collective-permute-start.13 = (f32[32,768]{1,0:T(8,128)S(1)}, f32[32,768]{1,0:T(8,128)S(1)}, u32[]{:S(2)}, u32[]{:S(2)}) collective-permute-start(f32[32,768]{1,0:T(8,128)S(1)} %add_add_fusion.z_mine), channel_id=1, source_target_pairs={{0,16},{16,0},{1,17},{17,1},{2,18},{18,2},{3,19},{19,3},{4,20},{20... | collective-permute-start | bytes 294920 | tf_op jit(solution)/shard_map/ppermute | solution.py:363

commit v5 on v4

--- a/solution.py
+++ b/solution.py
@@ -6,13 +6,12 @@
 from jax.sharding import Mesh, PartitionSpec as P
 
 F32, BF16 = jnp.float32, jnp.bfloat16
-HIGH = lax.Precision.HIGHEST
 RANK, HALF = 64, 32
 ROWS, COLS = 3072, 768
 WIDE = 256
 OWN = ROWS // 2
 EVEN = (1024,) * 3
-PART = (768,) * 2
+PART = (512,) * 3
 LAST = (256,) * 12
 CHIPS = 64
 TILES = HALF * ROWS // 512
@@ -125,9 +124,9 @@
         put_rows(core[0], mine, other, start, times_rows(stack, g, e, start, size))
 
 
-def right_stack(core, z_mine, z_other, inverse):
+def right_factor(core, z_mine, z_other, inverse):
     z = ordered(core[0], z_mine[...], z_other[...])
-    return stacked(jnp.dot(inverse[...], z, precision=HIGH, preferred_element_type=F32) * (1.0 / REPLICAS))
+    return product(inverse[...], z) * (1.0 / REPLICAS)
 
 
 def give_kernel(core, g, e, send):
@@ -136,31 +135,54 @@
         send[pl.ds(start, 256), :] = g[rows, :].astype(F32) + e[rows, :].astype(F32)
 
 
-def merge_kernel(core, g, e, received, high, low):
+def merge_rows(core, g, e, received, high, low, cols):
     for start in range(0, OWN, 256):
         rows = pl.ds(pl.multiple_of(core[0] * OWN + start, 256), 256)
         here = pl.ds(start, 256)
-        total = g[rows, :].astype(F32) + e[rows, :].astype(F32) + received[here, :]
-        high[here, :], low[here, :] = split(total, 2)
+        total = g[rows, cols].astype(F32) + e[rows, cols].astype(F32) + received[here, cols]
+        high[here, cols], low[here, cols] = split(total, 2)
+
+
+def product(a, b):
+    left, right = split(a, 3), split(b, 3)
+    pairs = ((0, 2), (1, 1), (2, 0), (0, 1), (1, 0), (0, 0))
+    left = jnp.concatenate([left[i] for i, _ in pairs], axis=1)
+    right = jnp.concatenate([right[j] for _, j in pairs], axis=0)
+    return jnp.dot(left, right, preferred_element_type=F32)
 
 
 def left_kernel(core, z_mine, z_other, inverse, high, low, term, stack):
-    stack[...] = right_stack(core, z_mine, z_other, inverse)
+    stack[...] = stacked(right_factor(core, z_mine, z_other, inverse))
     for start, size in ranges(PART):
         put(term, start, times_rows(stack, high, low, start, size))
 
 
-def right_kernel(core, left, high, low, z_mine, z_other, gram, stack):
+def times_columns(core, stack, first, second, z_mine, z_other, cols):
+    z = jnp.dot(stack[...], first[:, cols], preferred_element_type=F32)
+    z = fold(z + jnp.dot(stack[...], second[:, cols], preferred_element_type=F32))
+    z_mine[:, cols], z_other[:, cols] = parted(core[0], z)
+
+
+def stack_left(left, stack, gram):
     for start, size in ranges(PART):
         stack[:, pl.ds(start, size)] = stacked(take(left, start, size))
-    for part in range(COLS // WIDE):
-        cols = pl.ds(part * WIDE, WIDE)
-        z = jnp.dot(stack[...], high[:, cols], preferred_element_type=F32)
-        z = fold(z + jnp.dot(stack[...], low[:, cols], preferred_element_type=F32))
-        z_mine[:, cols], z_other[:, cols] = parted(core[0], z)
     products = lax.dot_general(stack[...], stack[...], (((1,), (1,)), ((), ())), preferred_element_type=F32)
     rows = fold(products)
     gram[...] = rows[:, :RANK] + (rows[:, RANK : 2 * RANK] + rows[:, 2 * RANK :])
+
+
+def first_right_kernel(core, left, g, e, received, high, low, z_mine, z_other, gram, stack):
+    stack_left(left, stack, gram)
+    for part in range(COLS // WIDE):
+        cols = pl.ds(part * WIDE, WIDE)
+        merge_rows(core, g, e, received, high, low, cols)
+        times_columns(core, stack, high, low, z_mine, z_other, cols)
+
+
+def right_kernel(core, left, high, low, z_mine, z_other, gram, stack):
+    stack_left(left, stack, gram)
+    for part in range(COLS // WIDE):
+        times_columns(core, stack, high, low, z_mine, z_other, pl.ds(part * WIDE, WIDE))
 
 
 def factor_kernel(grams, inverse):
@@ -196,10 +218,9 @@
 
 
 def renew_kernel(core, z_mine, z_other, inverse, factors, g, e, w, new_e, new_w, right_out, e_near, w_near, e_sem, w_sem):
-    z = ordered(core[0], z_mine[...], z_other[...])
-    right = jnp.dot(inverse[...], z, precision=HIGH, preferred_element_type=F32) * (1.0 / REPLICAS)
+    right = right_factor(core, z_mine, z_other, inverse)
     right_out[...] = right
-    mixed = lax.dot_general(inverse[...], right, (((0,), (0,)), ((), ())), precision=HIGH, preferred_element_type=F32)
+    mixed = product(inverse[...].T, right)
     high, low = split(mixed, 2)
     stack = jnp.concatenate([high, low, high], axis=0)
     stores = []
@@ -279,16 +300,17 @@
     )(core, *near(g, e))
 
 
-def merge(core, g, e, received):
-    return pl.pallas_call(
-        merge_kernel,
-        in_specs=[SCALAR] + [NEAR] * 3,
-        out_specs=[NEAR] * 2,
-        out_shape=[NEAR_HALF, NEAR_HALF],
-        compiler_params=params(SMALL),
-        cost_estimate=pl.CostEstimate(flops=10**9, bytes_accessed=8 * OWN * COLS, transcendentals=0),
-        name="merge",
-    )(core, *near(g, e, received))
+def first_right_pass(core, left, g, e, received):
+    return pl.pallas_call(
+        first_right_kernel,
+        in_specs=[SCALAR] + [NEAR] * 4,
+        out_specs=[NEAR] * 5,
+        out_shape=[NEAR_HALF, NEAR_HALF, ZHALF, ZHALF, SQUARE],
+        scratch_shapes=[pltpu.VMEM((3 * RANK, OWN), BF16)],
+        compiler_params=params(LIMIT),
+        cost_estimate=cost(3, 4 * ROWS * COLS),
+        name="first_right_pass",
+    )(core, left, *near(g, e, received))
 
 
 def left_pass(core, z_mine, z_other, inverse, high, low):
@@ -386,12 +408,12 @@
     return exchange(mean(exchange(term)))
 
 
-def sum_right(mine, other, run=None):
-    half, given = lax.optimization_barrier((mine + swap(other), run[1] if run else ()))
+def sum_right(mine, other, gram, run=None):
+    half, grams, given = lax.optimization_barrier((mine + swap(other), (gram, swap(gram)), run[1] if run else ()))
     parts = [along_y(half, shift) for shift in (1, 3, 2)]
-    parts, done = lax.optimization_barrier((parts, run[0](*given) if run else ()))
-    half = half + parts[0] + parts[1] + parts[2]
-    return (half, swap(half)), done
+    parts, inverse, done = lax.optimization_barrier((parts, factor(*grams), run[0](*given) if run else ()))
+    half = (half + parts[2]) + (parts[0] + parts[1])
+    return (half, swap(half), inverse), done
 
 
 def shards(gradients, errors, weight, start_q):
@@ -399,14 +421,12 @@
     mine, other, g, e = first_left_pass(core, start_q.T, gradients[0], errors[0])
     term, send = lax.optimization_barrier((mine + swap(other), give(core, g, e)))
     left, received = lax.optimization_barrier((mean_left(term), swap(send)))
-    high, low = merge(core, g, e, received)
-    z_mine, z_other, gram = right_pass(core, left, high, low)
-    right, _ = sum_right(z_mine, z_other)
-    left = mean_left(left_pass(core, *right, factor(gram, swap(gram)), high, low))
+    high, low, *terms = first_right_pass(core, left, g, e, received)
+    right, _ = sum_right(*terms)
+    left = mean_left(left_pass(core, *right, high, low))
     left_other = swap(left)
-    z_mine, z_other, gram = right_pass(core, left, high, low)
-    right, (factors, w) = sum_right(z_mine, z_other, (ready, (core, left, left_other, weight)))
-    new_e, new_w, right_factor = renew(core, *right, factor(gram, swap(gram)), factors, g, e, w)
+    right, (factors, w) = sum_right(*right_pass(core, left, high, low), (ready, (core, left, left_other, weight)))
+    new_e, new_w, right_factor = renew(core, *right, factors, g, e, w)
     return new_e[None], new_w, right_factor.T
 
 

time: 119 us -> 116 us (0.975)
  starting transfers between devices: 18.4 us -> 16.6 us
    ppermute x9, waiting for transfers between devices: 3.14 us -> 4.72 us  [swap(): return lax.ppermute(x, 'core', [(0, 1), (1, 0)])]
    pallas_call x2 -> x1, Pallas kernels: 2.78 us -> 1.25 us  [right_pass(): pl.pallas_call(right_kernel, in_specs=[SCALAR] + [NEAR] * 3, out_specs=[N...]
    ppermute x9, starting transfers between devices: 13.1 us -> 11.7 us  [swap(): return lax.ppermute(x, 'core', [(0, 1), (1, 0)])]
  transfers between devices with their start and end apart: 15 -> 15, of which waited for: 8 -> 11; matrix products, arithmetic and copies ran while one was open for 0% -> 0% of each run, Pallas kernels for 7% -> 6%
where the time goes in v5:
time: 116 us
  blocking collectives  66.5 us (57%)
  Pallas kernels  22.2 us (19%)
  starting transfers between devices  16.6 us (14%)
  waiting for transfers between devices  9.74 us (8%)
    all_to_all x4, blocking collectives, exchange(): return lax.all_to_all(x, CHIP_AXES, 0, 0, tiled=True).reshape(TILES, 4, 128)  66.5 us
    ppermute x9, starting transfers between devices, swap(): return lax.ppermute(x, 'core', [(0, 1), (1, 0)])  11.7 us
    pallas_call x1, Pallas kernels, first_left_pass(): pl.pallas_call(first_left_kernel, in_specs=[SCALAR, FAR, FAR, FAR], out_s...  5.58 us
    pallas_call x1, Pallas kernels, renew(): pl.pallas_call(renew_kernel, in_specs=[SCALAR] + [NEAR] * 7, out_specs=[F...  5.29 us
    ppermute x6, waiting for transfers between devices, along_y(): return lax.ppermute(x, 'y', [(i, (i + shift) % 4) for i in range(4)])  5.02 us
    ppermute x6, starting transfers between devices, along_y(): return lax.ppermute(x, 'y', [(i, (i + shift) % 4) for i in range(4)])  4.87 us
    ppermute x9, waiting for transfers between devices, swap(): return lax.ppermute(x, 'core', [(0, 1), (1, 0)])  4.72 us
    pallas_call x2, Pallas kernels, factor(): pl.pallas_call(factor_kernel, out_shape=SQUARE, compiler_params=params(SM...  3.29 us
  transfers between devices with their start and end apart: 15, of which 11 were waited for; matrix products, arithmetic and copies ran while one was open for 0% of the time, Pallas kernels for 6%

profile of v5, /device:TPU:1, one launch (start us, length us, event | category | flops | bytes accessed | tf_op | source)
XLA Modules:
  0.0 116.1 jit_solution(11774510268799372780)
XLA Ops:
  0.6 5.6 %first_left_pass.1 = (f32[192,4,128]{2,1,0:T(4,128)S(1)}, f32[192,4,128]{2,1,0:T(4,128)S(1)}, bf16[3072,768]{1,0:T(8,128)(2,1)S(1)}, bf16[3072,768]{1,0:T(8,128)(2,1)S(1)}) custom-call(s32[1]{0:T(128)} %bitcast.core, f32[64,768]{1,0:T(8,128)} %bitcast.26, bf16[3072,768]{1,0:T(8,128)(2,1)} %bitcast.23, bf16[3072,768]{1,0:T(8,128)(2,1)} %bitcast.24), custom_call_target="tpu_custom_call" | custom-call | flops 1811939328 | bytes 9437184 | tf_op jit(solution)/shard_map/first_left_pass/pallas_call | solution.py:273
  6.2 1.5 %collective-permute-start = (f32[192,4,128]{2,1,0:T(4,128)S(1)}, f32[192,4,128]{2,1,0:T(4,128)S(1)}, u32[]{:S(2)}, u32[]{:S(2)}) collective-permute-start(f32[192,4,128]{2,1,0:T(4,128)S(1)} %get-tuple-element.45), channel_id=1, source_target_pairs={{0,16},{16,0},{1,17},{17,1},{2,18},{18,2},{3,19},{19,3},{4,20},{20... | collective-permute-start | bytes 1179656 | tf_op jit(solution)/shard_map/ppermute | solution.py:385
  7.7 0.5 give.1
  8.2 0.9 collective-permute-done
  9.1 0.1 add.27
  9.2 0.5 collective-permute-start.1
  9.6 22.2 %all_to_all.20 = f32[64,3,4,128]{3,2,1,0:T(4,128)S(1)} all-to-all(f32[64,3,4,128]{3,2,1,0:T(4,128)S(1)} %bitcast.25), channel_id=1, replica_groups=mesh['y'=4,'core'=2,'x'=4,'z'=4] {'y','x','z'}, dimensions={0} | all-to-all | bytes 786432 | tf_op jit(solution)/shard_map/all_to_all | solution.py:404
  31.8 0.1 mean.2
  31.9 14.7 %all_to_all.21 = f32[64,3,4,128]{3,2,1,0:T(4,128)S(1)} all-to-all(f32[64,3,4,128]{3,2,1,0:T(4,128)S(1)} %bitcast.18), channel_id=1, replica_groups=mesh['y'=4,'core'=2,'x'=4,'z'=4] {'y','x','z'}, dimensions={0} | all-to-all | bytes 786432 | tf_op jit(solution)/shard_map/all_to_all | solution.py:404
  46.6 0.0 collective-permute-done.1.received
  46.6 2.0 %first_right_pass.1 = (bf16[1536,768]{1,0:T(8,128)(2,1)S(1)}, bf16[1536,768]{1,0:T(8,128)(2,1)S(1)}, f32[32,768]{1,0:T(8,128)S(1)}, f32[32,768]{1,0:T(8,128)S(1)}, f32[64,64]{1,0:T(8,128)S(1)}) custom-call(s32[1]{0:T(128)} %bitcast.core, f32[192,4,128]{2,1,0:T(4,128)S(1)} %bitcast.21, bf16[3072,768]{1,0:T(8,128)(2,1)S(1)} %get-tuple-element.46.g, ...), custom_call_target="tpu_custom_call" | custom-call | flops 905969664 | bytes 9437184 | tf_op jit(solution)/shard_map/first_right_pass/pallas_call | solution.py:304
  48.6 3.0 %collective-permute-start.2 = (f32[32,768]{1,0:T(8,128)S(1)}, f32[32,768]{1,0:T(8,128)S(1)}, u32[]{:S(2)}, u32[]{:S(2)}) collective-permute-start(f32[32,768]{1,0:T(8,128)S(1)} %get-tuple-element.53), channel_id=1, source_target_pairs={{0,16},{16,0},{1,17},{17,1},{2,18},{18,2},{3,19},{19,3},{4,20},{20... | collective-permute-start | bytes 294920 | tf_op jit(solution)/shard_map/ppermute | solution.py:385
  51.5 0.1 collective-permute-start.3
  51.6 0.9 collective-permute-done.2
  52.5 0.2 collective-permute-done.3.grams_1_
  52.8 0.4 collective-permute-start.6
  53.1 2.1 %collective-permute-start.5 = (f32[32,768]{1,0:T(8,128)S(1)}, f32[32,768]{1,0:T(8,128)S(1)}, u32[]{:S(2)}, u32[]{:S(2)}) collective-permute-start(f32[32,768]{1,0:T(8,128)S(1)} %add.28), channel_id=1, source_target_pairs={{0,96},{32,0},{64,32},{96,64},{1,97},{33,1},{65,33},{97,65},{2,98}... | collective-permute-start | bytes 294920 | tf_op jit(solution)/shard_map/ppermute | solution.py:389
  55.2 0.0 collective-permute-start.4
  55.2 1.6 %factor.2.inverse = f32[64,64]{1,0:T(8,128)S(1)} custom-call(f32[64,64]{1,0:T(8,128)S(1)} %get-tuple-element.56.grams_0_, f32[64,64]{1,0:T(8,128)S(1)} %collective-permute-done.3.grams_1_), custom_call_target="tpu_custom_call" | custom-call | flops 4000000000 | bytes 32768 | tf_op jit(solution)/shard_map/factor/pallas_call | solution.py:343
  56.8 1.6 %collective-permute-done.6 = f32[32,768]{1,0:T(8,128)S(1)} collective-permute-done((f32[32,768]{1,0:T(8,128)S(1)}, f32[32,768]{1,0:T(8,128)S(1)}, u32[]{:S(2)}, u32[]{:S(2)}) %collective-permute-start.6) | collective-permute-done | bytes 98336 | tf_op jit(solution)/shard_map/ppermute | solution.py:389
  58.5 0.3 collective-permute-done.5
  58.7 1.8 %collective-permute-done.4 = f32[32,768]{1,0:T(8,128)S(1)} collective-permute-done((f32[32,768]{1,0:T(8,128)S(1)}, f32[32,768]{1,0:T(8,128)S(1)}, u32[]{:S(2)}, u32[]{:S(2)}) %collective-permute-start.4) | collective-permute-done | bytes 98336 | tf_op jit(solution)/shard_map/ppermute | solution.py:389
  60.6 1.4 %collective-permute-start.7 = (f32[32,768]{1,0:T(8,128)S(1)}, f32[32,768]{1,0:T(8,128)S(1)}, u32[]{:S(2)}, u32[]{:S(2)}) collective-permute-start(f32[32,768]{1,0:T(8,128)S(1)} %add_add_fusion.1.z_mine), channel_id=1, source_target_pairs={{0,16},{16,0},{1,17},{17,1},{2,18},{18,2},{3,19},{19,3},{4,20},{20... | collective-permute-start | bytes 294920 | tf_op jit(solution)/shard_map/ppermute | solution.py:385
  62.0 0.9 collective-permute-done.7.z_other
  63.0 1.8 %left_pass.1 = f32[192,4,128]{2,1,0:T(4,128)S(1)} custom-call(s32[1]{0:T(128)} %bitcast.core, f32[32,768]{1,0:T(8,128)S(1)} %add_add_fusion.1.z_mine, f32[32,768]{1,0:T(8,128)S(1)} %collective-permute-done.7.z_other, f32[64,64]{1,0:T(8,128)S(1)} %factor.2.inverse, bf16[1536,768]{1,0:T(8,128)(2,1)S(1)} %get-tuple-element.62.high, ...), custom_call_target="tpu_custom_call" | custom-call | flops 905969664 | bytes 4718592 | tf_op jit(solution)/shard_map/left_pass/pallas_call | solution.py:317
  64.8 15.0 %all_to_all.22 = f32[64,3,4,128]{3,2,1,0:T(4,128)S(1)} all-to-all(f32[64,3,4,128]{3,2,1,0:T(4,128)S(1)} %bitcast.22), channel_id=1, replica_groups=mesh['y'=4,'core'=2,'x'=4,'z'=4] {'y','x','z'}, dimensions={0} | all-to-all | bytes 786432 | tf_op jit(solution)/shard_map/all_to_all | solution.py:404
  79.8 0.1 mean.3
  79.9 14.6 %all_to_all.23 = f32[64,3,4,128]{3,2,1,0:T(4,128)S(1)} all-to-all(f32[64,3,4,128]{3,2,1,0:T(4,128)S(1)} %bitcast.20), channel_id=1, replica_groups=mesh['y'=4,'core'=2,'x'=4,'z'=4] {'y','x','z'}, dimensions={0} | all-to-all | bytes 786432 | tf_op jit(solution)/shard_map/all_to_all | solution.py:404
  94.5 3.2 %collective-permute-start.10 = (f32[192,4,128]{2,1,0:T(4,128)S(1)}, f32[192,4,128]{2,1,0:T(4,128)S(1)}, u32[]{:S(2)}, u32[]{:S(2)}) collective-permute-start(f32[192,4,128]{2,1,0:T(4,128)S(1)} %bitcast.14), channel_id=1, source_target_pairs={{0,16},{16,0},{1,17},{17,1},{2,18},{18,2},{3,19},{19,3},{4,20},{20... | collective-permute-start | bytes 1179656 | tf_op jit(solution)/shard_map/ppermute | solution.py:385
  97.7 1.2 %right_pass.1 = (f32[32,768]{1,0:T(8,128)S(1)}, f32[32,768]{1,0:T(8,128)S(1)}, f32[64,64]{1,0:T(8,128)S(1)}) custom-call(s32[1]{0:T(128)} %bitcast.core, f32[192,4,128]{2,1,0:T(4,128)S(1)} %bitcast.15, bf16[1536,768]{1,0:T(8,128)(2,1)S(1)} %get-tuple-element.62.high, bf16[1536,768]{1,0:T(8,128)(2,1)S(1)} %get-tuple-element.63.low), custom_call_target="tpu_custom_call" | custom-call | flops 905969664 | bytes 4718592 | tf_op jit(solution)/shard_map/right_pass/pallas_call | solution.py:330
  99.0 0.1 collective-permute-start.8
  99.1 0.5 collective-permute-start.9
  99.6 0.8 collective-permute-done.8
  100.4 0.1 collective-permute-done.9.grams_1_
  100.4 0.0 collective-permute-done.10.l_other
  100.4 0.4 collective-permute-start.13
  100.9 2.0 %collective-permute-start.12 = (f32[32,768]{1,0:T(8,128)S(1)}, f32[32,768]{1,0:T(8,128)S(1)}, u32[]{:S(2)}, u32[]{:S(2)}) collective-permute-start(f32[32,768]{1,0:T(8,128)S(1)} %add.32), channel_id=1, source_target_pairs={{0,96},{32,0},{64,32},{96,64},{1,97},{33,1},{65,33},{97,65},{2,98}... | collective-permute-start | bytes 294920 | tf_op jit(solution)/shard_map/ppermute | solution.py:389
  102.9 0.0 collective-permute-start.11
  102.9 1.6 %factor.3.inverse = f32[64,64]{1,0:T(8,128)S(1)} custom-call(f32[64,64]{1,0:T(8,128)S(1)} %get-tuple-element.68.grams_0_, f32[64,64]{1,0:T(8,128)S(1)} %collective-permute-done.9.grams_1_), custom_call_target="tpu_custom_call" | custom-call | flops 4000000000 | bytes 32768 | tf_op jit(solution)/shard_map/factor/pallas_call | solution.py:343
  104.5 2.4 %ready.1 = (bf16[3072,192]{1,0:T(8,128)(2,1)S(1)}, bf16[3072,768]{1,0:T(8,128)(2,1)S(1)}) custom-call(s32[1]{0:T(128)} %bitcast.core, f32[192,4,128]{2,1,0:T(4,128)S(1)} %bitcast.16, f32[192,4,128]{2,1,0:T(4,128)S(1)} %collective-permute-done.10.l_other, bf16[3072,768]{1,0:T(8,128)(2,1)} %w_far), custom_call_target="tpu_custom_call" | custom-call | flops 301989888 | bytes 9437184 | tf_op jit(solution)/shard_map/ready/pallas_call | solution.py:353
  106.9 0.0 collective-permute-done.13
  106.9 0.0 collective-permute-done.12
  106.9 1.3 %collective-permute-done.11 = f32[32,768]{1,0:T(8,128)S(1)} collective-permute-done((f32[32,768]{1,0:T(8,128)S(1)}, f32[32,768]{1,0:T(8,128)S(1)}, u32[]{:S(2)}, u32[]{:S(2)}) %collective-permute-start.11) | collective-permute-done | bytes 98336 | tf_op jit(solution)/shard_map/ppermute | solution.py:389
  108.2 1.5 %collective-permute-start.14 = (f32[32,768]{1,0:T(8,128)S(1)}, f32[32,768]{1,0:T(8,128)S(1)}, u32[]{:S(2)}, u32[]{:S(2)}) collective-permute-start(f32[32,768]{1,0:T(8,128)S(1)} %add_add_fusion.z_mine), channel_id=1, source_target_pairs={{0,16},{16,0},{1,17},{17,1},{2,18},{18,2},{3,19},{19,3},{4,20},{20... | collective-permute-start | bytes 294920 | tf_op jit(solution)/shard_map/ppermute | solution.py:385
  109.7 0.9 collective-permute-done.14.z_other
  110.7 5.3 %renew.1 = (bf16[3072,768]{1,0:T(8,128)(2,1)}, bf16[3072,768]{1,0:T(8,128)(2,1)}, f32[64,768]{1,0:T(8,128)}) custom-call(s32[1]{0:T(128)} %bitcast.core, f32[32,768]{1,0:T(8,128)S(1)} %add_add_fusion.z_mine, f32[32,768]{1,0:T(8,128)S(1)} %collective-permute-done.14.z_other, f32[64,64]{1,0:T(8,128)S(1)} %factor.3.inverse, ...), custom_call_target="tpu_custom_call" | custom-call | flops 905969664 | bytes 23592960 | tf_op jit(solution)/shard_map/renew/pallas_call | solution.py:367
  (4 shorter events, 0.1 us)
Async XLA Ops:
  6.2 2.8 %collective-permute-start = (f32[192,4,128]{2,1,0:T(4,128)S(1)}, f32[192,4,128]{2,1,0:T(4,128)S(1)}, u32[]{:S(2)}, u32[]{:S(2)}) collective-permute-start(f32[192,4,128]{2,1,0:T(4,128)S(1)} %get-tuple-element.45), channel_id=1, source_target_pairs={{0,16},{16,0},{1,17},{17,1},{2,18},{18,2},{3,19},{19,3},{4,20},{20... | collective-permute-start | bytes 1179656 | tf_op jit(solution)/shard_map/ppermute | solution.py:385
  9.2 37.4 %collective-permute-start.1 = (f32[1536,768]{1,0:T(8,128)S(1)}, f32[1536,768]{1,0:T(8,128)S(1)}, u32[]{:S(2)}, u32[]{:S(2)}) collective-permute-start(f32[1536,768]{1,0:T(8,128)S(1)} %give.1), channel_id=1, source_target_pairs={{0,16},{16,0},{1,17},{17,1},{2,18},{18,2},{3,19},{19,3},{4,20},{20... | collective-permute-start | bytes 14155784 | tf_op jit(solution)/shard_map/ppermute | solution.py:385
  48.6 3.9 %collective-permute-start.2 = (f32[32,768]{1,0:T(8,128)S(1)}, f32[32,768]{1,0:T(8,128)S(1)}, u32[]{:S(2)}, u32[]{:S(2)}) collective-permute-start(f32[32,768]{1,0:T(8,128)S(1)} %get-tuple-element.53), channel_id=1, source_target_pairs={{0,16},{16,0},{1,17},{17,1},{2,18},{18,2},{3,19},{19,3},{4,20},{20... | collective-permute-start | bytes 294920 | tf_op jit(solution)/shard_map/ppermute | solution.py:385
  51.5 1.2 %collective-permute-start.3 = (f32[64,64]{1,0:T(8,128)S(1)}, f32[64,64]{1,0:T(8,128)S(1)}, u32[]{:S(2)}, u32[]{:S(2)}) collective-permute-start(f32[64,64]{1,0:T(8,128)S(1)} %get-tuple-element.56.grams_0_), channel_id=1, source_target_pairs={{0,16},{16,0},{1,17},{17,1},{2,18},{18,2},{3,19},{19,3},{4,20},{20... | collective-permute-start | bytes 49160 | tf_op jit(solution)/shard_map/ppermute | solution.py:385
  52.8 5.7 %collective-permute-start.6 = (f32[32,768]{1,0:T(8,128)S(1)}, f32[32,768]{1,0:T(8,128)S(1)}, u32[]{:S(2)}, u32[]{:S(2)}) collective-permute-start(f32[32,768]{1,0:T(8,128)S(1)} %add.28), channel_id=1, source_target_pairs={{0,64},{32,96},{64,0},{96,32},{1,65},{33,97},{65,1},{97,33},{2,66}... | collective-permute-start | bytes 294920 | tf_op jit(solution)/shard_map/ppermute | solution.py:389
  53.1 5.6 %collective-permute-start.5 = (f32[32,768]{1,0:T(8,128)S(1)}, f32[32,768]{1,0:T(8,128)S(1)}, u32[]{:S(2)}, u32[]{:S(2)}) collective-permute-start(f32[32,768]{1,0:T(8,128)S(1)} %add.28), channel_id=1, source_target_pairs={{0,96},{32,0},{64,32},{96,64},{1,97},{33,1},{65,33},{97,65},{2,98}... | collective-permute-start | bytes 294920 | tf_op jit(solution)/shard_map/ppermute | solution.py:389
  55.2 5.3 %collective-permute-start.4 = (f32[32,768]{1,0:T(8,128)S(1)}, f32[32,768]{1,0:T(8,128)S(1)}, u32[]{:S(2)}, u32[]{:S(2)}) collective-permute-start(f32[32,768]{1,0:T(8,128)S(1)} %add.28), channel_id=1, source_target_pairs={{0,32},{32,64},{64,96},{96,0},{1,33},{33,65},{65,97},{97,1},{2,34}... | collective-permute-start | bytes 294920 | tf_op jit(solution)/shard_map/ppermute | solution.py:389
  60.6 2.4 %collective-permute-start.7 = (f32[32,768]{1,0:T(8,128)S(1)}, f32[32,768]{1,0:T(8,128)S(1)}, u32[]{:S(2)}, u32[]{:S(2)}) collective-permute-start(f32[32,768]{1,0:T(8,128)S(1)} %add_add_fusion.1.z_mine), channel_id=1, source_target_pairs={{0,16},{16,0},{1,17},{17,1},{2,18},{18,2},{3,19},{19,3},{4,20},{20... | collective-permute-start | bytes 294920 | tf_op jit(solution)/shard_map/ppermute | solution.py:385
  94.5 5.9 %collective-permute-start.10 = (f32[192,4,128]{2,1,0:T(4,128)S(1)}, f32[192,4,128]{2,1,0:T(4,128)S(1)}, u32[]{:S(2)}, u32[]{:S(2)}) collective-permute-start(f32[192,4,128]{2,1,0:T(4,128)S(1)} %bitcast.14), channel_id=1, source_target_pairs={{0,16},{16,0},{1,17},{17,1},{2,18},{18,2},{3,19},{19,3},{4,20},{20... | collective-permute-start | bytes 1179656 | tf_op jit(solution)/shard_map/ppermute | solution.py:385
  99.0 1.4 %collective-permute-start.8 = (f32[32,768]{1,0:T(8,128)S(1)}, f32[32,768]{1,0:T(8,128)S(1)}, u32[]{:S(2)}, u32[]{:S(2)}) collective-permute-start(f32[32,768]{1,0:T(8,128)S(1)} %get-tuple-element.65), channel_id=1, source_target_pairs={{0,16},{16,0},{1,17},{17,1},{2,18},{18,2},{3,19},{19,3},{4,20},{20... | collective-permute-start | bytes 294920 | tf_op jit(solution)/shard_map/ppermute | solution.py:385
  99.1 1.4 %collective-permute-start.9 = (f32[64,64]{1,0:T(8,128)S(1)}, f32[64,64]{1,0:T(8,128)S(1)}, u32[]{:S(2)}, u32[]{:S(2)}) collective-permute-start(f32[64,64]{1,0:T(8,128)S(1)} %get-tuple-element.68.grams_0_), channel_id=1, source_target_pairs={{0,16},{16,0},{1,17},{17,1},{2,18},{18,2},{3,19},{19,3},{4,20},{20... | collective-permute-start | bytes 49160 | tf_op jit(solution)/shard_map/ppermute | solution.py:385
  100.4 6.4 %collective-permute-start.13 = (f32[32,768]{1,0:T(8,128)S(1)}, f32[32,768]{1,0:T(8,128)S(1)}, u32[]{:S(2)}, u32[]{:S(2)}) collective-permute-start(f32[32,768]{1,0:T(8,128)S(1)} %add.32), channel_id=1, source_target_pairs={{0,64},{32,96},{64,0},{96,32},{1,65},{33,97},{65,1},{97,33},{2,66}... | collective-permute-start | bytes 294920 | tf_op jit(solution)/shard_map/ppermute | solution.py:389
  100.9 6.1 %collective-permute-start.12 = (f32[32,768]{1,0:T(8,128)S(1)}, f32[32,768]{1,0:T(8,128)S(1)}, u32[]{:S(2)}, u32[]{:S(2)}) collective-permute-start(f32[32,768]{1,0:T(8,128)S(1)} %add.32), channel_id=1, source_target_pairs={{0,96},{32,0},{64,32},{96,64},{1,97},{33,1},{65,33},{97,65},{2,98}... | collective-permute-start | bytes 294920 | tf_op jit(solution)/shard_map/ppermute | solution.py:389
  102.9 5.4 %collective-permute-start.11 = (f32[32,768]{1,0:T(8,128)S(1)}, f32[32,768]{1,0:T(8,128)S(1)}, u32[]{:S(2)}, u32[]{:S(2)}) collective-permute-start(f32[32,768]{1,0:T(8,128)S(1)} %add.32), channel_id=1, source_target_pairs={{0,32},{32,64},{64,96},{96,0},{1,33},{33,65},{65,97},{97,1},{2,34}... | collective-permute-start | bytes 294920 | tf_op jit(solution)/shard_map/ppermute | solution.py:389
  108.2 2.4 %collective-permute-start.14 = (f32[32,768]{1,0:T(8,128)S(1)}, f32[32,768]{1,0:T(8,128)S(1)}, u32[]{:S(2)}, u32[]{:S(2)}) collective-permute-start(f32[32,768]{1,0:T(8,128)S(1)} %add_add_fusion.z_mine), channel_id=1, source_target_pairs={{0,16},{16,0},{1,17},{17,1},{2,18},{18,2},{3,19},{19,3},{4,20},{20... | collective-permute-start | bytes 294920 | tf_op jit(solution)/shard_map/ppermute | solution.py:385

commit v6 on v5

--- a/solution.py
+++ b/solution.py
@@ -10,7 +10,7 @@
 ROWS, COLS = 3072, 768
 WIDE = 256
 OWN = ROWS // 2
-EVEN = (1024,) * 3
+LOAD = (768,) * 2
 PART = (512,) * 3
 LAST = (256,) * 12
 CHIPS = 64
@@ -61,21 +61,6 @@
     return jnp.concatenate(columns, axis=1)
 
 
-def put_rows(core, mine, other, start, x):
-    for half in range(2):
-        low, high = max(start, half * OWN), min(start + x.shape[1], (half + 1) * OWN)
-        if low < high:
-            own = x[:, low - start : high - start]
-
-            @pl.when(core == half)
-            def _():
-                put(mine, low - half * OWN, own)
-
-            @pl.when(core != half)
-            def _():
-                put(other, low - half * OWN, own)
-
-
 def ranges(sizes):
     starts = [sum(sizes[:i]) for i in range(len(sizes))]
     return list(zip(starts, sizes))
@@ -98,41 +83,53 @@
     return fold(p + lax.dot_general(stack[...], e[rows, :], across, preferred_element_type=F32))
 
 
-def first_left_kernel(core, q_far, g_far, e_far, mine, other, g, e, stack, q, q_sem, g_sem, e_sem):
+def first_other_kernel(core, q_far, g_far, e_far, term, send, g, e, stack, q, q_sem, g_sem, e_sem):
     q_copy = pltpu.make_async_copy(q_far, q, q_sem)
     q_copy.start()
-    pieces = ranges(EVEN)
+    pieces = ranges(LOAD)
     copies = []
-    for i, (start, size) in enumerate(pieces):
-        rows = pl.ds(start, size)
-        copies.append(
-            (
-                pltpu.make_async_copy(g_far.at[rows, :], g.at[rows, :], g_sem.at[i]),
-                pltpu.make_async_copy(e_far.at[rows, :], e.at[rows, :], e_sem.at[i]),
+    for half in (1 - core[0], core[0]):
+        for start, size in pieces:
+            rows = pl.ds(pl.multiple_of(half * OWN + start, 256), size)
+            slot = len(copies)
+            copies.append(
+                (
+                    pltpu.make_async_copy(g_far.at[rows, :], g.at[rows, :], g_sem.at[slot]),
+                    pltpu.make_async_copy(e_far.at[rows, :], e.at[rows, :], e_sem.at[slot]),
+                )
             )
-        )
-    for pair in copies[:2]:
+    for pair in copies[: len(pieces)]:
         for copy in pair:
             copy.start()
     q_copy.wait()
     stack[...] = stacked(q[...])
-    for i, (start, size) in enumerate(pieces):
-        for copy in copies[i]:
+    for pair, later in zip(copies, copies[len(pieces) :]):
+        for copy in pair:
             copy.wait()
-        for copy in copies[i + 2] if i + 2 < len(copies) else ():
+        for copy in later:
             copy.start()
-        put_rows(core[0], mine, other, start, times_rows(stack, g, e, start, size))
+    for start, size in pieces:
+        put(term, start, times_rows(stack, g, e, pl.multiple_of((1 - core[0]) * OWN + start, 256), size))
+    for start in range(0, OWN, 256):
+        rows = pl.ds(pl.multiple_of((1 - core[0]) * OWN + start, 256), 256)
+        send[pl.ds(start, 256), :] = g[rows, :].astype(F32) + e[rows, :].astype(F32)
+    for pair in copies[len(pieces) :]:
+        for copy in pair:
+            copy.wait()
+
+
+def first_own_kernel(core, stack, g, e, term):
+    for half in range(2):
+
+        @pl.when(core[0] == half)
+        def _():
+            for start, size in ranges(PART):
+                put(term, start, times_rows(stack, g, e, half * OWN + start, size))
 
 
 def right_factor(core, z_mine, z_other, inverse):
     z = ordered(core[0], z_mine[...], z_other[...])
     return product(inverse[...], z) * (1.0 / REPLICAS)
-
-
-def give_kernel(core, g, e, send):
-    for start in range(0, OWN, 256):
-        rows = pl.ds(pl.multiple_of((1 - core[0]) * OWN + start, 256), 256)
-        send[pl.ds(start, 256), :] = g[rows, :].astype(F32) + e[rows, :].astype(F32)
 
 
 def merge_rows(core, g, e, received, high, low, cols):
@@ -269,35 +266,34 @@
     return pltpu.SemaphoreType.DMA((count,))
 
 
-def first_left_pass(core, q, g, e):
-    return pl.pallas_call(
-        first_left_kernel,
+def first_other_pass(core, q, g, e):
+    return pl.pallas_call(
+        first_other_kernel,
         in_specs=[SCALAR, FAR, FAR, FAR],
-        out_specs=[NEAR] * 4,
-        out_shape=[PIECES, PIECES, NEAR_ARRAY, NEAR_ARRAY],
+        out_specs=[NEAR] * 5,
+        out_shape=[PIECES, pltpu.VMEM((OWN, COLS), F32), NEAR_ARRAY, NEAR_ARRAY, STACK],
         scratch_shapes=[
-            STACK,
             pltpu.VMEM((RANK, COLS), F32),
             pltpu.SemaphoreType.DMA,
-            semaphores(len(EVEN)),
-            semaphores(len(EVEN)),
+            semaphores(2 * len(LOAD)),
+            semaphores(2 * len(LOAD)),
         ],
         compiler_params=params(LIMIT),
-        cost_estimate=cost(6, 4 * ROWS * COLS),
-        name="first_left_pass",
+        cost_estimate=cost(3, 4 * ROWS * COLS),
+        name="first_other_pass",
     )(core, *far(q, g, e))
 
 
-def give(core, g, e):
-    return pl.pallas_call(
-        give_kernel,
-        in_specs=[SCALAR] + [NEAR] * 2,
+def first_own_pass(core, stack, g, e):
+    return pl.pallas_call(
+        first_own_kernel,
+        in_specs=[SCALAR] + [NEAR] * 3,
         out_specs=NEAR,
-        out_shape=pltpu.VMEM((OWN, COLS), F32),
-        compiler_params=params(SMALL),
-        cost_estimate=pl.CostEstimate(flops=10**9, bytes_accessed=8 * OWN * COLS, transcendentals=0),
-        name="give",
-    )(core, *near(g, e))
+        out_shape=PIECES,
+        compiler_params=params(SMALL),
+        cost_estimate=cost(3, 2 * ROWS * COLS),
+        name="first_own_pass",
+    )(core, *near(stack, g, e))
 
 
 def first_right_pass(core, left, g, e, received):
@@ -418,8 +414,8 @@
 
 def shards(gradients, errors, weight, start_q):
     core = lax.axis_index("core").astype(jnp.int32).reshape(1)
-    mine, other, g, e = first_left_pass(core, start_q.T, gradients[0], errors[0])
-    term, send = lax.optimization_barrier((mine + swap(other), give(core, g, e)))
+    other, send, g, e, stack = first_other_pass(core, start_q.T, gradients[0], errors[0])
+    term, send = lax.optimization_barrier((first_own_pass(core, stack, g, e) + swap(other), send))
     left, received = lax.optimization_barrier((mean_left(term), swap(send)))
     high, low, *terms = first_right_pass(core, left, g, e, received)
     right, _ = sum_right(*terms)

time: 116 us -> 116 us (level)
  transfers between devices with their start and end apart: 15 -> 15, of which waited for: 11 -> 10; matrix products, arithmetic and copies ran while one was open for 0% -> 0% of each run, Pallas kernels for 6% -> 8%
where the time goes in v6:
time: 116 us; the launch traced here: 115 us
  blocking collectives  66.3 us (57%)
  Pallas kernels  22.4 us (19%)
  starting transfers between devices  16.6 us (14%)
  waiting for transfers between devices  8.92 us (8%)
    all_to_all x4, blocking collectives, exchange(): return lax.all_to_all(x, CHIP_AXES, 0, 0, tiled=True).reshape(TILES, 4, 128)  66.3 us
    ppermute x9, starting transfers between devices, swap(): return lax.ppermute(x, 'core', [(0, 1), (1, 0)])  11.8 us
    pallas_call x1, Pallas kernels, renew(): pl.pallas_call(renew_kernel, in_specs=[SCALAR] + [NEAR] * 7, out_specs=[F...  5.29 us
    ppermute x6, waiting for transfers between devices, along_y(): return lax.ppermute(x, 'y', [(i, (i + shift) % 4) for i in range(4)])  5.08 us
    ppermute x6, starting transfers between devices, along_y(): return lax.ppermute(x, 'y', [(i, (i + shift) % 4) for i in range(4)])  4.8 us
    pallas_call x1, Pallas kernels, first_other_pass(): pl.pallas_call(first_other_kernel, in_specs=[SCALAR, FAR, FAR, FAR], out_...  4.54 us
    ppermute x9, waiting for transfers between devices, swap(): return lax.ppermute(x, 'core', [(0, 1), (1, 0)])  3.84 us
    pallas_call x2, Pallas kernels, factor(): pl.pallas_call(factor_kernel, out_shape=SQUARE, compiler_params=params(SM...  3.29 us
  transfers between devices with their start and end apart: 15, of which 10 were waited for; matrix products, arithmetic and copies ran while one was open for 0% of the time, Pallas kernels for 8%

profile of v6, /device:TPU:1, one launch (start us, length us, event | category | flops | bytes accessed | tf_op | source)
XLA Modules:
  0.0 115.3 jit_solution(3829512234402604436)
XLA Ops:
  0.6 4.5 %first_other_pass.1 = (f32[192,4,128]{2,1,0:T(4,128)S(1)}, f32[1536,768]{1,0:T(8,128)S(1)}, bf16[3072,768]{1,0:T(8,128)(2,1)S(1)}, bf16[3072,768]{1,0:T(8,128)(2,1)S(1)}, bf16[192,768]{1,0:T(8,128)(2,1)S(1)}) custom-call(s32[1]{0:T(128)} %bitcast.core, f32[64,768]{1,0:T(8,128)} %bitcast.26, bf16[3072,768]{1,0:T(8,128)(2,1)} %bitcast.23, ...), custom_call_target="tpu_custom_call" | custom-call | flops 905969664 | bytes 9437184 | tf_op jit(solution)/shard_map/first_other_pass/pallas_call | solution.py:270
  5.2 1.5 %collective-permute-start = (f32[192,4,128]{2,1,0:T(4,128)S(1)}, f32[192,4,128]{2,1,0:T(4,128)S(1)}, u32[]{:S(2)}, u32[]{:S(2)}) collective-permute-start(f32[192,4,128]{2,1,0:T(4,128)S(1)} %get-tuple-element.48), channel_id=1, source_target_pairs={{0,16},{16,0},{1,17},{17,1},{2,18},{18,2},{3,19},{19,3},{4,20},{20... | collective-permute-start | bytes 1179656 | tf_op jit(solution)/shard_map/ppermute | solution.py:381
  6.7 1.7 %first_own_pass.1 = f32[192,4,128]{2,1,0:T(4,128)S(1)} custom-call(s32[1]{0:T(128)} %bitcast.core, bf16[192,768]{1,0:T(8,128)(2,1)S(1)} %get-tuple-element.45.stack, bf16[3072,768]{1,0:T(8,128)(2,1)S(1)} %get-tuple-element.46.g, bf16[3072,768]{1,0:T(8,128)(2,1)S(1)} %get-tuple-element.47.e), custom_call_target="tpu_custom_call" | custom-call | flops 905969664 | bytes 4718592 | tf_op jit(solution)/shard_map/first_own_pass/pallas_call | solution.py:288
  8.4 0.0 collective-permute-done
  8.4 0.1 add.27
  8.5 0.1 collective-permute-start.1
  8.6 21.8 %all_to_all.20 = f32[64,3,4,128]{3,2,1,0:T(4,128)S(1)} all-to-all(f32[64,3,4,128]{3,2,1,0:T(4,128)S(1)} %bitcast.25), channel_id=1, replica_groups=mesh['y'=4,'core'=2,'x'=4,'z'=4] {'y','x','z'}, dimensions={0} | all-to-all | bytes 786432 | tf_op jit(solution)/shard_map/all_to_all | solution.py:400
  30.4 0.1 mean.2
  30.5 14.6 %all_to_all.21 = f32[64,3,4,128]{3,2,1,0:T(4,128)S(1)} all-to-all(f32[64,3,4,128]{3,2,1,0:T(4,128)S(1)} %bitcast.18), channel_id=1, replica_groups=mesh['y'=4,'core'=2,'x'=4,'z'=4] {'y','x','z'}, dimensions={0} | all-to-all | bytes 786432 | tf_op jit(solution)/shard_map/all_to_all | solution.py:400
  45.1 0.0 collective-permute-done.1.received
  45.1 1.9 %first_right_pass.1 = (bf16[1536,768]{1,0:T(8,128)(2,1)S(1)}, bf16[1536,768]{1,0:T(8,128)(2,1)S(1)}, f32[32,768]{1,0:T(8,128)S(1)}, f32[32,768]{1,0:T(8,128)S(1)}, f32[64,64]{1,0:T(8,128)S(1)}) custom-call(s32[1]{0:T(128)} %bitcast.core, f32[192,4,128]{2,1,0:T(4,128)S(1)} %bitcast.21, bf16[3072,768]{1,0:T(8,128)(2,1)S(1)} %get-tuple-element.46.g, ...), custom_call_target="tpu_custom_call" | custom-call | flops 905969664 | bytes 9437184 | tf_op jit(solution)/shard_map/first_right_pass/pallas_call | solution.py:300
  47.1 3.4 %collective-permute-start.2 = (f32[32,768]{1,0:T(8,128)S(1)}, f32[32,768]{1,0:T(8,128)S(1)}, u32[]{:S(2)}, u32[]{:S(2)}) collective-permute-start(f32[32,768]{1,0:T(8,128)S(1)} %get-tuple-element.55), channel_id=1, source_target_pairs={{0,16},{16,0},{1,17},{17,1},{2,18},{18,2},{3,19},{19,3},{4,20},{20... | collective-permute-start | bytes 294920 | tf_op jit(solution)/shard_map/ppermute | solution.py:381
  50.5 0.1 collective-permute-start.3
  50.6 0.9 collective-permute-done.2
  51.5 0.2 collective-permute-done.3.grams_1_
  51.7 0.4 collective-permute-start.6
  52.1 2.0 %collective-permute-start.5 = (f32[32,768]{1,0:T(8,128)S(1)}, f32[32,768]{1,0:T(8,128)S(1)}, u32[]{:S(2)}, u32[]{:S(2)}) collective-permute-start(f32[32,768]{1,0:T(8,128)S(1)} %add.28), channel_id=1, source_target_pairs={{0,96},{32,0},{64,32},{96,64},{1,97},{33,1},{65,33},{97,65},{2,98}... | collective-permute-start | bytes 294920 | tf_op jit(solution)/shard_map/ppermute | solution.py:385
  54.1 0.0 collective-permute-start.4
  54.1 1.6 %factor.2.inverse = f32[64,64]{1,0:T(8,128)S(1)} custom-call(f32[64,64]{1,0:T(8,128)S(1)} %get-tuple-element.58.grams_0_, f32[64,64]{1,0:T(8,128)S(1)} %collective-permute-done.3.grams_1_), custom_call_target="tpu_custom_call" | custom-call | flops 4000000000 | bytes 32768 | tf_op jit(solution)/shard_map/factor/pallas_call | solution.py:339
  55.7 1.7 %collective-permute-done.6 = f32[32,768]{1,0:T(8,128)S(1)} collective-permute-done((f32[32,768]{1,0:T(8,128)S(1)}, f32[32,768]{1,0:T(8,128)S(1)}, u32[]{:S(2)}, u32[]{:S(2)}) %collective-permute-start.6) | collective-permute-done | bytes 98336 | tf_op jit(solution)/shard_map/ppermute | solution.py:385
  57.4 0.2 collective-permute-done.5
  57.6 1.9 %collective-permute-done.4 = f32[32,768]{1,0:T(8,128)S(1)} collective-permute-done((f32[32,768]{1,0:T(8,128)S(1)}, f32[32,768]{1,0:T(8,128)S(1)}, u32[]{:S(2)}, u32[]{:S(2)}) %collective-permute-start.4) | collective-permute-done | bytes 98336 | tf_op jit(solution)/shard_map/ppermute | solution.py:385
  59.5 1.4 %collective-permute-start.7 = (f32[32,768]{1,0:T(8,128)S(1)}, f32[32,768]{1,0:T(8,128)S(1)}, u32[]{:S(2)}, u32[]{:S(2)}) collective-permute-start(f32[32,768]{1,0:T(8,128)S(1)} %add_add_fusion.1.z_mine), channel_id=1, source_target_pairs={{0,16},{16,0},{1,17},{17,1},{2,18},{18,2},{3,19},{19,3},{4,20},{20... | collective-permute-start | bytes 294920 | tf_op jit(solution)/shard_map/ppermute | solution.py:381
  60.9 0.9 collective-permute-done.7.z_other
  61.9 1.8 %left_pass.1 = f32[192,4,128]{2,1,0:T(4,128)S(1)} custom-call(s32[1]{0:T(128)} %bitcast.core, f32[32,768]{1,0:T(8,128)S(1)} %add_add_fusion.1.z_mine, f32[32,768]{1,0:T(8,128)S(1)} %collective-permute-done.7.z_other, f32[64,64]{1,0:T(8,128)S(1)} %factor.2.inverse, bf16[1536,768]{1,0:T(8,128)(2,1)S(1)} %get-tuple-element.64.high, ...), custom_call_target="tpu_custom_call" | custom-call | flops 905969664 | bytes 4718592 | tf_op jit(solution)/shard_map/left_pass/pallas_call | solution.py:313
  63.7 15.2 %all_to_all.22 = f32[64,3,4,128]{3,2,1,0:T(4,128)S(1)} all-to-all(f32[64,3,4,128]{3,2,1,0:T(4,128)S(1)} %bitcast.22), channel_id=1, replica_groups=mesh['y'=4,'core'=2,'x'=4,'z'=4] {'y','x','z'}, dimensions={0} | all-to-all | bytes 786432 | tf_op jit(solution)/shard_map/all_to_all | solution.py:400
  78.9 0.1 mean.3
  79.1 14.6 %all_to_all.23 = f32[64,3,4,128]{3,2,1,0:T(4,128)S(1)} all-to-all(f32[64,3,4,128]{3,2,1,0:T(4,128)S(1)} %bitcast.20), channel_id=1, replica_groups=mesh['y'=4,'core'=2,'x'=4,'z'=4] {'y','x','z'}, dimensions={0} | all-to-all | bytes 786432 | tf_op jit(solution)/shard_map/all_to_all | solution.py:400
  93.7 3.2 %collective-permute-start.10 = (f32[192,4,128]{2,1,0:T(4,128)S(1)}, f32[192,4,128]{2,1,0:T(4,128)S(1)}, u32[]{:S(2)}, u32[]{:S(2)}) collective-permute-start(f32[192,4,128]{2,1,0:T(4,128)S(1)} %bitcast.14), channel_id=1, source_target_pairs={{0,16},{16,0},{1,17},{17,1},{2,18},{18,2},{3,19},{19,3},{4,20},{20... | collective-permute-start | bytes 1179656 | tf_op jit(solution)/shard_map/ppermute | solution.py:381
  96.9 1.3 %right_pass.1 = (f32[32,768]{1,0:T(8,128)S(1)}, f32[32,768]{1,0:T(8,128)S(1)}, f32[64,64]{1,0:T(8,128)S(1)}) custom-call(s32[1]{0:T(128)} %bitcast.core, f32[192,4,128]{2,1,0:T(4,128)S(1)} %bitcast.15, bf16[1536,768]{1,0:T(8,128)(2,1)S(1)} %get-tuple-element.64.high, bf16[1536,768]{1,0:T(8,128)(2,1)S(1)} %get-tuple-element.65.low), custom_call_target="tpu_custom_call" | custom-call | flops 905969664 | bytes 4718592 | tf_op jit(solution)/shard_map/right_pass/pallas_call | solution.py:326
  98.1 0.1 collective-permute-start.8
  98.2 0.5 collective-permute-start.9
  98.7 0.8 collective-permute-done.8
  99.5 0.1 collective-permute-done.9.grams_1_
  99.6 0.0 collective-permute-done.10.l_other
  99.6 0.4 collective-permute-start.13
  100.0 2.0 %collective-permute-start.12 = (f32[32,768]{1,0:T(8,128)S(1)}, f32[32,768]{1,0:T(8,128)S(1)}, u32[]{:S(2)}, u32[]{:S(2)}) collective-permute-start(f32[32,768]{1,0:T(8,128)S(1)} %add.32), channel_id=1, source_target_pairs={{0,96},{32,0},{64,32},{96,64},{1,97},{33,1},{65,33},{97,65},{2,98}... | collective-permute-start | bytes 294920 | tf_op jit(solution)/shard_map/ppermute | solution.py:385
  102.0 0.0 collective-permute-start.11
  102.0 1.6 %factor.3.inverse = f32[64,64]{1,0:T(8,128)S(1)} custom-call(f32[64,64]{1,0:T(8,128)S(1)} %get-tuple-element.70.grams_0_, f32[64,64]{1,0:T(8,128)S(1)} %collective-permute-done.9.grams_1_), custom_call_target="tpu_custom_call" | custom-call | flops 4000000000 | bytes 32768 | tf_op jit(solution)/shard_map/factor/pallas_call | solution.py:339
  103.7 2.4 %ready.1 = (bf16[3072,192]{1,0:T(8,128)(2,1)S(1)}, bf16[3072,768]{1,0:T(8,128)(2,1)S(1)}) custom-call(s32[1]{0:T(128)} %bitcast.core, f32[192,4,128]{2,1,0:T(4,128)S(1)} %bitcast.16, f32[192,4,128]{2,1,0:T(4,128)S(1)} %collective-permute-done.10.l_other, bf16[3072,768]{1,0:T(8,128)(2,1)} %w_far), custom_call_target="tpu_custom_call" | custom-call | flops 301989888 | bytes 9437184 | tf_op jit(solution)/shard_map/ready/pallas_call | solution.py:349
  106.0 0.0 collective-permute-done.13
  106.1 0.0 collective-permute-done.12
  106.1 1.3 %collective-permute-done.11 = f32[32,768]{1,0:T(8,128)S(1)} collective-permute-done((f32[32,768]{1,0:T(8,128)S(1)}, f32[32,768]{1,0:T(8,128)S(1)}, u32[]{:S(2)}, u32[]{:S(2)}) %collective-permute-start.11) | collective-permute-done | bytes 98336 | tf_op jit(solution)/shard_map/ppermute | solution.py:385
  107.4 1.5 %collective-permute-start.14 = (f32[32,768]{1,0:T(8,128)S(1)}, f32[32,768]{1,0:T(8,128)S(1)}, u32[]{:S(2)}, u32[]{:S(2)}) collective-permute-start(f32[32,768]{1,0:T(8,128)S(1)} %add_add_fusion.z_mine), channel_id=1, source_target_pairs={{0,16},{16,0},{1,17},{17,1},{2,18},{18,2},{3,19},{19,3},{4,20},{20... | collective-permute-start | bytes 294920 | tf_op jit(solution)/shard_map/ppermute | solution.py:381
  108.9 0.9 collective-permute-done.14.z_other
  109.8 5.3 %renew.1 = (bf16[3072,768]{1,0:T(8,128)(2,1)}, bf16[3072,768]{1,0:T(8,128)(2,1)}, f32[64,768]{1,0:T(8,128)}) custom-call(s32[1]{0:T(128)} %bitcast.core, f32[32,768]{1,0:T(8,128)S(1)} %add_add_fusion.z_mine, f32[32,768]{1,0:T(8,128)S(1)} %collective-permute-done.14.z_other, f32[64,64]{1,0:T(8,128)S(1)} %factor.3.inverse, ...), custom_call_target="tpu_custom_call" | custom-call | flops 905969664 | bytes 23592960 | tf_op jit(solution)/shard_map/renew/pallas_call | solution.py:363
  (4 shorter events, 0.1 us)
Async XLA Ops:
  5.2 3.2 %collective-permute-start = (f32[192,4,128]{2,1,0:T(4,128)S(1)}, f32[192,4,128]{2,1,0:T(4,128)S(1)}, u32[]{:S(2)}, u32[]{:S(2)}) collective-permute-start(f32[192,4,128]{2,1,0:T(4,128)S(1)} %get-tuple-element.48), channel_id=1, source_target_pairs={{0,16},{16,0},{1,17},{17,1},{2,18},{18,2},{3,19},{19,3},{4,20},{20... | collective-permute-start | bytes 1179656 | tf_op jit(solution)/shard_map/ppermute | solution.py:381
  8.5 36.7 %collective-permute-start.1 = (f32[1536,768]{1,0:T(8,128)S(1)}, f32[1536,768]{1,0:T(8,128)S(1)}, u32[]{:S(2)}, u32[]{:S(2)}) collective-permute-start(f32[1536,768]{1,0:T(8,128)S(1)} %get-tuple-element.51), channel_id=1, source_target_pairs={{0,16},{16,0},{1,17},{17,1},{2,18},{18,2},{3,19},{19,3},{4,20},{20... | collective-permute-start | bytes 14155784 | tf_op jit(solution)/shard_map/ppermute | solution.py:381
  47.1 4.4 %collective-permute-start.2 = (f32[32,768]{1,0:T(8,128)S(1)}, f32[32,768]{1,0:T(8,128)S(1)}, u32[]{:S(2)}, u32[]{:S(2)}) collective-permute-start(f32[32,768]{1,0:T(8,128)S(1)} %get-tuple-element.55), channel_id=1, source_target_pairs={{0,16},{16,0},{1,17},{17,1},{2,18},{18,2},{3,19},{19,3},{4,20},{20... | collective-permute-start | bytes 294920 | tf_op jit(solution)/shard_map/ppermute | solution.py:381
  50.5 1.2 %collective-permute-start.3 = (f32[64,64]{1,0:T(8,128)S(1)}, f32[64,64]{1,0:T(8,128)S(1)}, u32[]{:S(2)}, u32[]{:S(2)}) collective-permute-start(f32[64,64]{1,0:T(8,128)S(1)} %get-tuple-element.58.grams_0_), channel_id=1, source_target_pairs={{0,16},{16,0},{1,17},{17,1},{2,18},{18,2},{3,19},{19,3},{4,20},{20... | collective-permute-start | bytes 49160 | tf_op jit(solution)/shard_map/ppermute | solution.py:381
  51.7 5.7 %collective-permute-start.6 = (f32[32,768]{1,0:T(8,128)S(1)}, f32[32,768]{1,0:T(8,128)S(1)}, u32[]{:S(2)}, u32[]{:S(2)}) collective-permute-start(f32[32,768]{1,0:T(8,128)S(1)} %add.28), channel_id=1, source_target_pairs={{0,64},{32,96},{64,0},{96,32},{1,65},{33,97},{65,1},{97,33},{2,66}... | collective-permute-start | bytes 294920 | tf_op jit(solution)/shard_map/ppermute | solution.py:385
  52.1 5.6 %collective-permute-start.5 = (f32[32,768]{1,0:T(8,128)S(1)}, f32[32,768]{1,0:T(8,128)S(1)}, u32[]{:S(2)}, u32[]{:S(2)}) collective-permute-start(f32[32,768]{1,0:T(8,128)S(1)} %add.28), channel_id=1, source_target_pairs={{0,96},{32,0},{64,32},{96,64},{1,97},{33,1},{65,33},{97,65},{2,98}... | collective-permute-start | bytes 294920 | tf_op jit(solution)/shard_map/ppermute | solution.py:385
  54.1 5.4 %collective-permute-start.4 = (f32[32,768]{1,0:T(8,128)S(1)}, f32[32,768]{1,0:T(8,128)S(1)}, u32[]{:S(2)}, u32[]{:S(2)}) collective-permute-start(f32[32,768]{1,0:T(8,128)S(1)} %add.28), channel_id=1, source_target_pairs={{0,32},{32,64},{64,96},{96,0},{1,33},{33,65},{65,97},{97,1},{2,34}... | collective-permute-start | bytes 294920 | tf_op jit(solution)/shard_map/ppermute | solution.py:385
  59.5 2.4 %collective-permute-start.7 = (f32[32,768]{1,0:T(8,128)S(1)}, f32[32,768]{1,0:T(8,128)S(1)}, u32[]{:S(2)}, u32[]{:S(2)}) collective-permute-start(f32[32,768]{1,0:T(8,128)S(1)} %add_add_fusion.1.z_mine), channel_id=1, source_target_pairs={{0,16},{16,0},{1,17},{17,1},{2,18},{18,2},{3,19},{19,3},{4,20},{20... | collective-permute-start | bytes 294920 | tf_op jit(solution)/shard_map/ppermute | solution.py:381
  93.7 5.9 %collective-permute-start.10 = (f32[192,4,128]{2,1,0:T(4,128)S(1)}, f32[192,4,128]{2,1,0:T(4,128)S(1)}, u32[]{:S(2)}, u32[]{:S(2)}) collective-permute-start(f32[192,4,128]{2,1,0:T(4,128)S(1)} %bitcast.14), channel_id=1, source_target_pairs={{0,16},{16,0},{1,17},{17,1},{2,18},{18,2},{3,19},{19,3},{4,20},{20... | collective-permute-start | bytes 1179656 | tf_op jit(solution)/shard_map/ppermute | solution.py:381
  98.1 1.4 %collective-permute-start.8 = (f32[32,768]{1,0:T(8,128)S(1)}, f32[32,768]{1,0:T(8,128)S(1)}, u32[]{:S(2)}, u32[]{:S(2)}) collective-permute-start(f32[32,768]{1,0:T(8,128)S(1)} %get-tuple-element.67), channel_id=1, source_target_pairs={{0,16},{16,0},{1,17},{17,1},{2,18},{18,2},{3,19},{19,3},{4,20},{20... | collective-permute-start | bytes 294920 | tf_op jit(solution)/shard_map/ppermute | solution.py:381
  98.2 1.4 %collective-permute-start.9 = (f32[64,64]{1,0:T(8,128)S(1)}, f32[64,64]{1,0:T(8,128)S(1)}, u32[]{:S(2)}, u32[]{:S(2)}) collective-permute-start(f32[64,64]{1,0:T(8,128)S(1)} %get-tuple-element.70.grams_0_), channel_id=1, source_target_pairs={{0,16},{16,0},{1,17},{17,1},{2,18},{18,2},{3,19},{19,3},{4,20},{20... | collective-permute-start | bytes 49160 | tf_op jit(solution)/shard_map/ppermute | solution.py:381
  99.6 6.4 %collective-permute-start.13 = (f32[32,768]{1,0:T(8,128)S(1)}, f32[32,768]{1,0:T(8,128)S(1)}, u32[]{:S(2)}, u32[]{:S(2)}) collective-permute-start(f32[32,768]{1,0:T(8,128)S(1)} %add.32), channel_id=1, source_target_pairs={{0,64},{32,96},{64,0},{96,32},{1,65},{33,97},{65,1},{97,33},{2,66}... | collective-permute-start | bytes 294920 | tf_op jit(solution)/shard_map/ppermute | solution.py:385
  100.0 6.1 %collective-permute-start.12 = (f32[32,768]{1,0:T(8,128)S(1)}, f32[32,768]{1,0:T(8,128)S(1)}, u32[]{:S(2)}, u32[]{:S(2)}) collective-permute-start(f32[32,768]{1,0:T(8,128)S(1)} %add.32), channel_id=1, source_target_pairs={{0,96},{32,0},{64,32},{96,64},{1,97},{33,1},{65,33},{97,65},{2,98}... | collective-permute-start | bytes 294920 | tf_op jit(solution)/shard_map/ppermute | solution.py:385
  102.0 5.4 %collective-permute-start.11 = (f32[32,768]{1,0:T(8,128)S(1)}, f32[32,768]{1,0:T(8,128)S(1)}, u32[]{:S(2)}, u32[]{:S(2)}) collective-permute-start(f32[32,768]{1,0:T(8,128)S(1)} %add.32), channel_id=1, source_target_pairs={{0,32},{32,64},{64,96},{96,0},{1,33},{33,65},{65,97},{97,1},{2,34}... | collective-permute-start | bytes 294920 | tf_op jit(solution)/shard_map/ppermute | solution.py:385
  107.4 2.4 %collective-permute-start.14 = (f32[32,768]{1,0:T(8,128)S(1)}, f32[32,768]{1,0:T(8,128)S(1)}, u32[]{:S(2)}, u32[]{:S(2)}) collective-permute-start(f32[32,768]{1,0:T(8,128)S(1)} %add_add_fusion.z_mine), channel_id=1, source_target_pairs={{0,16},{16,0},{1,17},{17,1},{2,18},{18,2},{3,19},{19,3},{4,20},{20... | collective-permute-start | bytes 294920 | tf_op jit(solution)/shard_map/ppermute | solution.py:381

commit v7 on v6

--- a/solution.py
+++ b/solution.py
@@ -160,24 +160,27 @@
     z_mine[:, cols], z_other[:, cols] = parted(core[0], z)
 
 
-def stack_left(left, stack, gram):
+def stack_left(left, stack):
     for start, size in ranges(PART):
         stack[:, pl.ds(start, size)] = stacked(take(left, start, size))
+
+
+def gram_kernel(stack, gram):
     products = lax.dot_general(stack[...], stack[...], (((1,), (1,)), ((), ())), preferred_element_type=F32)
     rows = fold(products)
     gram[...] = rows[:, :RANK] + (rows[:, RANK : 2 * RANK] + rows[:, 2 * RANK :])
 
 
-def first_right_kernel(core, left, g, e, received, high, low, z_mine, z_other, gram, stack):
-    stack_left(left, stack, gram)
+def first_right_kernel(core, left, g, e, received, high, low, z_mine, z_other, stack):
+    stack_left(left, stack)
     for part in range(COLS // WIDE):
         cols = pl.ds(part * WIDE, WIDE)
         merge_rows(core, g, e, received, high, low, cols)
         times_columns(core, stack, high, low, z_mine, z_other, cols)
 
 
-def right_kernel(core, left, high, low, z_mine, z_other, gram, stack):
-    stack_left(left, stack, gram)
+def right_kernel(core, left, high, low, z_mine, z_other, stack):
+    stack_left(left, stack)
     for part in range(COLS // WIDE):
         times_columns(core, stack, high, low, z_mine, z_other, pl.ds(part * WIDE, WIDE))
 
@@ -301,8 +304,7 @@
         first_right_kernel,
         in_specs=[SCALAR] + [NEAR] * 4,
         out_specs=[NEAR] * 5,
-        out_shape=[NEAR_HALF, NEAR_HALF, ZHALF, ZHALF, SQUARE],
-        scratch_shapes=[pltpu.VMEM((3 * RANK, OWN), BF16)],
+        out_shape=[NEAR_HALF, NEAR_HALF, ZHALF, ZHALF, pltpu.VMEM((3 * RANK, OWN), BF16)],
         compiler_params=params(LIMIT),
         cost_estimate=cost(3, 4 * ROWS * COLS),
         name="first_right_pass",
@@ -327,12 +329,23 @@
         right_kernel,
         in_specs=[SCALAR] + [NEAR] * 3,
         out_specs=[NEAR] * 3,
-        out_shape=[ZHALF, ZHALF, SQUARE],
-        scratch_shapes=[pltpu.VMEM((3 * RANK, OWN), BF16)],
+        out_shape=[ZHALF, ZHALF, pltpu.VMEM((3 * RANK, OWN), BF16)],
         compiler_params=params(SMALL),
         cost_estimate=cost(3, 2 * ROWS * COLS),
         name="right_pass",
     )(core, left, *near(high, low))
+
+
+def gram_of(stack):
+    return pl.pallas_call(
+        gram_kernel,
+        in_specs=[NEAR],
+        out_specs=NEAR,
+        out_shape=SQUARE,
+        compiler_params=params(SMALL),
+        cost_estimate=pl.CostEstimate(flops=2 * 9 * RANK**2 * OWN, bytes_accessed=6 * RANK * OWN, transcendentals=0),
+        name="gram",
+    )(*near(stack))
 
 
 def factor(*grams):
@@ -404,10 +417,11 @@
     return exchange(mean(exchange(term)))
 
 
-def sum_right(mine, other, gram, run=None):
-    half, grams, given = lax.optimization_barrier((mine + swap(other), (gram, swap(gram)), run[1] if run else ()))
+def sum_right(mine, other, stack, run=None):
+    gram = gram_of(stack)
+    half, given = lax.optimization_barrier((mine + swap(other), run[1] if run else ()))
     parts = [along_y(half, shift) for shift in (1, 3, 2)]
-    parts, inverse, done = lax.optimization_barrier((parts, factor(*grams), run[0](*given) if run else ()))
+    parts, inverse, done = lax.optimization_barrier((parts, factor(gram, swap(gram)), run[0](*given) if run else ()))
     half = (half + parts[2]) + (parts[0] + parts[1])
     return (half, swap(half), inverse), done
 

time: 116 us -> 115 us (level)
  waiting for transfers between devices: 8.92 us -> 7.26 us
    ppermute x9, waiting for transfers between devices: 3.84 us -> 2.52 us  [swap(): return lax.ppermute(x, 'core', [(0, 1), (1, 0)])]
  transfers between devices with their start and end apart: 15 -> 15, of which waited for: 10 -> 8; matrix products, arithmetic and copies ran while one was open for 0% -> 0% of each run, Pallas kernels for 8% -> 8%
where the time goes in v7:
time: 115 us
  blocking collectives  66.2 us (58%)
  Pallas kernels  23.2 us (20%)
  starting transfers between devices  17.1 us (15%)
  waiting for transfers between devices  7.26 us (6%)
    all_to_all x4, blocking collectives, exchange(): return lax.all_to_all(x, CHIP_AXES, 0, 0, tiled=True).reshape(TILES, 4, 128)  66.2 us
    ppermute x9, starting transfers between devices, swap(): return lax.ppermute(x, 'core', [(0, 1), (1, 0)])  12.2 us
    pallas_call x1, Pallas kernels, renew(): pl.pallas_call(renew_kernel, in_specs=[SCALAR] + [NEAR] * 7, out_specs=[F...  5.29 us
    ppermute x6, starting transfers between devices, along_y(): return lax.ppermute(x, 'y', [(i, (i + shift) % 4) for i in range(4)])  4.92 us
    ppermute x6, waiting for transfers between devices, along_y(): return lax.ppermute(x, 'y', [(i, (i + shift) % 4) for i in range(4)])  4.74 us
    pallas_call x1, Pallas kernels, first_other_pass(): pl.pallas_call(first_other_kernel, in_specs=[SCALAR, FAR, FAR, FAR], out_...  4.54 us
    pallas_call x2, Pallas kernels, factor(): pl.pallas_call(factor_kernel, out_shape=SQUARE, compiler_params=params(SM...  3.29 us
    ppermute x9, waiting for transfers between devices, swap(): return lax.ppermute(x, 'core', [(0, 1), (1, 0)])  2.52 us
  transfers between devices with their start and end apart: 15, of which 8 were waited for; matrix products, arithmetic and copies ran while one was open for 0% of the time, Pallas kernels for 8%

profile of v7, /device:TPU:1, one launch (start us, length us, event | category | flops | bytes accessed | tf_op | source)
XLA Modules:
  0.0 114.9 jit_solution(12765184707186774022)
XLA Ops:
  0.6 4.5 %first_other_pass.1 = (f32[192,4,128]{2,1,0:T(4,128)S(1)}, f32[1536,768]{1,0:T(8,128)S(1)}, bf16[3072,768]{1,0:T(8,128)(2,1)S(1)}, bf16[3072,768]{1,0:T(8,128)(2,1)S(1)}, bf16[192,768]{1,0:T(8,128)(2,1)S(1)}) custom-call(s32[1]{0:T(128)} %bitcast.core, f32[64,768]{1,0:T(8,128)} %bitcast.26, bf16[3072,768]{1,0:T(8,128)(2,1)} %bitcast.23, ...), custom_call_target="tpu_custom_call" | custom-call | flops 905969664 | bytes 9437184 | tf_op jit(solution)/shard_map/first_other_pass/pallas_call | solution.py:273
  5.2 1.5 %collective-permute-start = (f32[192,4,128]{2,1,0:T(4,128)S(1)}, f32[192,4,128]{2,1,0:T(4,128)S(1)}, u32[]{:S(2)}, u32[]{:S(2)}) collective-permute-start(f32[192,4,128]{2,1,0:T(4,128)S(1)} %get-tuple-element.43), channel_id=1, source_target_pairs={{0,16},{16,0},{1,17},{17,1},{2,18},{18,2},{3,19},{19,3},{4,20},{20... | collective-permute-start | bytes 1179656 | tf_op jit(solution)/shard_map/ppermute | solution.py:394
  6.7 1.7 %first_own_pass.1 = f32[192,4,128]{2,1,0:T(4,128)S(1)} custom-call(s32[1]{0:T(128)} %bitcast.core, bf16[192,768]{1,0:T(8,128)(2,1)S(1)} %get-tuple-element.40.stack, bf16[3072,768]{1,0:T(8,128)(2,1)S(1)} %get-tuple-element.41.g, bf16[3072,768]{1,0:T(8,128)(2,1)S(1)} %get-tuple-element.42.e), custom_call_target="tpu_custom_call" | custom-call | flops 905969664 | bytes 4718592 | tf_op jit(solution)/shard_map/first_own_pass/pallas_call | solution.py:291
  8.4 0.0 collective-permute-done
  8.4 0.1 add.27
  8.5 0.1 collective-permute-start.1
  8.6 21.8 %all_to_all.20 = f32[64,3,4,128]{3,2,1,0:T(4,128)S(1)} all-to-all(f32[64,3,4,128]{3,2,1,0:T(4,128)S(1)} %bitcast.25), channel_id=1, replica_groups=mesh['y'=4,'core'=2,'x'=4,'z'=4] {'y','x','z'}, dimensions={0} | all-to-all | bytes 786432 | tf_op jit(solution)/shard_map/all_to_all | solution.py:413
  30.4 0.1 mean.2
  30.5 14.6 %all_to_all.21 = f32[64,3,4,128]{3,2,1,0:T(4,128)S(1)} all-to-all(f32[64,3,4,128]{3,2,1,0:T(4,128)S(1)} %bitcast.18), channel_id=1, replica_groups=mesh['y'=4,'core'=2,'x'=4,'z'=4] {'y','x','z'}, dimensions={0} | all-to-all | bytes 786432 | tf_op jit(solution)/shard_map/all_to_all | solution.py:413
  45.1 0.0 collective-permute-done.1.received
  45.1 2.0 %first_right_pass.1 = (bf16[1536,768]{1,0:T(8,128)(2,1)S(1)}, bf16[1536,768]{1,0:T(8,128)(2,1)S(1)}, f32[32,768]{1,0:T(8,128)S(1)}, f32[32,768]{1,0:T(8,128)S(1)}, bf16[192,1536]{1,0:T(8,128)(2,1)S(1)}) custom-call(s32[1]{0:T(128)} %bitcast.core, f32[192,4,128]{2,1,0:T(4,128)S(1)} %bitcast.21, bf16[3072,768]{1,0:T(8,128)(2,1)S(1)} %get-tuple-element.41.g, ...), custom_call_target="tpu_custom_call" | custom-call | flops 905969664 | bytes 9437184 | tf_op jit(solution)/shard_map/first_right_pass/pallas_call | solution.py:303
  47.1 3.4 %collective-permute-start.2 = (f32[32,768]{1,0:T(8,128)S(1)}, f32[32,768]{1,0:T(8,128)S(1)}, u32[]{:S(2)}, u32[]{:S(2)}) collective-permute-start(f32[32,768]{1,0:T(8,128)S(1)} %get-tuple-element.50), channel_id=1, source_target_pairs={{0,16},{16,0},{1,17},{17,1},{2,18},{18,2},{3,19},{19,3},{4,20},{20... | collective-permute-start | bytes 294920 | tf_op jit(solution)/shard_map/ppermute | solution.py:394
  50.5 0.5 gram.2.grams_0_
  51.0 0.1 collective-permute-start.6
  51.1 0.4 collective-permute-done.2
  51.5 0.4 collective-permute-start.5
  51.9 2.0 %collective-permute-start.4 = (f32[32,768]{1,0:T(8,128)S(1)}, f32[32,768]{1,0:T(8,128)S(1)}, u32[]{:S(2)}, u32[]{:S(2)}) collective-permute-start(f32[32,768]{1,0:T(8,128)S(1)} %add.28), channel_id=1, source_target_pairs={{0,96},{32,0},{64,32},{96,64},{1,97},{33,1},{65,33},{97,65},{2,98}... | collective-permute-start | bytes 294920 | tf_op jit(solution)/shard_map/ppermute | solution.py:398
  53.9 0.0 collective-permute-start.3
  53.9 0.0 collective-permute-done.6.grams_1_
  53.9 1.6 %factor.2.inverse = f32[64,64]{1,0:T(8,128)S(1)} custom-call(f32[64,64]{1,0:T(8,128)S(1)} %gram.2.grams_0_, f32[64,64]{1,0:T(8,128)S(1)} %collective-permute-done.6.grams_1_), custom_call_target="tpu_custom_call" | custom-call | flops 4000000000 | bytes 32768 | tf_op jit(solution)/shard_map/factor/pallas_call | solution.py:352
  55.6 1.5 %collective-permute-done.5 = f32[32,768]{1,0:T(8,128)S(1)} collective-permute-done((f32[32,768]{1,0:T(8,128)S(1)}, f32[32,768]{1,0:T(8,128)S(1)}, u32[]{:S(2)}, u32[]{:S(2)}) %collective-permute-start.5) | collective-permute-done | bytes 98336 | tf_op jit(solution)/shard_map/ppermute | solution.py:398
  57.1 0.2 collective-permute-done.4
  57.3 1.7 %collective-permute-done.3 = f32[32,768]{1,0:T(8,128)S(1)} collective-permute-done((f32[32,768]{1,0:T(8,128)S(1)}, f32[32,768]{1,0:T(8,128)S(1)}, u32[]{:S(2)}, u32[]{:S(2)}) %collective-permute-start.3) | collective-permute-done | bytes 98336 | tf_op jit(solution)/shard_map/ppermute | solution.py:398
  59.0 1.8 %collective-permute-start.7 = (f32[32,768]{1,0:T(8,128)S(1)}, f32[32,768]{1,0:T(8,128)S(1)}, u32[]{:S(2)}, u32[]{:S(2)}) collective-permute-start(f32[32,768]{1,0:T(8,128)S(1)} %add_add_fusion.1.z_mine), channel_id=1, source_target_pairs={{0,16},{16,0},{1,17},{17,1},{2,18},{18,2},{3,19},{19,3},{4,20},{20... | collective-permute-start | bytes 294920 | tf_op jit(solution)/shard_map/ppermute | solution.py:394
  60.8 0.9 collective-permute-done.7.z_other
  61.8 1.8 %left_pass.1 = f32[192,4,128]{2,1,0:T(4,128)S(1)} custom-call(s32[1]{0:T(128)} %bitcast.core, f32[32,768]{1,0:T(8,128)S(1)} %add_add_fusion.1.z_mine, f32[32,768]{1,0:T(8,128)S(1)} %collective-permute-done.7.z_other, f32[64,64]{1,0:T(8,128)S(1)} %factor.2.inverse, bf16[1536,768]{1,0:T(8,128)(2,1)S(1)} %get-tuple-element.56.high, ...), custom_call_target="tpu_custom_call" | custom-call | flops 905969664 | bytes 4718592 | tf_op jit(solution)/shard_map/left_pass/pallas_call | solution.py:315
  63.6 15.2 %all_to_all.22 = f32[64,3,4,128]{3,2,1,0:T(4,128)S(1)} all-to-all(f32[64,3,4,128]{3,2,1,0:T(4,128)S(1)} %bitcast.22), channel_id=1, replica_groups=mesh['y'=4,'core'=2,'x'=4,'z'=4] {'y','x','z'}, dimensions={0} | all-to-all | bytes 786432 | tf_op jit(solution)/shard_map/all_to_all | solution.py:413
  78.8 0.1 mean.3
  78.9 14.6 %all_to_all.23 = f32[64,3,4,128]{3,2,1,0:T(4,128)S(1)} all-to-all(f32[64,3,4,128]{3,2,1,0:T(4,128)S(1)} %bitcast.20), channel_id=1, replica_groups=mesh['y'=4,'core'=2,'x'=4,'z'=4] {'y','x','z'}, dimensions={0} | all-to-all | bytes 786432 | tf_op jit(solution)/shard_map/all_to_all | solution.py:413
  93.5 3.2 %collective-permute-start.9 = (f32[192,4,128]{2,1,0:T(4,128)S(1)}, f32[192,4,128]{2,1,0:T(4,128)S(1)}, u32[]{:S(2)}, u32[]{:S(2)}) collective-permute-start(f32[192,4,128]{2,1,0:T(4,128)S(1)} %bitcast.14), channel_id=1, source_target_pairs={{0,16},{16,0},{1,17},{17,1},{2,18},{18,2},{3,19},{19,3},{4,20},{20... | collective-permute-start | bytes 1179656 | tf_op jit(solution)/shard_map/ppermute | solution.py:394
  96.7 1.1 right_pass.1
  97.8 0.1 collective-permute-start.8
  97.9 0.5 gram.3.grams_0_
  98.4 0.6 collective-permute-start.13
  99.0 0.2 collective-permute-done.8
  99.2 0.0 collective-permute-done.9.l_other
  99.2 0.4 collective-permute-start.12
  99.7 2.0 %collective-permute-start.11 = (f32[32,768]{1,0:T(8,128)S(1)}, f32[32,768]{1,0:T(8,128)S(1)}, u32[]{:S(2)}, u32[]{:S(2)}) collective-permute-start(f32[32,768]{1,0:T(8,128)S(1)} %add.32), channel_id=1, source_target_pairs={{0,96},{32,0},{64,32},{96,64},{1,97},{33,1},{65,33},{97,65},{2,98}... | collective-permute-start | bytes 294920 | tf_op jit(solution)/shard_map/ppermute | solution.py:398
  101.7 0.0 collective-permute-start.10
  101.7 0.0 collective-permute-done.13.grams_1_
  101.7 1.6 %factor.3.inverse = f32[64,64]{1,0:T(8,128)S(1)} custom-call(f32[64,64]{1,0:T(8,128)S(1)} %gram.3.grams_0_, f32[64,64]{1,0:T(8,128)S(1)} %collective-permute-done.13.grams_1_), custom_call_target="tpu_custom_call" | custom-call | flops 4000000000 | bytes 32768 | tf_op jit(solution)/shard_map/factor/pallas_call | solution.py:352
  103.3 2.4 %ready.1 = (bf16[3072,192]{1,0:T(8,128)(2,1)S(1)}, bf16[3072,768]{1,0:T(8,128)(2,1)S(1)}) custom-call(s32[1]{0:T(128)} %bitcast.core, f32[192,4,128]{2,1,0:T(4,128)S(1)} %bitcast.16, f32[192,4,128]{2,1,0:T(4,128)S(1)} %collective-permute-done.9.l_other, bf16[3072,768]{1,0:T(8,128)(2,1)} %w_far), custom_call_target="tpu_custom_call" | custom-call | flops 301989888 | bytes 9437184 | tf_op jit(solution)/shard_map/ready/pallas_call | solution.py:362
  105.7 0.0 collective-permute-done.12
  105.7 0.0 collective-permute-done.11
  105.7 1.4 %collective-permute-done.10 = f32[32,768]{1,0:T(8,128)S(1)} collective-permute-done((f32[32,768]{1,0:T(8,128)S(1)}, f32[32,768]{1,0:T(8,128)S(1)}, u32[]{:S(2)}, u32[]{:S(2)}) %collective-permute-start.10) | collective-permute-done | bytes 98336 | tf_op jit(solution)/shard_map/ppermute | solution.py:398
  107.1 1.4 %collective-permute-start.14 = (f32[32,768]{1,0:T(8,128)S(1)}, f32[32,768]{1,0:T(8,128)S(1)}, u32[]{:S(2)}, u32[]{:S(2)}) collective-permute-start(f32[32,768]{1,0:T(8,128)S(1)} %add_add_fusion.z_mine), channel_id=1, source_target_pairs={{0,16},{16,0},{1,17},{17,1},{2,18},{18,2},{3,19},{19,3},{4,20},{20... | collective-permute-start | bytes 294920 | tf_op jit(solution)/shard_map/ppermute | solution.py:394
  108.5 0.9 collective-permute-done.14.z_other
  109.4 5.3 %renew.1 = (bf16[3072,768]{1,0:T(8,128)(2,1)}, bf16[3072,768]{1,0:T(8,128)(2,1)}, f32[64,768]{1,0:T(8,128)}) custom-call(s32[1]{0:T(128)} %bitcast.core, f32[32,768]{1,0:T(8,128)S(1)} %add_add_fusion.z_mine, f32[32,768]{1,0:T(8,128)S(1)} %collective-permute-done.14.z_other, f32[64,64]{1,0:T(8,128)S(1)} %factor.3.inverse, ...), custom_call_target="tpu_custom_call" | custom-call | flops 905969664 | bytes 23592960 | tf_op jit(solution)/shard_map/renew/pallas_call | solution.py:376
  (4 shorter events, 0.1 us)
Async XLA Ops:
  5.2 3.2 %collective-permute-start = (f32[192,4,128]{2,1,0:T(4,128)S(1)}, f32[192,4,128]{2,1,0:T(4,128)S(1)}, u32[]{:S(2)}, u32[]{:S(2)}) collective-permute-start(f32[192,4,128]{2,1,0:T(4,128)S(1)} %get-tuple-element.43), channel_id=1, source_target_pairs={{0,16},{16,0},{1,17},{17,1},{2,18},{18,2},{3,19},{19,3},{4,20},{20... | collective-permute-start | bytes 1179656 | tf_op jit(solution)/shard_map/ppermute | solution.py:394
  8.5 36.7 %collective-permute-start.1 = (f32[1536,768]{1,0:T(8,128)S(1)}, f32[1536,768]{1,0:T(8,128)S(1)}, u32[]{:S(2)}, u32[]{:S(2)}) collective-permute-start(f32[1536,768]{1,0:T(8,128)S(1)} %get-tuple-element.46), channel_id=1, source_target_pairs={{0,16},{16,0},{1,17},{17,1},{2,18},{18,2},{3,19},{19,3},{4,20},{20... | collective-permute-start | bytes 14155784 | tf_op jit(solution)/shard_map/ppermute | solution.py:394
  47.1 4.4 %collective-permute-start.2 = (f32[32,768]{1,0:T(8,128)S(1)}, f32[32,768]{1,0:T(8,128)S(1)}, u32[]{:S(2)}, u32[]{:S(2)}) collective-permute-start(f32[32,768]{1,0:T(8,128)S(1)} %get-tuple-element.50), channel_id=1, source_target_pairs={{0,16},{16,0},{1,17},{17,1},{2,18},{18,2},{3,19},{19,3},{4,20},{20... | collective-permute-start | bytes 294920 | tf_op jit(solution)/shard_map/ppermute | solution.py:394
  51.0 3.0 %collective-permute-start.6 = (f32[64,64]{1,0:T(8,128)S(1)}, f32[64,64]{1,0:T(8,128)S(1)}, u32[]{:S(2)}, u32[]{:S(2)}) collective-permute-start(f32[64,64]{1,0:T(8,128)S(1)} %gram.2.grams_0_), channel_id=1, source_target_pairs={{0,16},{16,0},{1,17},{17,1},{2,18},{18,2},{3,19},{19,3},{4,20},{20... | collective-permute-start | bytes 49160 | tf_op jit(solution)/shard_map/ppermute | solution.py:394
  51.5 5.6 %collective-permute-start.5 = (f32[32,768]{1,0:T(8,128)S(1)}, f32[32,768]{1,0:T(8,128)S(1)}, u32[]{:S(2)}, u32[]{:S(2)}) collective-permute-start(f32[32,768]{1,0:T(8,128)S(1)} %add.28), channel_id=1, source_target_pairs={{0,64},{32,96},{64,0},{96,32},{1,65},{33,97},{65,1},{97,33},{2,66}... | collective-permute-start | bytes 294920 | tf_op jit(solution)/shard_map/ppermute | solution.py:398
  51.9 5.4 %collective-permute-start.4 = (f32[32,768]{1,0:T(8,128)S(1)}, f32[32,768]{1,0:T(8,128)S(1)}, u32[]{:S(2)}, u32[]{:S(2)}) collective-permute-start(f32[32,768]{1,0:T(8,128)S(1)} %add.28), channel_id=1, source_target_pairs={{0,96},{32,0},{64,32},{96,64},{1,97},{33,1},{65,33},{97,65},{2,98}... | collective-permute-start | bytes 294920 | tf_op jit(solution)/shard_map/ppermute | solution.py:398
  53.9 5.0 %collective-permute-start.3 = (f32[32,768]{1,0:T(8,128)S(1)}, f32[32,768]{1,0:T(8,128)S(1)}, u32[]{:S(2)}, u32[]{:S(2)}) collective-permute-start(f32[32,768]{1,0:T(8,128)S(1)} %add.28), channel_id=1, source_target_pairs={{0,32},{32,64},{64,96},{96,0},{1,33},{33,65},{65,97},{97,1},{2,34}... | collective-permute-start | bytes 294920 | tf_op jit(solution)/shard_map/ppermute | solution.py:398
  59.0 2.8 %collective-permute-start.7 = (f32[32,768]{1,0:T(8,128)S(1)}, f32[32,768]{1,0:T(8,128)S(1)}, u32[]{:S(2)}, u32[]{:S(2)}) collective-permute-start(f32[32,768]{1,0:T(8,128)S(1)} %add_add_fusion.1.z_mine), channel_id=1, source_target_pairs={{0,16},{16,0},{1,17},{17,1},{2,18},{18,2},{3,19},{19,3},{4,20},{20... | collective-permute-start | bytes 294920 | tf_op jit(solution)/shard_map/ppermute | solution.py:394
  93.5 5.7 %collective-permute-start.9 = (f32[192,4,128]{2,1,0:T(4,128)S(1)}, f32[192,4,128]{2,1,0:T(4,128)S(1)}, u32[]{:S(2)}, u32[]{:S(2)}) collective-permute-start(f32[192,4,128]{2,1,0:T(4,128)S(1)} %bitcast.14), channel_id=1, source_target_pairs={{0,16},{16,0},{1,17},{17,1},{2,18},{18,2},{3,19},{19,3},{4,20},{20... | collective-permute-start | bytes 1179656 | tf_op jit(solution)/shard_map/ppermute | solution.py:394
  97.8 1.4 %collective-permute-start.8 = (f32[32,768]{1,0:T(8,128)S(1)}, f32[32,768]{1,0:T(8,128)S(1)}, u32[]{:S(2)}, u32[]{:S(2)}) collective-permute-start(f32[32,768]{1,0:T(8,128)S(1)} %get-tuple-element.59), channel_id=1, source_target_pairs={{0,16},{16,0},{1,17},{17,1},{2,18},{18,2},{3,19},{19,3},{4,20},{20... | collective-permute-start | bytes 294920 | tf_op jit(solution)/shard_map/ppermute | solution.py:394
  98.4 3.3 %collective-permute-start.13 = (f32[64,64]{1,0:T(8,128)S(1)}, f32[64,64]{1,0:T(8,128)S(1)}, u32[]{:S(2)}, u32[]{:S(2)}) collective-permute-start(f32[64,64]{1,0:T(8,128)S(1)} %gram.3.grams_0_), channel_id=1, source_target_pairs={{0,16},{16,0},{1,17},{17,1},{2,18},{18,2},{3,19},{19,3},{4,20},{20... | collective-permute-start | bytes 49160 | tf_op jit(solution)/shard_map/ppermute | solution.py:394
  99.2 6.5 %collective-permute-start.12 = (f32[32,768]{1,0:T(8,128)S(1)}, f32[32,768]{1,0:T(8,128)S(1)}, u32[]{:S(2)}, u32[]{:S(2)}) collective-permute-start(f32[32,768]{1,0:T(8,128)S(1)} %add.32), channel_id=1, source_target_pairs={{0,64},{32,96},{64,0},{96,32},{1,65},{33,97},{65,1},{97,33},{2,66}... | collective-permute-start | bytes 294920 | tf_op jit(solution)/shard_map/ppermute | solution.py:398
  99.7 6.1 %collective-permute-start.11 = (f32[32,768]{1,0:T(8,128)S(1)}, f32[32,768]{1,0:T(8,128)S(1)}, u32[]{:S(2)}, u32[]{:S(2)}) collective-permute-start(f32[32,768]{1,0:T(8,128)S(1)} %add.32), channel_id=1, source_target_pairs={{0,96},{32,0},{64,32},{96,64},{1,97},{33,1},{65,33},{97,65},{2,98}... | collective-permute-start | bytes 294920 | tf_op jit(solution)/shard_map/ppermute | solution.py:398
  101.7 5.4 %collective-permute-start.10 = (f32[32,768]{1,0:T(8,128)S(1)}, f32[32,768]{1,0:T(8,128)S(1)}, u32[]{:S(2)}, u32[]{:S(2)}) collective-permute-start(f32[32,768]{1,0:T(8,128)S(1)} %add.32), channel_id=1, source_target_pairs={{0,32},{32,64},{64,96},{96,0},{1,33},{33,65},{65,97},{97,1},{2,34}... | collective-permute-start | bytes 294920 | tf_op jit(solution)/shard_map/ppermute | solution.py:398
  107.1 2.3 %collective-permute-start.14 = (f32[32,768]{1,0:T(8,128)S(1)}, f32[32,768]{1,0:T(8,128)S(1)}, u32[]{:S(2)}, u32[]{:S(2)}) collective-permute-start(f32[32,768]{1,0:T(8,128)S(1)} %add_add_fusion.z_mine), channel_id=1, source_target_pairs={{0,16},{16,0},{1,17},{17,1},{2,18},{18,2},{3,19},{19,3},{4,20},{20... | collective-permute-start | bytes 294920 | tf_op jit(solution)/shard_map/ppermute | solution.py:394
